TPU v7x, 32 devices: a whole 2x2x4 slice. The times are simulated.
32 devices in a mesh: grp: 2 (over y), qb: 16 (over z, x, core).
Axes of the slice: x: 2, y: 2, z: 4, core: 2. Of those that a mesh axis runs over, the one named last changes fastest.
Arguments:
- query_rows: bfloat16 [49152, 128], P(('grp', 'qb')), parts along dimension 0, may hold values from -6 to 6
- key_rows: bfloat16 [49152, 128], P(('grp', 'qb')), parts along dimension 0, may hold values from -6 to 6
- value_rows: bfloat16 [49152, 128], P(('grp', 'qb')), parts along dimension 0, may hold values from -6 to 6
- output_rows: bfloat16 [49152, 128], P(('grp', 'qb')), parts along dimension 0, may hold values from -4 to 4
- output_grad: bfloat16 [49152, 128], P(('grp', 'qb')), parts along dimension 0, may hold values from -192 to 192
- logsumexp: float32 [49152], P(('grp', 'qb')), parts along dimension 0, may hold values from 6.8 to 7.8
- layout: int32 [384, 3], P('grp'), parts along dimension 0, may hold values from 0 to 191, as said below
Outputs:
- query_grad: bfloat16 [49152, 128], P(('grp', 'qb')), parts along dimension 0
- key_grad: bfloat16 [49152, 128], P(('grp', 'qb')), parts along dimension 0
- value_grad: bfloat16 [49152, 128], P(('grp', 'qb')), parts along dimension 0
There are 2 independent parts, one for each index of `grp`. A program takes and returns all parts, laid end to end along the dimension named above; each array names one. Nothing has to cross between parts.
Inputs may be any that keep to these rules, and one draw needn't show every extreme that they name: `layout`: blocks j * 12 to (j + 1) * 12 - 1 are those of device j. Among the rows of one device's 12 query blocks, at most 4 entries name blocks of any one device, and exactly 4 name blocks of some device.
All inputs are finite; a program needn't handle non-finite values.
Results may differ from a plain program's by a relative error of at most 0.0059.
Values may be sent and summed in bfloat16 or wider, within the bound.
No kernel may reach another device: no remote copies, remote signals or barrier semaphores. Data moves between devices by JAX's collectives and lax.ppermute only.
A program may use at most 192 MiB of HBM per device.

v0:
```python
import jax
import jax.numpy as jnp
from jax import lax
from jax.sharding import PartitionSpec as P

BLK = 128
GLOB = 2


def with_halo(array, sides, width):
    for axis, dim in sides:
        count, length = (lax.axis_size(axis), array.shape[dim])
        up = [(i, (i + 1) % count) for i in range(count - 1)]
        down = [(j, i) for i, j in up]
        last = lax.slice_in_dim(array, length - width, length, axis=dim)
        leading = lax.slice_in_dim(array, 0, width, axis=dim)
        before = lax.ppermute(last, axis, up)
        after = lax.ppermute(leading, axis, down)
        array = jnp.concatenate([before, array, after], axis=dim)
    return array


def broadcast(block, axis, source):
    block = jnp.where(lax.axis_index(axis) == source, block, jnp.zeros_like(block))
    return lax.psum(block, axis)


def block_grads(query_blk, key_blk, value_blk, grad_blk, lse_blk, delta_blk, masking, scaling):
    scores = (
        jnp.einsum("nqd,nkd->nqk", query_blk, key_blk, preferred_element_type=jnp.float32) * scaling
    )
    probability = jnp.exp(scores - lse_blk[:, :, None]) * masking[:, None, None]
    dweights = jnp.einsum("nqd,nkd->nqk", grad_blk, value_blk, preferred_element_type=jnp.float32)
    score_grad = probability * (dweights - delta_blk[:, :, None])
    prob_low = probability.astype(jnp.bfloat16)
    score_low = score_grad.astype(jnp.bfloat16)
    query_part = (
        jnp.einsum("nqk,nkd->nqd", score_low, key_blk, preferred_element_type=jnp.float32) * scaling
    )
    key_part = (
        jnp.einsum("nqk,nqd->nkd", score_low, query_blk, preferred_element_type=jnp.float32)
        * scaling
    )
    value_part = jnp.einsum("nqk,nqd->nkd", prob_low, grad_blk, preferred_element_type=jnp.float32)
    return (query_part, key_part, value_part)


def body(query_rows, key_rows, value_rows, output_rows, output_grad, logsumexp, layout):
    shards = lax.axis_size("qb")
    myself = lax.axis_index("qb")
    width = query_rows.shape[1]
    scaling = width ** (-0.5)
    local_count = query_rows.shape[0] // BLK
    total = local_count * shards
    query_blocks = query_rows.reshape(local_count, BLK, width)
    grad_blocks = output_grad.reshape(local_count, BLK, width)
    kv_local = jnp.stack(
        [key_rows.reshape(local_count, BLK, width), value_rows.reshape(local_count, BLK, width)], 1
    )
    deltas = jnp.sum(output_grad.astype(jnp.float32) * output_rows.astype(jnp.float32), -1).reshape(
        local_count, BLK
    )
    lse_rows = logsumexp.reshape(local_count, BLK)
    blocks = myself * local_count + jnp.arange(local_count, dtype=jnp.int32)
    all_ones = jnp.ones((local_count,), jnp.float32)
    query_acc = jnp.zeros((local_count, BLK, width), jnp.float32)
    widened = with_halo(kv_local, (("qb", 0),), 1)
    rim_acc = jnp.zeros((local_count + 2, 2, BLK, width), jnp.float32)
    for offset in range(3):
        if offset == 0:
            masking = (blocks > 0).astype(jnp.float32)
        elif offset == 1:
            masking = all_ones
        else:
            masking = (blocks < total - 1).astype(jnp.float32)
        query_part, key_part, value_part = block_grads(
            query_blocks,
            widened[offset : offset + local_count, 0],
            widened[offset : offset + local_count, 1],
            grad_blocks,
            lse_rows,
            deltas,
            masking,
            scaling,
        )
        query_acc = query_acc + query_part
        rim_acc = rim_acc.at[offset : offset + local_count].add(
            jnp.stack([key_part, value_part], 1)
        )
    owned = rim_acc[1 : local_count + 1]
    border = jnp.stack([rim_acc[0], rim_acc[local_count + 1]])
    returned = with_halo(border.astype(jnp.bfloat16), (("qb", 0),), 1).astype(border.dtype)
    owned = owned.at[0].add(returned[0]).at[local_count - 1].add(returned[3])
    anchors = broadcast(kv_local[:GLOB], "qb", 0)
    sums_list = []
    for anchor in range(GLOB):
        key_same = jnp.broadcast_to(anchors[anchor, 0], query_blocks.shape)
        value_same = jnp.broadcast_to(anchors[anchor, 1], query_blocks.shape)
        query_part, key_part, value_part = block_grads(
            query_blocks, key_same, value_same, grad_blocks, lse_rows, deltas, all_ones, scaling
        )
        query_acc = query_acc + query_part
        sums_list.append(jnp.stack([jnp.sum(key_part, 0), jnp.sum(value_part, 0)]))
    totals = lax.psum(jnp.stack(sums_list), "qb")
    owned = owned.at[:GLOB].add(totals * (myself == 0).astype(jnp.float32))
    fanout = layout.shape[1]
    requests = local_count * fanout
    capacity = -(-requests // shards) + 1
    wanted = layout.reshape(shards, requests)
    owners = wanted // local_count
    in_owner = wanted % local_count
    devices = jnp.arange(shards, dtype=jnp.int32)
    onehot = (owners[:, :, None] == devices).astype(jnp.int32)
    ranking = jnp.sum(jnp.cumsum(onehot, 1) * onehot, -1) - 1
    my_owner = lax.dynamic_index_in_dim(owners, myself, 0, keepdims=False)
    my_rank = lax.dynamic_index_in_dim(ranking, myself, 0, keepdims=False)
    slot_index = my_owner * capacity + my_rank
    slots = jnp.arange(capacity, dtype=jnp.int32)
    hits = ((owners == myself)[:, :, None] & (ranking[:, :, None] == slots)).astype(jnp.int32)
    chosen = jnp.sum(hits * in_owner[:, :, None], 1).reshape(-1)
    present = jnp.sum(hits, 1).reshape(-1)
    buffer_rows = shards * capacity
    query_side = jnp.stack([query_blocks, grad_blocks], 1)
    stats = jnp.stack([lse_rows, deltas], 1)
    block_of = jnp.arange(requests, dtype=jnp.int32) // fanout
    query_out = (
        jnp.zeros((buffer_rows, 2, BLK, width), jnp.bfloat16)
        .at[slot_index]
        .set(query_side[block_of])
    )
    stats_out = jnp.zeros((buffer_rows, 2, BLK), jnp.float32).at[slot_index].set(stats[block_of])
    query_in = lax.all_to_all(
        query_out.reshape(shards, capacity, 2, BLK, width),
        "qb",
        split_axis=0,
        concat_axis=0,
        tiled=True,
    ).reshape(buffer_rows, 2, BLK, width)
    stats_in = lax.all_to_all(
        stats_out.reshape(shards, capacity, 2, BLK), "qb", split_axis=0, concat_axis=0, tiled=True
    ).reshape(buffer_rows, 2, BLK)
    span = 1
    while span * 2 <= max(1, 32 // capacity) and shards % (span * 2) == 0:
        span = span * 2
    group = span * capacity
    steps_count = shards // span
    local_ids = jnp.arange(local_count, dtype=jnp.int32)

    def owner_step(accum, item):
        query_item, stats_item, index_item, live_item = item
        kv_far = jnp.take(kv_local, index_item, axis=0)
        live_mask = (live_item > 0).astype(jnp.float32)
        query_part, key_part, value_part = block_grads(
            query_item[:, 0],
            kv_far[:, 0],
            kv_far[:, 1],
            query_item[:, 1],
            stats_item[:, 0],
            stats_item[:, 1],
            live_mask,
            scaling,
        )
        picker = ((index_item[:, None] == local_ids) & (live_item[:, None] > 0)).astype(jnp.float32)
        joined = jnp.stack([key_part, value_part], 1).reshape(group, -1)
        gained = jnp.dot(picker.T, joined, precision=lax.Precision.HIGHEST).reshape(
            local_count, 2, BLK, width
        )
        return (accum + gained, query_part.astype(jnp.bfloat16))

    inputs = (
        query_in.reshape(steps_count, group, 2, BLK, width),
        stats_in.reshape(steps_count, group, 2, BLK),
        chosen.reshape(steps_count, group),
        present.reshape(steps_count, group),
    )
    added, answer_out = lax.scan(
        owner_step, jnp.zeros((local_count, 2, BLK, width), jnp.float32), inputs
    )
    answers = lax.all_to_all(
        answer_out.reshape(shards, capacity, BLK, width),
        "qb",
        split_axis=0,
        concat_axis=0,
        tiled=True,
    ).reshape(buffer_rows, BLK, width)
    query_acc = query_acc + jnp.sum(
        jnp.take(answers, slot_index, axis=0)
        .astype(jnp.float32)
        .reshape(local_count, fanout, BLK, width),
        1,
    )
    owned = owned + added
    query_grad = query_acc.reshape(local_count * BLK, width).astype(jnp.bfloat16)
    key_grad = owned[:, 0].reshape(local_count * BLK, width).astype(jnp.bfloat16)
    value_grad = owned[:, 1].reshape(local_count * BLK, width).astype(jnp.bfloat16)
    return (query_grad, key_grad, value_grad)


def solution(mesh):
    in_specs = (
        P(("grp", "qb"), None),
        P(("grp", "qb"), None),
        P(("grp", "qb"), None),
        P(("grp", "qb"), None),
        P(("grp", "qb"), None),
        P(("grp", "qb")),
        P("grp", None),
    )
    out_specs = (P(("grp", "qb"), None), P(("grp", "qb"), None), P(("grp", "qb"), None))
    return jax.shard_map(body, mesh=mesh, in_specs=in_specs, out_specs=out_specs, check_vma=False)
```

profile of v0, /device:TPU:0, one launch (start us, length us, event | category | flops | bytes accessed | tf_op | source)
XLA Modules:
  0.0 387.7 jit_solution(3395903919044896074)
XLA Ops:
  11.6 1.4 multiply_reduce_fusion
  14.4 2.0 scatter_fusion.1
  17.1 7.4 %all-to-all-start.1 = ((f32[16,4,2,128]{3,1,2,0:T(4,128)}), f32[16,4,2,128]{3,1,2,0:T(4,128)S(1)}, u32[]{:S(2)}, u32[]{:S(2)}) async-start(f32[16,4,2,128]{3,1,2,0:T(4,128)} %copy.168), calls=%async_computation.1 | async-start | bytes 131072 | tf_op jit(solution)/shard_map/all_to_all | solution.py:139
  24.5 2.4 gather_fusion.1
  27.0 3.1 broadcast_in_dim.76
  30.0 8.6 %scatter_fusion = bf16[64,2,128,128]{3,2,1,0:T(8,128)(2,1)} fusion(bf16[64,2,128,128]{3,2,1,0:T(8,128)(2,1)} %broadcast_in_dim.76, s32[36]{0:T(128)S(1)} %get-tuple-element.251, bf16[36,2,128,128]{3,2,1,0:T(8,128)(2,1)} %gather_fusion.1), kind=kCustom, calls=%fused_computation.4 | custom fusion | bytes 7078032 | tf_op jit(solution)/shard_map/scatter | solution.py:129
  38.6 6.5 %all-to-all-start = ((bf16[16,4,2,128,128]{4,3,2,1,0:T(8,128)(2,1)}), bf16[16,4,2,128,128]{4,3,2,1,0:T(8,128)(2,1)}, u32[]{:S(2)}, u32[]{:S(2)}) async-start(bf16[16,4,2,128,128]{4,3,2,1,0:T(8,128)(2,1)} %bitcast.242), calls=%async_computation | async-start | bytes 8388608 | tf_op jit(solution)/shard_map/all_to_all | solution.py:132
  45.9 1.3 collective-permute-start.1
  47.2 3.0 collective-permute-start
  54.2 1.2 fusion.93
  60.1 1.2 copy-done.12
  61.3 1.3 collective-permute-start.3
  62.6 14.4 %collective-permute-start.2 = (bf16[1,2,128,128]{3,2,0,1:T(8,128)(2,1)S(1)}, bf16[1,2,128,128]{3,2,0,1:T(8,128)(2,1)}, u32[]{:S(2)}, u32[]{:S(2)}) collective-permute-start(bf16[1,2,128,128]{3,2,0,1:T(8,128)(2,1)S(1)} %slice.365), channel_id=1, source_target_pairs={{0,1},{1,2},{2,3},{3,4},{4,5},{5,6},{6,7},{7,8},{8,9},{9,10},{10,1... | collective-permute-start | bytes 196616 | tf_op jit(solution)/shard_map/ppermute | solution.py:17
  77.0 114.7 %all-reduce.4.cloned.1.call-done = bf16[2,2,128,128]{3,2,0,1:T(8,128)(2,1)} async-done(((bf16[2,2,128,128]{3,2,0,1:T(8,128)(2,1)}), bf16[2,2,128,128]{3,2,0,1:T(8,128)(2,1)}) %all-reduce.4.cloned.1.call-update) | async-done | bytes 131088 | tf_op jit(solution)/shard_map/psum | solution.py:25
  191.7 1.4 slice_bitcast_fusion.13
  193.2 1.3 fusion.35
  194.5 56.7 %while.19 = (s32[]{:T(128)}, f32[12,2,128,128]{3,0,2,1:T(8,128)}, bf16[2,32,128,128]{3,2,1,0:T(8,128)(2,1)}, s32[2,32]{1,0:T(2,128)}, s32[2,32]{1,0:T(2,128)S(1)...) while((s32[]{:T(128)}, f32[12,2,128,128]{3,0,2,1:T(8,128)}, ...), condition=%wide.region_9.10_spmd.clone, body=%wide.region_8.9_spmd.clone.sunk | while | flops 830212224 | bytes 130197952 | solution.py:176
  195.4 1.7 copy_bitcast_fusion.2
  197.7 2.3 gather_fusion
  200.0 1.2 compare_and_fusion.3
  201.2 1.8 copy_select_fusion.2
  203.1 1.4 exponential_multiply_fusion.2
  205.0 1.1 multiply_convert_fusion.3
  206.1 1.0 copy-done.2
  208.5 2.4 copy.210
  211.0 2.8 copy.211
  213.8 7.1 %select_add_fusion.2 = f32[12,2,128,128]{3,0,2,1:T(8,128)S(1)} fusion(f32[12,2,128,128]{3,0,2,1:T(8,128)S(1)} %copy-done.4, f32[2,128,128,32]{2,1,0,3:T(8,128)} %bitcast.218, pred[]{:T(512)S(6)} %compare.40, s32[32]{0:T(128)S(1)} %copy-done.36, pred[32]{0:T(512)(128)(4,1)S(1)} %copy-done.35), kind=kOutput, calls=%fused_computation.13.clone.1 | convolution fusion | flops 151782144 | bytes 7340193 | tf_op jit(solution)/shard_map/while/body/eval_jaxpr/dot_general | solution.py:165
  223.6 1.7 copy_bitcast_fusion.2
  225.9 2.3 gather_fusion
  228.3 1.2 compare_and_fusion.3
  229.4 1.8 copy_select_fusion.2
  231.3 1.4 exponential_multiply_fusion.2
  233.2 1.1 multiply_convert_fusion.3
  234.3 1.0 copy-done.2
  236.8 2.4 copy.210
  239.2 2.8 copy.211
  242.0 7.1 %select_add_fusion.2 = f32[12,2,128,128]{3,0,2,1:T(8,128)S(1)} fusion(f32[12,2,128,128]{3,0,2,1:T(8,128)S(1)} %copy-done.4, f32[2,128,128,32]{2,1,0,3:T(8,128)} %bitcast.218, pred[]{:T(512)S(6)} %compare.40, s32[32]{0:T(128)S(1)} %copy-done.36, pred[32]{0:T(512)(128)(4,1)S(1)} %copy-done.35), kind=kOutput, calls=%fused_computation.13.clone.1 | convolution fusion | flops 151782144 | bytes 7340193 | tf_op jit(solution)/shard_map/while/body/eval_jaxpr/dot_general | solution.py:165
  251.2 6.5 %all-to-all-start.2 = ((bf16[16,4,128,128]{3,2,1,0:T(8,128)(2,1)}), bf16[16,4,128,128]{3,2,1,0:T(8,128)(2,1)}, u32[]{:S(2)}, u32[]{:S(2)}) async-start(bf16[16,4,128,128]{3,2,1,0:T(8,128)(2,1)} %bitcast.265), calls=%async_computation.2 | async-start | bytes 4194304 | tf_op jit(solution)/shard_map/all_to_all | solution.py:179
  262.8 1.2 copy-done.13
  263.9 1.3 slice.306
  265.2 1.5 fusion.76
  266.7 1.6 fusion.75
  268.3 103.8 %all-reduce.6.cloned.1.call-done = f32[2,2,128,128]{3,2,0,1:T(8,128)} async-done(((f32[2,2,128,128]{3,2,0,1:T(8,128)}), f32[2,2,128,128]{3,2,0,1:T(8,128)}) %all-reduce.6.cloned.1.call-update) | async-done | bytes 262160 | tf_op jit(solution)/shard_map/psum | solution.py:104
  372.1 1.8 fusion.64
  373.9 2.0 fusion.17
  375.8 0.9 fusion.91
  376.8 2.5 gather_fusion.3
  379.7 1.1 fusion.42
  (211 shorter events, 31.4 us)
Async XLA Ops:
  7.2 17.3 %copy-start.7 = (bf16[1536,128]{1,0:T(8,128)(2,1)S(1)}, bf16[1536,128]{1,0:T(8,128)(2,1)}, u32[]{:S(2)}) copy-start(bf16[1536,128]{1,0:T(8,128)(2,1)} %param.25) | copy-start | bytes 1179652
  7.2 17.3 %copy-start.14 = (bf16[1536,128]{1,0:T(8,128)(2,1)S(1)}, bf16[1536,128]{1,0:T(8,128)(2,1)}, u32[]{:S(2)}) copy-start(bf16[1536,128]{1,0:T(8,128)(2,1)} %param.21) | copy-start | bytes 1179652
  17.1 21.5 %all-to-all-start.1 = ((f32[16,4,2,128]{3,1,2,0:T(4,128)}), f32[16,4,2,128]{3,1,2,0:T(4,128)S(1)}, u32[]{:S(2)}, u32[]{:S(2)}) async-start(f32[16,4,2,128]{3,1,2,0:T(4,128)} %copy.168), calls=%async_computation.1 | async-start | bytes 131072 | tf_op jit(solution)/shard_map/all_to_all | solution.py:139
  38.6 6.5 %copy-start.8 = (bf16[1536,128]{1,0:T(8,128)(2,1)S(1)}, bf16[1536,128]{1,0:T(8,128)(2,1)}, u32[]{:S(2)}) copy-start(bf16[1536,128]{1,0:T(8,128)(2,1)} %param.22) | copy-start | bytes 1179652
  38.6 6.6 %copy-start.10 = (bf16[1536,128]{1,0:T(8,128)(2,1)S(1)}, bf16[1536,128]{1,0:T(8,128)(2,1)}, u32[]{:S(2)}) copy-start(bf16[1536,128]{1,0:T(8,128)(2,1)} %param.23) | copy-start | bytes 1179652
  38.6 155.9 %all-to-all-start = ((bf16[16,4,2,128,128]{4,3,2,1,0:T(8,128)(2,1)}), bf16[16,4,2,128,128]{4,3,2,1,0:T(8,128)(2,1)}, u32[]{:S(2)}, u32[]{:S(2)}) async-start(bf16[16,4,2,128,128]{4,3,2,1,0:T(8,128)(2,1)} %bitcast.242), calls=%async_computation | async-start | bytes 8388608 | tf_op jit(solution)/shard_map/all_to_all | solution.py:132
  45.1 146.7 %all-reduce.4.cloned.1.call-start = ((), (), s32[]{:S(2)}) async-start(), calls=%async_computation.3 | async-start | bytes 262144 | tf_op jit(solution)/shard_map/psum | solution.py:25
  45.9 6.3 %copy-start.32 = (f32[1536]{0:T(1024)S(1)}, f32[1536]{0:T(1024)}, u32[]{:S(2)}) copy-start(f32[1536]{0:T(1024)} %param.26) | copy-start | bytes 18436
  45.9 10.6 %collective-permute-start.1 = (bf16[1,2,128,128]{3,2,0,1:T(8,128)(2,1)S(1)}, bf16[1,2,128,128]{3,2,0,1:T(8,128)(2,1)S(1)}, u32[]{:S(2)}, u32[]{:S(2)}) collective-permute-start(bf16[1,2,128,128]{3,2,0,1:T(8,128)(2,1)S(1)} %get-tuple-element.243), channel_id=1, source_target_pairs={{1,0},{2,1},{3,2},{4,3},{5,4},{6,5},{7,6},{8,7},{9,8},{10,9},{11,1... | collective-permute-start | bytes 196616 | tf_op jit(solution)/shard_map/ppermute | solution.py:18
  47.2 8.2 %collective-permute-start = (bf16[1,2,128,128]{3,2,0,1:T(8,128)(2,1)S(1)}, bf16[1,2,128,128]{3,2,0,1:T(8,128)(2,1)S(1)}, u32[]{:S(2)}, u32[]{:S(2)}) collective-permute-start(bf16[1,2,128,128]{3,2,0,1:T(8,128)(2,1)S(1)} %get-tuple-element.242), channel_id=1, source_target_pairs={{0,1},{1,2},{2,3},{3,4},{4,5},{5,6},{6,7},{7,8},{8,9},{9,10},{10,1... | collective-permute-start | bytes 196616 | tf_op jit(solution)/shard_map/ppermute | solution.py:17
  61.3 203.9 %collective-permute-start.3 = (bf16[1,2,128,128]{3,2,0,1:T(8,128)(2,1)S(1)}, bf16[1,2,128,128]{3,2,0,1:T(8,128)(2,1)}, u32[]{:S(2)}, u32[]{:S(2)}) collective-permute-start(bf16[1,2,128,128]{3,2,0,1:T(8,128)(2,1)S(1)} %slice.364), channel_id=1, source_target_pairs={{1,0},{2,1},{3,2},{4,3},{5,4},{6,5},{7,6},{8,7},{9,8},{10,9},{11,1... | collective-permute-start | bytes 196616 | tf_op jit(solution)/shard_map/ppermute | solution.py:18
  62.6 202.6 %collective-permute-start.2 = (bf16[1,2,128,128]{3,2,0,1:T(8,128)(2,1)S(1)}, bf16[1,2,128,128]{3,2,0,1:T(8,128)(2,1)}, u32[]{:S(2)}, u32[]{:S(2)}) collective-permute-start(bf16[1,2,128,128]{3,2,0,1:T(8,128)(2,1)S(1)} %slice.365), channel_id=1, source_target_pairs={{0,1},{1,2},{2,3},{3,4},{4,5},{5,6},{6,7},{7,8},{8,9},{9,10},{10,1... | collective-permute-start | bytes 196616 | tf_op jit(solution)/shard_map/ppermute | solution.py:17
  195.3 1.7 copy-start.38
  201.2 1.9 copy-start.37
  203.1 1.9 copy-start
  211.0 2.8 copy-start.4
  211.0 2.8 copy-start.35
  211.0 2.8 copy-start.36
  213.8 7.2 %copy-start.1 = (bf16[32,2,128,128]{3,2,0,1:T(8,128)(2,1)S(1)}, bf16[32,2,128,128]{3,2,0,1:T(8,128)(2,1)}, u32[]{:S(2)}) copy-start(bf16[32,2,128,128]{3,2,0,1:T(8,128)(2,1)} %copy-done) | copy-start | bytes 6291460 | tf_op jit(solution)/shard_map/while
  213.8 7.2 %copy-start.3 = (bf16[32,128,128]{2,1,0:T(8,128)(2,1)S(1)}, bf16[32,128,128]{2,1,0:T(8,128)(2,1)}, u32[]{:S(2)}) copy-start(bf16[32,128,128]{2,1,0:T(8,128)(2,1)} %copy-done.2) | copy-start | bytes 3145732 | tf_op jit(solution)/shard_map/while
  213.8 7.2 %copy-start.22 = (bf16[2,32,128,128]{3,2,1,0:T(8,128)(2,1)S(1)}, bf16[2,32,128,128]{3,2,1,0:T(8,128)(2,1)}, u32[]{:S(2)}) copy-start(bf16[2,32,128,128]{3,2,1,0:T(8,128)(2,1)} %get-tuple-element.329) | copy-start | bytes 6291460 | tf_op jit(solution)/shard_map/while
  221.0 2.0 copy-start.40
  221.6 1.4 copy-start.23
  223.6 1.7 copy-start.38
  229.4 1.9 copy-start.37
  231.3 1.9 copy-start
  239.2 2.8 copy-start.4
  239.2 2.8 copy-start.35
  239.2 2.8 copy-start.36
  242.0 7.2 %copy-start.1 = (bf16[32,2,128,128]{3,2,0,1:T(8,128)(2,1)S(1)}, bf16[32,2,128,128]{3,2,0,1:T(8,128)(2,1)}, u32[]{:S(2)}) copy-start(bf16[32,2,128,128]{3,2,0,1:T(8,128)(2,1)} %copy-done) | copy-start | bytes 6291460 | tf_op jit(solution)/shard_map/while
  242.0 7.2 %copy-start.3 = (bf16[32,128,128]{2,1,0:T(8,128)(2,1)S(1)}, bf16[32,128,128]{2,1,0:T(8,128)(2,1)}, u32[]{:S(2)}) copy-start(bf16[32,128,128]{2,1,0:T(8,128)(2,1)} %copy-done.2) | copy-start | bytes 3145732 | tf_op jit(solution)/shard_map/while
  242.0 7.2 %copy-start.22 = (bf16[2,32,128,128]{3,2,1,0:T(8,128)(2,1)S(1)}, bf16[2,32,128,128]{3,2,1,0:T(8,128)(2,1)}, u32[]{:S(2)}) copy-start(bf16[2,32,128,128]{3,2,1,0:T(8,128)(2,1)} %get-tuple-element.329) | copy-start | bytes 6291460 | tf_op jit(solution)/shard_map/while
  249.2 2.0 copy-start.40
  249.8 1.4 copy-start.23
  251.2 6.6 %copy-start.16 = (f32[12,128,128]{2,1,0:T(8,128)S(1)}, f32[12,128,128]{2,1,0:T(8,128)}, u32[]{:S(2)}) copy-start(f32[12,128,128]{2,1,0:T(8,128)} %fusion.35) | copy-start | bytes 2359300
  251.2 6.6 %copy-start.34 = (bf16[128,128]{1,0:T(8,128)(2,1)S(1)}, bf16[128,128]{1,0:T(8,128)(2,1)}, u32[]{:S(2)}) copy-start(bf16[128,128]{1,0:T(8,128)(2,1)} %get-tuple-element.246) | copy-start | bytes 98308
  251.2 7.0 %copy-start.15 = (bf16[1536,128]{1,0:T(8,128)(2,1)S(1)}, bf16[1536,128]{1,0:T(8,128)(2,1)}, u32[]{:S(2)}) copy-start(bf16[1536,128]{1,0:T(8,128)(2,1)} %param.21) | copy-start | bytes 1179652
  251.2 125.6 %all-to-all-start.2 = ((bf16[16,4,128,128]{3,2,1,0:T(8,128)(2,1)}), bf16[16,4,128,128]{3,2,1,0:T(8,128)(2,1)}, u32[]{:S(2)}, u32[]{:S(2)}) async-start(bf16[16,4,128,128]{3,2,1,0:T(8,128)(2,1)} %bitcast.265), calls=%async_computation.2 | async-start | bytes 4194304 | tf_op jit(solution)/shard_map/all_to_all | solution.py:179
  257.8 114.3 %all-reduce.6.cloned.1.call-start = ((), (), s32[]{:S(2)}) async-start(), calls=%async_computation.4 | async-start | bytes 524288 | tf_op jit(solution)/shard_map/psum | solution.py:104
  260.3 1.4 copy-start.9
  260.6 1.4 copy-start.27
  260.9 1.5 copy-start.18
  261.0 1.5 copy-start.21
  261.0 1.5 copy-start.29
  262.4 1.5 copy-start.13
  263.9 109.9 %copy-start.6 = (f32[12,2,128,128]{3,0,2,1:T(8,128)S(1)}, f32[12,2,128,128]{3,0,2,1:T(8,128)}, u32[]{:S(2)}) copy-start(f32[12,2,128,128]{3,0,2,1:T(8,128)} %get-tuple-element.124) | copy-start | bytes 4718596
  375.8 3.5 copy-start.41
  376.8 3.0 copy-start.25
  (17 other events, 18.0 us)
Sparse Core Ops, SparseCore 0:
  50.0 141.7 all-reduce.3
  262.0 110.0 all-reduce.5
where the time goes:
time: 389 us; the launch traced here: 388 us
  waiting for transfers between devices  219 us (56%)
  local copies, waits for them, and re-layouts  54.5 us (14%)
  starting transfers between devices  40.5 us (10%)
  matrix products  33.2 us (9%)
  other arithmetic  25.5 us (7%)
  between operations  14.8 us (4%)
    psum x1, waiting for transfers between devices, broadcast(): return lax.psum(block, axis)  115 us
    psum x1, waiting for transfers between devices, body(): totals = lax.psum(jnp.stack(sums_list), 'qb')  104 us
    ppermute x2, starting transfers between devices, with_halo(): before = lax.ppermute(last, axis, up)  17.4 us
    while x60, local copies, waits for them, and re-layouts  15.2 us
    dot_general x2, matrix products, owner_step(): jnp.dot(picker.T, joined, precision=lax.Precision.HIGHEST)  14.3 us
    scatter x1, local copies, waits for them, and re-layouts, body(): query_out = jnp.zeros((buffer_rows, 2, BLK, width), jnp.bfloat16).at[slot...  8.55 us
  transfers between devices with their start and end apart: 9, of which 2 were waited for; matrix products, arithmetic and copies ran while one was open for 23% of the time, Pallas kernels for 0%

commit v1 on v0

v1 whole, which is shorter than its diff:
```python
import functools

import jax
import jax.numpy as jnp
from jax import lax
from jax.experimental import pallas as pl
from jax.experimental.pallas import tpu as pltpu
from jax.sharding import PartitionSpec as P

BLK = 128
GLOB = 2
STAT = 16
PAIRS = 2
FAR = 1e30


def pieces(row):
    high = row.astype(jnp.bfloat16)
    rest = row - high.astype(jnp.float32)
    middle = rest.astype(jnp.bfloat16)
    low = (rest - middle.astype(jnp.float32)).astype(jnp.bfloat16)
    return [high.astype(jnp.float32), middle.astype(jnp.float32), low.astype(jnp.float32)]


def pack_kernel(query, grad, output, key, value, lse, unit, keyval):
    count = unit.shape[0]
    width = unit.shape[2]

    def block(b, carry):
        rows = pl.ds(pl.multiple_of(b * BLK, BLK), BLK)
        grads = grad[rows, :]
        unit[b, 0:BLK] = query[rows, :]
        unit[b, BLK : 2 * BLK] = grads
        keyval[b, 0] = key[rows, :]
        keyval[b, 1] = value[rows, :]
        product = grads.astype(jnp.float32) * output[rows, :].astype(jnp.float32)
        delta = jnp.sum(product.T, axis=0, keepdims=True)
        stats = pieces(lse[pl.ds(b, 1), :]) + pieces(delta)
        stats.append(jnp.zeros((STAT - len(stats), width), jnp.float32))
        unit[b, 2 * BLK :] = jnp.concatenate(stats, 0).astype(jnp.bfloat16)
        return carry

    lax.fori_loop(0, count, block, 0)


def pack(query, grad, output, key, value, lse):
    count, width = (query.shape[0] // BLK, query.shape[1])
    return pl.pallas_call(
        pack_kernel,
        out_shape=(
            jax.ShapeDtypeStruct((count, 2 * BLK + STAT, width), jnp.bfloat16),
            jax.ShapeDtypeStruct((count, 2, BLK, width), jnp.bfloat16),
        ),
        name="pack",
    )(query, grad, output, key, value, lse)


def pair_grads(keys, values, queries, grads, lse, delta, scaling, mask=None):
    scores = lax.dot_general(
        keys, queries, (((1,), (1,)), ((), ())), preferred_element_type=jnp.float32
    )
    probability = jnp.exp(scores * scaling - lse)
    if mask is not None:
        probability = jnp.where(mask, probability, 0.0)
    dweights = lax.dot_general(
        values, grads, (((1,), (1,)), ((), ())), preferred_element_type=jnp.float32
    )
    score_low = (probability * (dweights - delta)).astype(jnp.bfloat16)
    prob_low = probability.astype(jnp.bfloat16)
    value_part = jnp.dot(prob_low, grads, preferred_element_type=jnp.float32)
    key_part = jnp.dot(score_low, queries, preferred_element_type=jnp.float32)
    query_part = lax.dot_general(
        score_low, keys, (((0,), (0,)), ((), ())), preferred_element_type=jnp.float32
    )
    return query_part, key_part, value_part


def step_kernel(plan, me_ref, layout_ref, *refs):
    offsets, span, fanout, scaling, first, last = plan
    visits = len(offsets)
    refs = list(refs)
    units = [refs.pop(0) for _ in range(visits)]
    keyvals = [refs.pop(0) for _ in range(span)]
    acc_in = None if first else refs.pop(0)
    dq_out = [refs.pop(0) for _ in range(visits)]
    if last:
        send_out, keep_out = (refs.pop(0), refs.pop(0))
    else:
        acc_out = refs.pop(0)
    unit_s, kv_s, acc_s, dq_s, who, whom, far, sems, acc_sem = refs
    count = unit_s.shape[1]
    width = unit_s.shape[3]
    held = span * count
    me = me_ref[0]
    shards = me_ref[1]
    seat = lax.rem(me, span)
    row = lax.div(me, span)
    low = row * held

    loads = []
    for m in range(span):
        other = jnp.bitwise_xor(seat, m)
        loads.append(
            pltpu.make_async_copy(
                keyvals[m], kv_s.at[pl.ds(other * count, count)], sems.at[visits + m]
            )
        )
    for v in range(visits):
        loads.append(pltpu.make_async_copy(units[v], unit_s.at[v], sems.at[v]))
    for load in loads:
        load.start()
    if not first:
        load = pltpu.make_async_copy(acc_in, acc_s, acc_sem)
        load.start()
        loads.append(load)
    else:

        def clear(b, carry):
            acc_s[b] = jnp.zeros(acc_s.shape[1:], jnp.float32)
            return carry

        lax.fori_loop(0, held, clear, 0)

    def clear_dq(b, carry):
        for v in range(visits):
            dq_s[v, b] = jnp.zeros(dq_s.shape[2:], jnp.float32)
        return carry

    lax.fori_loop(0, count, clear_dq, 0)
    for load in loads:
        load.wait()

    def stats(v, q):
        rows = unit_s[v, q, 2 * BLK :].astype(jnp.float32)
        lse = rows[0:1] + rows[1:2] + rows[2:3]
        delta = rows[3:4] + rows[4:5] + rows[5:6]
        return lse, delta

    def window(v):
        def step(q, carry):
            at = seat * count + q
            start = jnp.clip(at - 1, 0, held - 3)
            keys = kv_s[pl.ds(start, 3), 0].reshape(3 * BLK, width)
            values = kv_s[pl.ds(start, 3), 1].reshape(3 * BLK, width)
            lse, delta = stats(v, q)
            block = lax.broadcasted_iota(jnp.int32, (3 * BLK, BLK), 0) // BLK + start - at
            query_part, key_part, value_part = pair_grads(
                keys,
                values,
                unit_s[v, q, 0:BLK],
                unit_s[v, q, BLK : 2 * BLK],
                lse,
                delta,
                scaling,
                (block >= -1) & (block <= 1),
            )
            dq_s[v, q] += query_part
            acc_s[pl.ds(start, 3), 0] += key_part.reshape(3, BLK, width)
            acc_s[pl.ds(start, 3), 1] += value_part.reshape(3, BLK, width)
            return carry

        lax.fori_loop(0, count, step, 0)

    def anchors(v):
        chunk = 2 if count % 2 == 0 else 1

        def step(c, carry):
            blocks = pl.ds(c * chunk, chunk)
            queries = unit_s[v, blocks, 0:BLK].reshape(chunk * BLK, width)
            grads = unit_s[v, blocks, BLK : 2 * BLK].reshape(chunk * BLK, width)
            lines = [stats(v, c * chunk + k) for k in range(chunk)]
            lse = jnp.concatenate([line[0] for line in lines], 1)
            delta = jnp.concatenate([line[1] for line in lines], 1)
            query_part, key_part, value_part = pair_grads(
                kv_s[0:GLOB, 0].reshape(GLOB * BLK, width),
                kv_s[0:GLOB, 1].reshape(GLOB * BLK, width),
                queries,
                grads,
                lse,
                delta,
                scaling,
            )
            dq_s[v, blocks] += query_part.reshape(chunk, BLK, width)
            acc_s[0:GLOB, 0] += key_part.reshape(GLOB, BLK, width)
            acc_s[0:GLOB, 1] += value_part.reshape(GLOB, BLK, width)
            return carry

        lax.fori_loop(0, count // chunk, step, 0)

    def scattered(v, guest, near):
        def note(at, q, target):
            local = target - low
            hit = (local >= 0) & (local < held)

            @pl.when(hit)
            def _():
                who[at] = q
                whom[at] = local
                far[at] = 0.0

            return at + hit.astype(jnp.int32)

        def gather(q, at):
            block = guest * count + q
            for r in range(fanout):
                at = note(at, q, layout_ref[block * fanout + r])
            if near:
                at = note(at, q, block - 1)
                at = note(at, q, block + 1)
            return at

        found = lax.fori_loop(0, count, gather, 0)
        for k in range(PAIRS - 1):
            who[found + k] = 0
            whom[found + k] = 0
            far[found + k] = FAR

        def step(g, carry):
            places, parts = ([], [])
            for k in range(PAIRS):
                at = g * PAIRS + k
                q, j = (who[at], whom[at])
                lse, delta = stats(v, q)
                places.append((q, j))
                parts.append(
                    pair_grads(
                        kv_s[j, 0],
                        kv_s[j, 1],
                        unit_s[v, q, 0:BLK],
                        unit_s[v, q, BLK : 2 * BLK],
                        lse + far[at],
                        delta,
                        scaling,
                    )
                )
            for (q, j), (query_part, key_part, value_part) in zip(places, parts):
                dq_s[v, q] += query_part
                acc_s[j, 0] += key_part
                acc_s[j, 1] += value_part
            return carry

        lax.fori_loop(0, (found + PAIRS - 1) // PAIRS, step, 0)

    for v, offset in enumerate(offsets):
        guest = me + offset * span
        if offset == 0:
            window(v)

        @pl.when((guest >= 0) & (guest < shards))
        def _(v=v, offset=offset, guest=guest):
            @pl.when(row == 0)
            def _():
                anchors(v)

            scattered(v, guest, abs(offset) == 1)

    def finish_dq(q, carry):
        for v in range(visits):
            dq_out[v][q] = (dq_s[v, q] * scaling).astype(dq_out[v].dtype)
        return carry

    lax.fori_loop(0, count, finish_dq, 0)
    if last:

        def finish(b, carry):
            for k in range(span // 2):
                mine = jnp.bitwise_xor(seat, 2 * k) * count + b
                theirs = jnp.bitwise_xor(seat, 2 * k + 1) * count + b
                keep_out[k, b, 0] = acc_s[mine, 0] * scaling
                keep_out[k, b, 1] = acc_s[mine, 1]
                send_out[k, b, 0] = (acc_s[theirs, 0] * scaling).astype(jnp.bfloat16)
                send_out[k, b, 1] = acc_s[theirs, 1].astype(jnp.bfloat16)
            return carry

        lax.fori_loop(0, count, finish, 0)
    else:
        store = pltpu.make_async_copy(acc_s, acc_out, acc_sem)
        store.start()
        store.wait()


def visit(me, layout, units, offsets, keyvals, acc, last, fanout):
    span = len(keyvals)
    visits = len(units)
    count, _, width = units[0].shape
    first = acc is None
    scaling = width ** (-0.5)
    plan = (offsets, span, fanout, scaling, first, last)
    held = span * count
    smem = pl.BlockSpec(memory_space=pltpu.SMEM)
    hbm = pl.BlockSpec(memory_space=pl.ANY)
    vmem = pl.BlockSpec(memory_space=pltpu.VMEM)
    kinds = [jnp.float32 if offset == 0 else jnp.bfloat16 for offset in offsets]
    outs = [jax.ShapeDtypeStruct((count, BLK, width), kind) for kind in kinds]
    out_specs = [vmem] * visits
    if last:
        outs.append(jax.ShapeDtypeStruct((span // 2, count, 2, BLK, width), jnp.bfloat16))
        outs.append(jax.ShapeDtypeStruct((span // 2, count, 2, BLK, width), jnp.float32))
        out_specs += [vmem, vmem]
    else:
        outs.append(jax.ShapeDtypeStruct((held, 2, BLK, width), jnp.float32))
        out_specs.append(hbm)
    entries = count * (fanout + 2) + PAIRS
    pairs = visits * count * 2 + (3 * count if first else 0)
    return pl.pallas_call(
        functools.partial(step_kernel, plan),
        out_shape=outs,
        in_specs=[smem, smem] + [hbm] * (visits + span + (0 if first else 1)),
        out_specs=out_specs,
        scratch_shapes=[
            pltpu.VMEM((visits,) + units[0].shape, jnp.bfloat16),
            pltpu.VMEM((held, 2, BLK, width), jnp.bfloat16),
            pltpu.VMEM((held, 2, BLK, width), jnp.float32),
            pltpu.VMEM((visits, count, BLK, width), jnp.float32),
            pltpu.SMEM((entries,), jnp.int32),
            pltpu.SMEM((entries,), jnp.int32),
            pltpu.SMEM((entries,), jnp.float32),
            pltpu.SemaphoreType.DMA((visits + span,)),
            pltpu.SemaphoreType.DMA(()),
        ],
        compiler_params=pltpu.CompilerParams(vmem_limit_bytes=40 * 2**20),
        cost_estimate=pl.CostEstimate(
            flops=pairs * 10 * BLK * BLK * width,
            bytes_accessed=16 * 2**20,
            transcendentals=pairs * BLK * BLK,
        ),
        name="visit",
    )(me, layout, *units, *keyvals, *([] if first else [acc]))


def body(query_rows, key_rows, value_rows, output_rows, output_grad, logsumexp, layout):
    shards = lax.axis_size("qb")
    myself = lax.axis_index("qb")
    width = query_rows.shape[1]
    count = query_rows.shape[0] // BLK
    fanout = layout.shape[1]
    span = 4
    while shards // span > 16:
        span = span * 2
    planes = shards // span

    def send(array, pairs):
        return lax.ppermute(array, "qb", pairs)

    def swap(array, bit):
        return send(array, [(i, i ^ bit) for i in range(shards)])

    def shift(array, planes_away, low, high):
        return send(
            array,
            [
                (p * span + e, (p + planes_away) * span + e)
                for p in range(low, high)
                for e in range(span)
            ],
        )

    unit, keyval = pack(
        query_rows, output_grad, output_rows, key_rows, value_rows, logsumexp.reshape(count, BLK)
    )
    keyvals = {0: keyval}
    bit = span // 2
    while bit:
        for m in list(keyvals):
            keyvals[m | bit] = swap(keyvals[m], bit)
        bit = bit // 2
    keyvals = [keyvals[m] for m in range(span)]
    me = jnp.stack([myself, jnp.int32(shards)]).astype(jnp.int32)
    entries = layout.reshape(-1)

    up, down = (unit, unit)
    ups, downs = ([], [])
    for s in range(1, planes):
        up = shift(up, 1, s - 1, planes - 1)
        down = shift(down, -1, 1, planes - s + 1)
        ups.append(up)
        downs.append(down)

    acc = None
    up_parts, down_parts = ([], [])
    for s in range(1, planes):
        guests, offsets = ([ups[s - 1], downs[s - 1]], [-s, s])
        if s == 1:
            guests, offsets = ([unit] + guests, [0] + offsets)
        last = s == planes - 1
        outs = list(visit(me, entries, guests, tuple(offsets), keyvals, acc, last, fanout))
        if s == 1:
            query_acc = outs.pop(0)
        up_parts.append(outs.pop(0))
        down_parts.append(outs.pop(0))
        if last:
            sent, kept = outs
        else:
            acc = outs[0]

    def merge(one, two):
        return (one.astype(jnp.float32) + two.astype(jnp.float32)).astype(jnp.bfloat16)

    far = planes - 1
    query_acc = query_acc + shift(up_parts[-1], -far, far, planes).astype(jnp.float32)
    query_acc = query_acc + shift(down_parts[-1], far, 0, 1).astype(jnp.float32)
    up_back, down_back = (None, None)
    for s in range(planes - 2, 0, -1):
        up_back = up_parts[s - 1] if up_back is None else merge(up_parts[s - 1], up_back)
        down_back = down_parts[s - 1] if down_back is None else merge(down_parts[s - 1], down_back)
        up_back = shift(up_back, -1, s, planes)
        down_back = shift(down_back, 1, 0, planes - s)
    if up_back is not None:
        query_acc = query_acc + up_back.astype(jnp.float32) + down_back.astype(jnp.float32)

    bit = 1
    while True:
        kept = kept + swap(sent, bit).astype(jnp.float32)
        bit = bit * 2
        if bit == span:
            break
        halves = kept.reshape((kept.shape[0] // 2, 2) + kept.shape[1:])
        kept = halves[:, 0]
        sent = halves[:, 1].astype(jnp.bfloat16)
    owned = kept[0]
    query_grad = query_acc.reshape(count * BLK, width).astype(jnp.bfloat16)
    key_grad = owned[:, 0].reshape(count * BLK, width).astype(jnp.bfloat16)
    value_grad = owned[:, 1].reshape(count * BLK, width).astype(jnp.bfloat16)
    return (query_grad, key_grad, value_grad)


def solution(mesh):
    in_specs = (
        P(("grp", "qb"), None),
        P(("grp", "qb"), None),
        P(("grp", "qb"), None),
        P(("grp", "qb"), None),
        P(("grp", "qb"), None),
        P(("grp", "qb")),
        P("grp", None),
    )
    out_specs = (P(("grp", "qb"), None), P(("grp", "qb"), None), P(("grp", "qb"), None))
    return jax.shard_map(body, mesh=mesh, in_specs=in_specs, out_specs=out_specs, check_vma=False)
```

time: 389 us -> 145 us (0.37)
  waiting for transfers between devices: 219 us -> 55.9 us
  Pallas kernels: 0 us -> 47.1 us
  local copies, waits for them, and re-layouts: 54.5 us -> 13.7 us
  matrix products: 33.2 us -> 0 us
  other arithmetic: 25.5 us -> 2.16 us
  starting transfers between devices: 40.5 us -> 24.5 us
  between operations: 14.8 us -> 0.89 us
    psum x2 -> x0, waiting for transfers between devices: 219 us -> none  [the longest x1 115 us: broadcast(): return lax.psum(block, axis)]
    ppermute x4 -> x17, waiting for transfers between devices: 0.01 us -> 55.9 us  [send(): return lax.ppermute(array, 'qb', pairs)]
    pallas_call x0 -> x4, Pallas kernels: none -> 47.1 us  [the longest x3 43.1 us: visit(): pl.pallas_call(functools.partial(step_kernel, plan), out_shape=outs, in_s...]
    dot_general x37 -> x0, matrix products: 33.2 us -> none  [the longest x2 14.3 us: owner_step(): jnp.dot(picker.T, joined, precision=lax.Precision.HIGHEST)]
    all_to_all x3 -> x0, starting transfers between devices: 20.4 us -> none  [the longest x1 7.36 us: body(): lax.all_to_all(stats_out.reshape(shards, capacity, 2, BLK), 'qb', split_a...]
    while x60 -> x0, local copies, waits for them, and re-layouts: 15.2 us -> none
    scatter x2 -> x0, local copies, waits for them, and re-layouts: 10.6 us -> none  [the longest x1 8.55 us: body(): query_out = jnp.zeros((buffer_rows, 2, BLK, width), jnp.bfloat16).at[slot...]
    gather x5 -> x0, local copies, waits for them, and re-layouts: 10.2 us -> none  [the longest x2 4.61 us: owner_step(): kv_far = jnp.take(kv_local, index_item, axis=0)]
  transfers between devices with their start and end apart: 9 -> 17, of which waited for: 2 -> 6; matrix products, arithmetic and copies ran while one was open for 23% -> 2% of each run, Pallas kernels for 0% -> 22%
where the time goes in v1:
time: 145 us; the launch traced here: 144 us
  waiting for transfers between devices  55.9 us (39%)
  Pallas kernels  47.1 us (32%)
  starting transfers between devices  24.5 us (17%)
  local copies, waits for them, and re-layouts  13.7 us (9%)
  other arithmetic  2.16 us (1%)
    ppermute x17, waiting for transfers between devices, send(): return lax.ppermute(array, 'qb', pairs)  55.9 us
    pallas_call x3, Pallas kernels, visit(): pl.pallas_call(functools.partial(step_kernel, plan), out_shape=outs, in_s...  43.1 us
    ppermute x17, starting transfers between devices, send(): return lax.ppermute(array, 'qb', pairs)  24.5 us
    unnamed x19, local copies, waits for them, and re-layouts  12.4 us
    pallas_call x1, Pallas kernels, pack(): pl.pallas_call(pack_kernel, out_shape=(jax.ShapeDtypeStruct((count, 2 * B...  4.04 us
  transfers between devices with their start and end apart: 17, of which 6 were waited for; matrix products, arithmetic and copies ran while one was open for 2% of the time, Pallas kernels for 22%

profile of v1, /device:TPU:0, one launch (start us, length us, event | category | flops | bytes accessed | tf_op | source)
XLA Modules:
  0.0 144.3 jit_solution(15049518232179503394)
XLA Ops:
  0.6 4.0 %pack.1 = (bf16[12,272,128]{2,1,0:T(8,128)(2,1)}, bf16[12,2,128,128]{3,2,1,0:T(8,128)(2,1)}) custom-call(bf16[1536,128]{1,0:T(8,128)(2,1)} %query.1, bf16[1536,128]{1,0:T(8,128)(2,1)} %grad.1, bf16[1536,128]{1,0:T(8,128)(2,1)} %output.1, bf16[1536,128]{1,0:T(8,128)(2,1)} %key.1, bf16[1536,128]{1,0:T(8,128)(2,1)} %value.1, f32[12,128]{1,0:T(8,128)} %bitcast.22), custom_call_target="tpu_custom_call" | custom-call | tf_op jit(solution)/shard_map/pack/pallas_call | solution.py:48
  4.7 5.0 %collective-permute-start = (bf16[12,272,128]{2,1,0:T(8,128)(2,1)}, bf16[12,272,128]{2,1,0:T(8,128)(2,1)S(1)}, u32[]{:S(2)}, u32[]{:S(2)}) collective-permute-start(bf16[12,272,128]{2,1,0:T(8,128)(2,1)} %get-tuple-element.16.refs_0_), channel_id=1, source_target_pairs={{0,4},{1,5},{2,6},{3,7},{4,8},{5,9},{6,10},{7,11},{8,12},{9,13},{1... | collective-permute-start | bytes 2506760 | tf_op jit(solution)/shard_map/ppermute | solution.py:343
  9.6 1.3 collective-permute-start.1
  10.9 1.6 %collective-permute-start.3 = (bf16[12,2,128,128]{3,2,1,0:T(8,128)(2,1)}, bf16[12,2,128,128]{3,2,1,0:T(8,128)(2,1)S(1)}, u32[]{:S(2)}, u32[]{:S(2)}) collective-permute-start(bf16[12,2,128,128]{3,2,1,0:T(8,128)(2,1)} %get-tuple-element.17.refs_3_.refs_2_), channel_id=1, source_target_pairs={{0,2},{1,3},{2,0},{3,1},{4,6},{5,7},{6,4},{7,5},{8,10},{9,11},{10,... | collective-permute-start | bytes 2359304 | tf_op jit(solution)/shard_map/ppermute | solution.py:343
  12.5 15.2 %collective-permute-done.refs_1_ = bf16[12,272,128]{2,1,0:T(8,128)(2,1)S(1)} collective-permute-done((bf16[12,272,128]{2,1,0:T(8,128)(2,1)}, bf16[12,272,128]{2,1,0:T(8,128)(2,1)S(1)}, u32[]{:S(2)}, u32[]{:S(2)}) %collective-permute-start) | collective-permute-done | bytes 835616 | tf_op jit(solution)/shard_map/ppermute | solution.py:343
  27.7 0.7 collective-permute-start.5
  28.5 0.9 copy-done.5
  29.4 2.4 %collective-permute-done.1.refs_2_ = bf16[12,272,128]{2,1,0:T(8,128)(2,1)S(1)} collective-permute-done((bf16[12,272,128]{2,1,0:T(8,128)(2,1)}, bf16[12,272,128]{2,1,0:T(8,128)(2,1)S(1)}, u32[]{:S(2)}, u32[]{:S(2)}) %collective-permute-start.1) | collective-permute-done | bytes 835616 | tf_op jit(solution)/shard_map/ppermute | solution.py:343
  31.8 1.3 collective-permute-start.7
  33.1 0.9 copy-done.7
  34.0 0.0 collective-permute-done.3.refs_5_.refs_4_
  34.0 0.5 collective-permute-start.4
  34.5 0.0 collective-permute-done.5.refs_0_
  34.5 1.6 %collective-permute-start.6 = (bf16[12,272,128]{2,1,0:T(8,128)(2,1)S(1)}, bf16[12,272,128]{2,1,0:T(8,128)(2,1)}, u32[]{:S(2)}, u32[]{:S(2)}) collective-permute-start(bf16[12,272,128]{2,1,0:T(8,128)(2,1)S(1)} %collective-permute-done.5.refs_0_), channel_id=1, source_target_pairs={{8,12},{9,13},{10,14},{11,15},{24,28},{25,29},{26,30},{27,31}} | collective-permute-start | bytes 2506760 | tf_op jit(solution)/shard_map/ppermute | solution.py:343
  36.1 17.9 %collective-permute-done.7.refs_1_ = bf16[12,272,128]{2,1,0:T(8,128)(2,1)} collective-permute-done((bf16[12,272,128]{2,1,0:T(8,128)(2,1)S(1)}, bf16[12,272,128]{2,1,0:T(8,128)(2,1)}, u32[]{:S(2)}, u32[]{:S(2)}) %collective-permute-start.7) | collective-permute-done | bytes 835616 | tf_op jit(solution)/shard_map/ppermute | solution.py:343
  54.0 1.3 collective-permute-start.8
  55.3 0.8 copy.10
  56.1 0.2 reshape.32.layout_ref
  56.3 0.1 pad_add_fusion.me_ref
  56.4 1.1 copy-done.2
  57.6 1.1 copy-done.4
  58.7 1.1 copy-done.6
  59.9 1.1 copy-done.8
  61.0 20.6 %visit.3 = (f32[12,128,128]{2,1,0:T(8,128)S(1)}, bf16[12,128,128]{2,1,0:T(8,128)(2,1)S(1)}, bf16[12,128,128]{2,1,0:T(8,128)(2,1)S(1)}, f32[48,2,128,128]{3,2,1,0:T(8,128)S(1)}) custom-call(s32[2]{0:T(128)S(1)} %pad_add_fusion.me_ref, s32[576]{0:T(1024)S(1)} %reshape.32.layout_ref, bf16[12,272,128]{2,1,0:T(8,128)(2,1)S(1)} %copy-done.4, ...), custom_call_target="tpu_custom_call" | custom-call | flops 2264924160 | bytes 16777216 | tf_op jit(solution)/shard_map/visit/pallas_call | solution.py:305
  81.7 2.6 %copy-done.1 = f32[48,2,128,128]{3,2,1,0:T(8,128)} copy-done((f32[48,2,128,128]{3,2,1,0:T(8,128)}, f32[48,2,128,128]{3,2,1,0:T(8,128)S(1)}, u32[]{:S(2)}) %copy-start.1) | copy-done | bytes 6291480
  84.3 11.4 %visit.4 = (bf16[12,128,128]{2,1,0:T(8,128)(2,1)S(1)}, bf16[12,128,128]{2,1,0:T(8,128)(2,1)S(1)}, f32[48,2,128,128]{3,2,1,0:T(8,128)S(1)}) custom-call(s32[2]{0:T(128)S(1)} %pad_add_fusion.me_ref, s32[576]{0:T(1024)S(1)} %reshape.32.layout_ref, bf16[12,272,128]{2,1,0:T(8,128)(2,1)S(1)} %collective-permute-done.5.refs_0_, ...), custom_call_target="tpu_custom_call" | custom-call | flops 1006632960 | bytes 16777216 | tf_op jit(solution)/shard_map/visit/pallas_call | solution.py:305
  95.7 2.6 %copy-done = f32[48,2,128,128]{3,2,1,0:T(8,128)} copy-done((f32[48,2,128,128]{3,2,1,0:T(8,128)}, f32[48,2,128,128]{3,2,1,0:T(8,128)S(1)}, u32[]{:S(2)}) %copy-start) | copy-done | bytes 6291480
  98.3 0.0 collective-permute-done.8.refs_1_
  98.3 11.0 %visit.5 = (bf16[12,128,128]{2,1,0:T(8,128)(2,1)S(1)}, bf16[12,128,128]{2,1,0:T(8,128)(2,1)S(1)}, bf16[2,12,2,128,128]{4,3,2,1,0:T(8,128)(2,1)S(1)}, f32[2,12,2,128,128]{4,3,2,1,0:T(8,128)S(1)}) custom-call(s32[2]{0:T(128)S(1)} %pad_add_fusion.me_ref, s32[576]{0:T(1024)S(1)} %reshape.32.layout_ref, bf16[12,272,128]{2,1,0:T(8,128)(2,1)} %collective-permute-done.6.refs_0_, ...), custom_call_target="tpu_custom_call" | custom-call | flops 1006632960 | bytes 16777216 | tf_op jit(solution)/shard_map/visit/pallas_call | solution.py:305
  109.4 0.1 collective-permute-start.15
  109.5 0.7 collective-permute-start.11
  110.2 1.3 collective-permute-start.13
  111.5 0.1 add_convert_fusion.2
  111.6 1.3 collective-permute-start.12
  112.9 0.0 collective-permute-done.15
  112.9 0.6 add_bitcast_fusion
  113.5 0.1 fusion.3
  113.7 1.0 collective-permute-start.16
  114.7 6.1 %collective-permute-done.13 = bf16[12,128,128]{2,1,0:T(8,128)(2,1)S(1)} collective-permute-done((bf16[12,128,128]{2,1,0:T(8,128)(2,1)S(1)}, bf16[12,128,128]{2,1,0:T(8,128)(2,1)S(1)}, u32[]{:S(2)}, u32[]{:S(2)}) %collective-permute-start.13) | collective-permute-done | bytes 393248 | tf_op jit(solution)/shard_map/ppermute | solution.py:343
  120.7 0.1 add_convert_fusion.1
  120.9 4.4 %collective-permute-start.14 = (bf16[12,128,128]{2,1,0:T(8,128)(2,1)S(1)}, bf16[12,128,128]{2,1,0:T(8,128)(2,1)S(1)}, u32[]{:S(2)}, u32[]{:S(2)}) collective-permute-start(bf16[12,128,128]{2,1,0:T(8,128)(2,1)S(1)} %add_convert_fusion.1), channel_id=1, source_target_pairs={{0,4},{1,5},{2,6},{3,7},{4,8},{5,9},{6,10},{7,11},{8,12},{9,13},{1... | collective-permute-start | bytes 1179656 | tf_op jit(solution)/shard_map/ppermute | solution.py:343
  125.3 1.3 collective-permute-start.10
  126.6 1.3 collective-permute-start.9
  127.9 6.8 %collective-permute-done.14 = bf16[12,128,128]{2,1,0:T(8,128)(2,1)S(1)} collective-permute-done((bf16[12,128,128]{2,1,0:T(8,128)(2,1)S(1)}, bf16[12,128,128]{2,1,0:T(8,128)(2,1)S(1)}, u32[]{:S(2)}, u32[]{:S(2)}) %collective-permute-start.14) | collective-permute-done | bytes 393248 | tf_op jit(solution)/shard_map/ppermute | solution.py:343
  134.7 7.4 %collective-permute-done.10 = bf16[12,128,128]{2,1,0:T(8,128)(2,1)S(1)} collective-permute-done((bf16[12,128,128]{2,1,0:T(8,128)(2,1)S(1)}, bf16[12,128,128]{2,1,0:T(8,128)(2,1)S(1)}, u32[]{:S(2)}, u32[]{:S(2)}) %collective-permute-start.10) | collective-permute-done | bytes 393248 | tf_op jit(solution)/shard_map/ppermute | solution.py:343
  142.1 1.0 add_convert_fusion
  143.1 0.2 fusion.2
  143.4 1.0 fusion.4
  (18 shorter events, 0.0 us)
Async XLA Ops:
  4.7 23.1 %collective-permute-start = (bf16[12,272,128]{2,1,0:T(8,128)(2,1)}, bf16[12,272,128]{2,1,0:T(8,128)(2,1)S(1)}, u32[]{:S(2)}, u32[]{:S(2)}) collective-permute-start(bf16[12,272,128]{2,1,0:T(8,128)(2,1)} %get-tuple-element.16.refs_0_), channel_id=1, source_target_pairs={{0,4},{1,5},{2,6},{3,7},{4,8},{5,9},{6,10},{7,11},{8,12},{9,13},{1... | collective-permute-start | bytes 2506760 | tf_op jit(solution)/shard_map/ppermute | solution.py:343
  9.6 22.2 %collective-permute-start.1 = (bf16[12,272,128]{2,1,0:T(8,128)(2,1)}, bf16[12,272,128]{2,1,0:T(8,128)(2,1)S(1)}, u32[]{:S(2)}, u32[]{:S(2)}) collective-permute-start(bf16[12,272,128]{2,1,0:T(8,128)(2,1)} %get-tuple-element.16.refs_0_), channel_id=1, source_target_pairs={{4,0},{5,1},{6,2},{7,3},{8,4},{9,5},{10,6},{11,7},{12,8},{13,9},{1... | collective-permute-start | bytes 2506760 | tf_op jit(solution)/shard_map/ppermute | solution.py:343
  10.9 23.0 %collective-permute-start.3 = (bf16[12,2,128,128]{3,2,1,0:T(8,128)(2,1)}, bf16[12,2,128,128]{3,2,1,0:T(8,128)(2,1)S(1)}, u32[]{:S(2)}, u32[]{:S(2)}) collective-permute-start(bf16[12,2,128,128]{3,2,1,0:T(8,128)(2,1)} %get-tuple-element.17.refs_3_.refs_2_), channel_id=1, source_target_pairs={{0,2},{1,3},{2,0},{3,1},{4,6},{5,7},{6,4},{7,5},{8,10},{9,11},{10,... | collective-permute-start | bytes 2359304 | tf_op jit(solution)/shard_map/ppermute | solution.py:343
  27.7 6.8 %collective-permute-start.5 = (bf16[12,272,128]{2,1,0:T(8,128)(2,1)S(1)}, bf16[12,272,128]{2,1,0:T(8,128)(2,1)S(1)}, u32[]{:S(2)}, u32[]{:S(2)}) collective-permute-start(bf16[12,272,128]{2,1,0:T(8,128)(2,1)S(1)} %collective-permute-done.refs_1_), channel_id=1, source_target_pairs={{4,8},{5,9},{6,10},{7,11},{8,12},{9,13},{10,14},{11,15},{20,24},{2... | collective-permute-start | bytes 2506760 | tf_op jit(solution)/shard_map/ppermute | solution.py:343
  28.5 0.9 copy-start.5
  31.8 22.2 %collective-permute-start.7 = (bf16[12,272,128]{2,1,0:T(8,128)(2,1)S(1)}, bf16[12,272,128]{2,1,0:T(8,128)(2,1)}, u32[]{:S(2)}, u32[]{:S(2)}) collective-permute-start(bf16[12,272,128]{2,1,0:T(8,128)(2,1)S(1)} %collective-permute-done.1.refs_2_), channel_id=1, source_target_pairs={{4,0},{5,1},{6,2},{7,3},{8,4},{9,5},{10,6},{11,7},{20,16},{21,17},... | collective-permute-start | bytes 2506760 | tf_op jit(solution)/shard_map/ppermute | solution.py:343
  33.1 0.9 copy-start.7
  34.0 22.4 %collective-permute-start.2 = (bf16[12,2,128,128]{3,2,1,0:T(8,128)(2,1)}, bf16[12,2,128,128]{3,2,1,0:T(8,128)(2,1)S(1)}, u32[]{:S(2)}, u32[]{:S(2)}) collective-permute-start(bf16[12,2,128,128]{3,2,1,0:T(8,128)(2,1)} %get-tuple-element.17.refs_3_.refs_2_), channel_id=1, source_target_pairs={{0,1},{1,0},{2,3},{3,2},{4,5},{5,4},{6,7},{7,6},{8,9},{9,8},{10,11... | collective-permute-start | bytes 2359304 | tf_op jit(solution)/shard_map/ppermute | solution.py:343
  34.0 22.4 %collective-permute-start.4 = (bf16[12,2,128,128]{3,2,1,0:T(8,128)(2,1)S(1)}, bf16[12,2,128,128]{3,2,1,0:T(8,128)(2,1)S(1)}, u32[]{:S(2)}, u32[]{:S(2)}) collective-permute-start(bf16[12,2,128,128]{3,2,1,0:T(8,128)(2,1)S(1)} %collective-permute-done.3.refs_5_.refs_4_), channel_id=1, source_target_pairs={{0,1},{1,0},{2,3},{3,2},{4,5},{5,4},{6,7},{7,6},{8,9},{9,8},{10,11... | collective-permute-start | bytes 2359304 | tf_op jit(solution)/shard_map/ppermute | solution.py:343
  34.5 63.8 %collective-permute-start.6 = (bf16[12,272,128]{2,1,0:T(8,128)(2,1)S(1)}, bf16[12,272,128]{2,1,0:T(8,128)(2,1)}, u32[]{:S(2)}, u32[]{:S(2)}) collective-permute-start(bf16[12,272,128]{2,1,0:T(8,128)(2,1)S(1)} %collective-permute-done.5.refs_0_), channel_id=1, source_target_pairs={{8,12},{9,13},{10,14},{11,15},{24,28},{25,29},{26,30},{27,31}} | collective-permute-start | bytes 2506760 | tf_op jit(solution)/shard_map/ppermute | solution.py:343
  54.0 44.3 %collective-permute-start.8 = (bf16[12,272,128]{2,1,0:T(8,128)(2,1)}, bf16[12,272,128]{2,1,0:T(8,128)(2,1)}, u32[]{:S(2)}, u32[]{:S(2)}) collective-permute-start(bf16[12,272,128]{2,1,0:T(8,128)(2,1)} %collective-permute-done.7.refs_1_), channel_id=1, source_target_pairs={{4,0},{5,1},{6,2},{7,3},{20,16},{21,17},{22,18},{23,19}} | collective-permute-start | bytes 2506760 | tf_op jit(solution)/shard_map/ppermute | solution.py:343
  56.4 1.1 copy-start.2
  57.6 1.1 copy-start.4
  58.7 1.1 copy-start.6
  59.9 1.1 copy-start.8
  61.0 23.3 %copy-start.3 = (bf16[12,2,128,128]{3,2,1,0:T(8,128)(2,1)S(1)}, bf16[12,2,128,128]{3,2,1,0:T(8,128)(2,1)}, u32[]{:S(2)}) copy-start(bf16[12,2,128,128]{3,2,1,0:T(8,128)(2,1)} %get-tuple-element.17.refs_3_.refs_2_) | copy-start | bytes 2359300
  81.7 2.6 %copy-start.1 = (f32[48,2,128,128]{3,2,1,0:T(8,128)}, f32[48,2,128,128]{3,2,1,0:T(8,128)S(1)}, u32[]{:S(2)}) copy-start(f32[48,2,128,128]{3,2,1,0:T(8,128)S(1)} %get-tuple-element.19.refs_6_) | copy-start | bytes 18874372
  95.7 2.6 %copy-start = (f32[48,2,128,128]{3,2,1,0:T(8,128)}, f32[48,2,128,128]{3,2,1,0:T(8,128)S(1)}, u32[]{:S(2)}) copy-start(f32[48,2,128,128]{3,2,1,0:T(8,128)S(1)} %get-tuple-element.20.refs_6_) | copy-start | bytes 18874372
  109.4 3.5 %collective-permute-start.15 = (bf16[2,12,2,128,128]{4,3,2,1,0:T(8,128)(2,1)S(1)}, bf16[2,12,2,128,128]{4,3,2,1,0:T(8,128)(2,1)S(1)}, u32[]{:S(2)}, u32[]{:S(2)}) collective-permute-start(bf16[2,12,2,128,128]{4,3,2,1,0:T(8,128)(2,1)S(1)} %get-tuple-element.28), channel_id=1, source_target_pairs={{0,1},{1,0},{2,3},{3,2},{4,5},{5,4},{6,7},{7,6},{8,9},{9,8},{10,11... | collective-permute-start | bytes 4718600 | tf_op jit(solution)/shard_map/ppermute | solution.py:343
  109.5 2.0 %collective-permute-start.11 = (bf16[12,128,128]{2,1,0:T(8,128)(2,1)S(1)}, bf16[12,128,128]{2,1,0:T(8,128)(2,1)S(1)}, u32[]{:S(2)}, u32[]{:S(2)}) collective-permute-start(bf16[12,128,128]{2,1,0:T(8,128)(2,1)S(1)} %get-tuple-element.24), channel_id=1, source_target_pairs={{8,4},{9,5},{10,6},{11,7},{12,8},{13,9},{14,10},{15,11},{24,20},{2... | collective-permute-start | bytes 1179656 | tf_op jit(solution)/shard_map/ppermute | solution.py:343
  110.2 10.6 %collective-permute-start.13 = (bf16[12,128,128]{2,1,0:T(8,128)(2,1)S(1)}, bf16[12,128,128]{2,1,0:T(8,128)(2,1)S(1)}, u32[]{:S(2)}, u32[]{:S(2)}) collective-permute-start(bf16[12,128,128]{2,1,0:T(8,128)(2,1)S(1)} %get-tuple-element.26), channel_id=1, source_target_pairs={{0,4},{1,5},{2,6},{3,7},{4,8},{5,9},{6,10},{7,11},{16,20},{17,21},... | collective-permute-start | bytes 1179656 | tf_op jit(solution)/shard_map/ppermute | solution.py:343
  111.6 16.3 %collective-permute-start.12 = (bf16[12,128,128]{2,1,0:T(8,128)(2,1)S(1)}, bf16[12,128,128]{2,1,0:T(8,128)(2,1)S(1)}, u32[]{:S(2)}, u32[]{:S(2)}) collective-permute-start(bf16[12,128,128]{2,1,0:T(8,128)(2,1)S(1)} %add_convert_fusion.2), channel_id=1, source_target_pairs={{4,0},{5,1},{6,2},{7,3},{8,4},{9,5},{10,6},{11,7},{12,8},{13,9},{1... | collective-permute-start | bytes 1179656 | tf_op jit(solution)/shard_map/ppermute | solution.py:343
  113.7 29.4 %collective-permute-start.16 = (bf16[1,12,2,128,128]{4,3,2,1,0:T(8,128)(2,1)S(1)}, bf16[1,12,2,128,128]{4,3,2,1,0:T(8,128)(2,1)S(1)}, u32[]{:S(2)}, u32[]{:S(2)}) collective-permute-start(bf16[1,12,2,128,128]{4,3,2,1,0:T(8,128)(2,1)S(1)} %fusion.3), channel_id=1, source_target_pairs={{0,2},{1,3},{2,0},{3,1},{4,6},{5,7},{6,4},{7,5},{8,10},{9,11},{10,... | collective-permute-start | bytes 2359304 | tf_op jit(solution)/shard_map/ppermute | solution.py:343
  120.9 13.9 %collective-permute-start.14 = (bf16[12,128,128]{2,1,0:T(8,128)(2,1)S(1)}, bf16[12,128,128]{2,1,0:T(8,128)(2,1)S(1)}, u32[]{:S(2)}, u32[]{:S(2)}) collective-permute-start(bf16[12,128,128]{2,1,0:T(8,128)(2,1)S(1)} %add_convert_fusion.1), channel_id=1, source_target_pairs={{0,4},{1,5},{2,6},{3,7},{4,8},{5,9},{6,10},{7,11},{8,12},{9,13},{1... | collective-permute-start | bytes 1179656 | tf_op jit(solution)/shard_map/ppermute | solution.py:343
  125.3 16.8 %collective-permute-start.10 = (bf16[12,128,128]{2,1,0:T(8,128)(2,1)S(1)}, bf16[12,128,128]{2,1,0:T(8,128)(2,1)S(1)}, u32[]{:S(2)}, u32[]{:S(2)}) collective-permute-start(bf16[12,128,128]{2,1,0:T(8,128)(2,1)S(1)} %get-tuple-element.22), channel_id=1, source_target_pairs={{0,12},{1,13},{2,14},{3,15},{16,28},{17,29},{18,30},{19,31}} | collective-permute-start | bytes 1179656 | tf_op jit(solution)/shard_map/ppermute | solution.py:343
  126.6 15.5 %collective-permute-start.9 = (bf16[12,128,128]{2,1,0:T(8,128)(2,1)S(1)}, bf16[12,128,128]{2,1,0:T(8,128)(2,1)S(1)}, u32[]{:S(2)}, u32[]{:S(2)}) collective-permute-start(bf16[12,128,128]{2,1,0:T(8,128)(2,1)S(1)} %get-tuple-element.21), channel_id=1, source_target_pairs={{12,0},{13,1},{14,2},{15,3},{28,16},{29,17},{30,18},{31,19}} | collective-permute-start | bytes 1179656 | tf_op jit(solution)/shard_map/ppermute | solution.py:343

commit v2 on v0

v2 whole, which is shorter than its diff:
```python
import functools

import jax
import jax.numpy as jnp
from jax import lax
from jax.experimental import pallas as pl
from jax.experimental.pallas import tpu as pltpu
from jax.sharding import PartitionSpec as P

BLK = 128
GLOB = 2
TILE = 16
PAIRS = 3
FAR = 1e30
COST = 0
LIMIT = 24 * 2**20


def pieces(row):
    high = row.astype(jnp.bfloat16)
    rest = row - high.astype(jnp.float32)
    middle = rest.astype(jnp.bfloat16)
    low = (rest - middle.astype(jnp.float32)).astype(jnp.bfloat16)
    return [high.astype(jnp.float32), middle.astype(jnp.float32), low.astype(jnp.float32)]


def stat_rows(count):
    return -(-count // TILE) * TILE


def pack_kernel(query, grad, output, key, value, lse, unit, keyval, delta_s):
    count, width = lse.shape
    rows = stat_rows(count)
    group = 4 if count % 4 == 0 else 1
    ones = jnp.ones((TILE, width), jnp.bfloat16)

    def total(part):
        return lax.dot_general(
            ones, part, (((1,), (1,)), ((), ())), preferred_element_type=jnp.float32
        )

    def step(g, carry):
        highs, lows = ([], [])
        for k in range(group):
            at = pl.ds(pl.multiple_of((g * group + k) * BLK, BLK), BLK)
            after = pl.ds(pl.multiple_of((count + g * group + k) * BLK, BLK), BLK)
            grads = grad[at, :]
            unit[at, :] = query[at, :]
            unit[after, :] = grads
            keyval[at, :] = key[at, :]
            keyval[after, :] = value[at, :]
            product = grads.astype(jnp.float32) * output[at, :].astype(jnp.float32)
            highs.append(product.astype(jnp.bfloat16))
            lows.append((product - highs[-1].astype(jnp.float32)).astype(jnp.bfloat16))
        sums = [total(high) + total(low) for high, low in zip(highs, lows)]
        for k in range(group):
            delta_s[pl.ds(g * group + k, 1), :] = sums[k][0:1]
        return carry

    delta_s[...] = jnp.zeros(delta_s.shape, jnp.float32)
    lax.fori_loop(0, count // group, step, 0)
    lines = lse[...]
    if rows > count:
        lines = jnp.concatenate([lines, jnp.zeros((rows - count, width), jnp.float32)], 0)
    stats = pieces(lines) + pieces(delta_s[...])
    unit[2 * count * BLK :, :] = jnp.concatenate(stats, 0).astype(jnp.bfloat16)


def pack(query, grad, output, key, value, lse):
    count, width = lse.shape
    rows = stat_rows(count)
    return pl.pallas_call(
        pack_kernel,
        out_shape=(
            jax.ShapeDtypeStruct((2 * count * BLK + 6 * rows, width), jnp.bfloat16),
            jax.ShapeDtypeStruct((2 * count * BLK, width), jnp.bfloat16),
        ),
        scratch_shapes=[pltpu.VMEM((rows, width), jnp.float32)],
        name="pack",
    )(query, grad, output, key, value, lse)


def pair_grads(pairs, scaling):
    def outer(one, two):
        return lax.dot_general(
            one, two, (((1,), (1,)), ((), ())), preferred_element_type=jnp.float32
        )

    def inner(one, two):
        return jnp.dot(one, two, preferred_element_type=jnp.float32)

    def flipped(one, two):
        return lax.dot_general(
            one, two, (((0,), (0,)), ((), ())), preferred_element_type=jnp.float32
        )

    scores = [outer(keys, queries) for keys, _, queries, _, _, _, _ in pairs]
    dweights = [outer(values, grads) for _, values, _, grads, _, _, _ in pairs]
    probs = []
    for score, (_, _, _, _, lse, _, mask) in zip(scores, pairs):
        prob = jnp.exp(score * scaling - lse)
        probs.append(prob if mask is None else jnp.where(mask, prob, 0.0))
    prob_lows = [prob.astype(jnp.bfloat16) for prob in probs]
    score_lows = [
        (prob * (dweight - pair[5])).astype(jnp.bfloat16)
        for prob, dweight, pair in zip(probs, dweights, pairs)
    ]
    value_parts = [inner(low, pair[3]) for low, pair in zip(prob_lows, pairs)]
    key_parts = [inner(low, pair[2]) for low, pair in zip(score_lows, pairs)]
    query_parts = [flipped(low, pair[0]) for low, pair in zip(score_lows, pairs)]
    return list(zip(query_parts, key_parts, value_parts))


class Visitor:
    def __init__(self, count, unit, lse, delta, dq, keys, values, acc, layout, lists):
        self.count = count
        self.unit, self.lse, self.delta = (unit, lse, delta)
        self.dq, self.keys, self.values, self.acc = (dq, keys, values, acc)
        self.layout, self.lists = (layout, lists)
        self.width = unit.shape[1]
        self.scaling = self.width ** (-0.5)
        self.held = keys.shape[0] // BLK

    def begin(self):
        count = self.count
        rows = stat_rows(count)
        stats = self.unit[2 * count * BLK :, :].astype(jnp.float32)
        lines = [stats[k * rows : (k + 1) * rows] for k in range(6)]
        self.lse[...] = lines[0] + lines[1] + lines[2]
        self.delta[...] = lines[3] + lines[4] + lines[5]

        def step(q, carry):
            self.dq[q] = jnp.zeros(self.dq.shape[1:], jnp.float32)
            return carry

        lax.fori_loop(0, count, step, 0)

    def rows(self, array, block, blocks=1):
        return array[pl.ds(pl.multiple_of(block * BLK, BLK), blocks * BLK), :]

    def pair(self, q, j, keys=1, shift=0.0, mask=None):
        return (
            self.rows(self.keys, j, keys),
            self.rows(self.values, j, keys),
            self.rows(self.unit, q),
            self.rows(self.unit, self.count + q),
            self.lse[pl.ds(q, 1), :] + shift,
            self.delta[pl.ds(q, 1), :],
            mask,
        )

    def window(self, base):
        count, width = (self.count, self.width)
        chunk = 2 if count % 2 == 0 else 1

        def step(c, carry):
            places, pairs = ([], [])
            for k in range(chunk):
                q = c * chunk + k
                start = jnp.clip(base + q - 1, 0, self.held - 3)
                block = lax.broadcasted_iota(jnp.int32, (3 * BLK, BLK), 0) // BLK
                block = block + start - base - q
                places.append((q, start))
                pairs.append(self.pair(q, start, 3, 0.0, (block >= -1) & (block <= 1)))
            parts = pair_grads(pairs, self.scaling)
            for (q, start), (query_part, key_part, value_part) in zip(places, parts):
                self.dq[q] += query_part
                self.acc[pl.ds(start, 3), 0] += key_part.reshape(3, BLK, width)
                self.acc[pl.ds(start, 3), 1] += value_part.reshape(3, BLK, width)
            return carry

        lax.fori_loop(0, count // chunk, step, 0)

    def anchors(self):
        count, width = (self.count, self.width)
        chunk = 2 if count % 2 == 0 else 1
        turns = 2 if count % (2 * chunk) == 0 else 1

        def step(c, carry):
            places, pairs = ([], [])
            for k in range(turns):
                at = (c * turns + k) * chunk
                places.append(pl.ds(at, chunk))
                pairs.append(
                    (
                        self.keys[0 : GLOB * BLK, :],
                        self.values[0 : GLOB * BLK, :],
                        self.rows(self.unit, at, chunk),
                        self.rows(self.unit, count + at, chunk),
                        jnp.concatenate(
                            [self.lse[pl.ds(at + i, 1), :] for i in range(chunk)], 1
                        ),
                        jnp.concatenate(
                            [self.delta[pl.ds(at + i, 1), :] for i in range(chunk)], 1
                        ),
                        None,
                    )
                )
            parts = pair_grads(pairs, self.scaling)
            for blocks, (query_part, _, _) in zip(places, parts):
                self.dq[blocks] += query_part.reshape(chunk, BLK, width)
            key_part = sum(part[1] for part in parts)
            value_part = sum(part[2] for part in parts)
            self.acc[0:GLOB, 0] += key_part.reshape(GLOB, BLK, width)
            self.acc[0:GLOB, 1] += value_part.reshape(GLOB, BLK, width)
            return carry

        lax.fori_loop(0, count // (chunk * turns), step, 0)

    def scattered(self, guest, low, fanout, near):
        who, whom, far = self.lists
        count = self.count

        def note(at, q, target):
            local = target - low
            hit = (local >= 0) & (local < self.held)
            who[at] = q
            whom[at] = local
            far[at] = 0.0
            return at + hit.astype(jnp.int32)

        def gather(q, at):
            block = guest * count + q
            for r in range(fanout):
                at = note(at, q, self.layout[block * fanout + r])
            return at

        found = lax.fori_loop(0, count, gather, 0)
        if near:
            found = note(found, 0, guest * count - 1)
            found = note(found, count - 1, (guest + 1) * count)
        for k in range(PAIRS - 1):
            who[found + k] = 0
            whom[found + k] = 0
            far[found + k] = FAR

        def step(g, carry):
            places, pairs = ([], [])
            for k in range(PAIRS):
                at = g * PAIRS + k
                places.append((who[at], whom[at]))
                pairs.append(self.pair(who[at], whom[at], 1, far[at]))
            parts = pair_grads(pairs, self.scaling)
            for (q, j), (query_part, key_part, value_part) in zip(places, parts):
                self.dq[q] += query_part
                self.acc[j, 0] += key_part
                self.acc[j, 1] += value_part
            return carry

        lax.fori_loop(0, (found + PAIRS - 1) // PAIRS, step, 0)

    def finish(self, out):
        def step(q, carry):
            out[q] = (self.dq[q] * self.scaling).astype(out.dtype)
            return carry

        lax.fori_loop(0, self.count, step, 0)


def visit_kernel(plan, me_ref, layout, *refs):
    offsets, count, span, fanout, last = plan
    refs = list(refs)
    first = offsets == (0,)
    guests = [refs.pop(0) for _ in offsets]
    me = me_ref[0]
    shards = me_ref[1]
    seat = lax.rem(me, span)
    row = lax.div(me, span)
    low = row * span * count
    if first:
        parts = [refs.pop(0) for _ in range(span)]
        keys, values = (refs.pop(0), refs.pop(0))
    else:
        keys, values = (refs.pop(0), refs.pop(0))
        refs.pop(0)
    acc = refs.pop(0)
    outs = [refs.pop(0) for _ in offsets]
    if last:
        sent, kept = (refs.pop(0), refs.pop(0))
    sums = outs if first else [refs.pop(0) for _ in offsets]
    lse, delta = (refs.pop(0), refs.pop(0))
    lists = refs
    if first:

        def lay(b, carry):
            for m in range(span):
                there = jnp.bitwise_xor(seat, m) * count + b
                acc[there] = jnp.zeros(acc.shape[1:], jnp.float32)
                there = pl.ds(pl.multiple_of(there * BLK, BLK), BLK)
                here = pl.ds(pl.multiple_of(b * BLK, BLK), BLK)
                keys[there, :] = parts[m][here, :]
                here = pl.ds(pl.multiple_of((count + b) * BLK, BLK), BLK)
                values[there, :] = parts[m][here, :]
            return carry

        lax.fori_loop(0, count, lay, 0)

    for v, offset in enumerate(offsets):
        if offset is None:
            guest = jnp.where(row == 0, me + shards - span, me + span - shards)
            present = (row == 0) | (me + span >= shards)
        else:
            guest = me + offset * span
            present = (guest >= 0) & (guest < shards)
        visitor = Visitor(count, guests[v], lse, delta, sums[v], keys, values, acc, layout, lists)
        visitor.begin()
        if offset == 0:
            visitor.window(seat * count)

        @pl.when(present)
        def _(visitor=visitor, near=offset in (-1, 1), guest=guest):
            @pl.when(row == 0)
            def _():
                visitor.anchors()

            visitor.scattered(guest, low, fanout, near)

        visitor.finish(outs[v])

    if last:
        scaling = keys.shape[1] ** (-0.5)

        def finish(b, carry):
            for k in range(span // 2):
                mine = jnp.bitwise_xor(seat, 2 * k) * count + b
                theirs = jnp.bitwise_xor(seat, 2 * k + 1) * count + b
                sent[0, k, b] = (acc[theirs, 0] * scaling).astype(jnp.bfloat16)
                sent[1, k, b] = acc[theirs, 1].astype(jnp.bfloat16)
                kept[0, k, b] = acc[mine, 0] * scaling
                kept[1, k, b] = acc[mine, 1]
            return carry

        lax.fori_loop(0, count, finish, 0)


SMEM = pl.BlockSpec(memory_space=pltpu.SMEM)
VMEM = pl.BlockSpec(memory_space=pltpu.VMEM)


def in_place(array):
    return pltpu.with_memory_space_constraint(array, pltpu.VMEM)


def visit(me, layout, units, offsets, keyvals, acc, last, count, span, fanout):
    first = acc is None
    width = units[0].shape[1]
    held = span * count
    plan = (offsets, count, span, fanout, last)
    operands = units + keyvals
    keys = jax.ShapeDtypeStruct((held * BLK, width), jnp.bfloat16)
    outs = [jax.ShapeDtypeStruct((held, 2, BLK, width), jnp.float32)]
    aliases = {}
    if first:
        outs = [keys, keys] + outs
    else:
        aliases[len(operands) + 2] = 0
        operands = operands + [in_place(acc)]
    kind = jnp.float32 if first else jnp.bfloat16
    outs += [jax.ShapeDtypeStruct((count, BLK, width), kind)] * len(units)
    if last:
        outs.append(jax.ShapeDtypeStruct((2, span // 2, count, BLK, width), jnp.bfloat16))
        outs.append(jax.ShapeDtypeStruct((2, span // 2, count, BLK, width), jnp.float32))
    entries = count * fanout + 2 + PAIRS
    stats = pltpu.VMEM((stat_rows(count), width), jnp.float32)
    return list(
        pl.pallas_call(
            functools.partial(visit_kernel, plan),
            out_shape=outs,
            in_specs=[SMEM, SMEM] + [VMEM] * len(operands),
            out_specs=[VMEM] * len(outs),
            input_output_aliases=aliases,
            scratch_shapes=[pltpu.VMEM((count, BLK, width), jnp.float32)]
            * (0 if first else len(units))
            + [
                stats,
                stats,
                pltpu.SMEM((entries,), jnp.int32),
                pltpu.SMEM((entries,), jnp.int32),
                pltpu.SMEM((entries,), jnp.float32),
            ],
            compiler_params=pltpu.CompilerParams(vmem_limit_bytes=LIMIT),
            cost_estimate=pl.CostEstimate(
                flops=COST * len(offsets) * count * 10 * BLK * BLK * width,
                bytes_accessed=2**20,
                transcendentals=len(offsets) * count * BLK * BLK,
            ),
            name="visit",
        )(me, layout, *operands)
    )


def body(query_rows, key_rows, value_rows, output_rows, output_grad, logsumexp, layout):
    shards = lax.axis_size("qb")
    myself = lax.axis_index("qb")
    width = query_rows.shape[1]
    count = query_rows.shape[0] // BLK
    fanout = layout.shape[1]
    span = 4
    while shards // span > 16:
        span = span * 2
    planes = shards // span

    def send(array, pairs):
        return lax.ppermute(array, "qb", pairs)

    def swap(array, bit):
        return send(array, [(i, i ^ bit) for i in range(shards)])

    def shift(array, planes_away, low, high):
        return send(
            array,
            [
                (p * span + e, (p + planes_away) * span + e)
                for p in range(low, high)
                for e in range(span)
            ],
        )

    me = jnp.stack([myself, jnp.int32(shards)]).astype(jnp.int32)
    entries = layout.reshape(-1)
    unit, keyval = pack(
        query_rows, output_grad, output_rows, key_rows, value_rows, logsumexp.reshape(count, BLK)
    )

    def merge(one, two):
        return (one.astype(jnp.float32) + two.astype(jnp.float32)).astype(jnp.bfloat16)

    def wide(array):
        return array.astype(jnp.float32)

    def tie(*arrays):
        return lax.optimization_barrier(arrays)

    last = planes - 1
    ends = [(last * span + e, e) for e in range(span)]
    ends = ends + [(two, one) for one, two in ends]
    up, down = (shift(unit, 1, 0, last), shift(unit, -1, 1, planes))
    keyvals = {0: keyval}
    singles = [m for m in range(1, span) if m & (m - 1) == 0]
    for m in singles:
        keyvals[m] = swap(keyval, m)
    up, down, far, *arrived = tie(up, down, unit, *[keyvals[m] for m in singles])
    keyvals.update(zip(singles, arrived))
    far = send(far, ends)
    for m in range(1, span):
        if m & (m - 1):
            keyvals[m] = swap(keyvals[m & (m - 1)], m & -m)
    keyvals = [keyvals[m] for m in range(span)]

    def meet(units, offsets, keyvals, acc, final=False):
        return visit(me, entries, units, offsets, keyvals, acc, final, count, span, fanout)

    keys, values, acc, query_acc = meet([unit], (0,), keyvals, None)
    up_parts, down_parts = ([], [])
    for s in range(1, last):
        if s + 1 < last:
            next_up, next_down = (shift(up, 1, s, last), shift(down, -1, 1, planes - s))
        final = s + 1 == last
        units, offsets = ([up, down], (-s, s))
        if final:
            units, offsets = (units + [far], offsets + (None,))
        acc, up_part, down_part, *rest = meet(units, offsets, [keys, values], acc, final)
        up_parts.append(up_part)
        down_parts.append(down_part)
        if not final:
            up, down = (next_up, next_down)
    far_part, sent, kept = rest

    up_back, down_back = (up_parts[-1], down_parts[-1])
    for t in range(last - 1, 0, -1):
        up_back = shift(up_back, -1, t, planes)
        down_back = shift(down_back, 1, 0, planes - t)
        if t > 1:
            up_back = merge(up_parts[t - 2], up_back)
            down_back = merge(down_parts[t - 2], down_back)
    query_acc = query_acc + wide(send(far_part, ends)) + wide(up_back) + wide(down_back)

    bit = 1
    while True:
        kept = kept + swap(sent, bit).astype(jnp.float32)
        bit = bit * 2
        if bit == span:
            break
        halves = kept.reshape((2, kept.shape[1] // 2, 2) + kept.shape[2:])
        kept = halves[:, :, 0]
        sent = halves[:, :, 1].astype(jnp.bfloat16)
    query_grad = query_acc.reshape(count * BLK, width).astype(jnp.bfloat16)
    key_grad = kept[0, 0].reshape(count * BLK, width).astype(jnp.bfloat16)
    value_grad = kept[1, 0].reshape(count * BLK, width).astype(jnp.bfloat16)
    return (query_grad, key_grad, value_grad)


def solution(mesh):
    in_specs = (
        P(("grp", "qb"), None),
        P(("grp", "qb"), None),
        P(("grp", "qb"), None),
        P(("grp", "qb"), None),
        P(("grp", "qb"), None),
        P(("grp", "qb")),
        P("grp", None),
    )
    out_specs = (P(("grp", "qb"), None), P(("grp", "qb"), None), P(("grp", "qb"), None))
    return jax.shard_map(body, mesh=mesh, in_specs=in_specs, out_specs=out_specs, check_vma=False)
```

time: 389 us -> 117 us (0.30)
  waiting for transfers between devices: 219 us -> 54.9 us
  local copies, waits for them, and re-layouts: 54.5 us -> 6.4 us
  matrix products: 33.2 us -> 0 us
  Pallas kernels: 0 us -> 27.4 us
  other arithmetic: 25.5 us -> 1.94 us
  starting transfers between devices: 40.5 us -> 25.3 us
  between operations: 14.8 us -> 0.86 us
    psum x2 -> x0, waiting for transfers between devices: 219 us -> none  [the longest x1 115 us: broadcast(): return lax.psum(block, axis)]
    ppermute x4 -> x15, waiting for transfers between devices: 0.01 us -> 54.9 us  [send(): return lax.ppermute(array, 'qb', pairs)]
    dot_general x37 -> x0, matrix products: 33.2 us -> none  [the longest x2 14.3 us: owner_step(): jnp.dot(picker.T, joined, precision=lax.Precision.HIGHEST)]
    pallas_call x0 -> x4, Pallas kernels: none -> 27.4 us  [the longest x3 24.2 us: visit(): pl.pallas_call(functools.partial(visit_kernel, plan), out_shape=outs, in_...]
    all_to_all x3 -> x0, starting transfers between devices: 20.4 us -> none  [the longest x1 7.36 us: body(): lax.all_to_all(stats_out.reshape(shards, capacity, 2, BLK), 'qb', split_a...]
    while x60 -> x0, local copies, waits for them, and re-layouts: 15.2 us -> none
    scatter x2 -> x0, local copies, waits for them, and re-layouts: 10.6 us -> none  [the longest x1 8.55 us: body(): query_out = jnp.zeros((buffer_rows, 2, BLK, width), jnp.bfloat16).at[slot...]
    gather x5 -> x0, local copies, waits for them, and re-layouts: 10.2 us -> none  [the longest x2 4.61 us: owner_step(): kv_far = jnp.take(kv_local, index_item, axis=0)]
  transfers between devices with their start and end apart: 9 -> 15, of which waited for: 2 -> 6; matrix products, arithmetic and copies ran while one was open for 23% -> 2% of each run, Pallas kernels for 0% -> 12%
where the time goes in v2:
time: 117 us
  waiting for transfers between devices  54.9 us (47%)
  Pallas kernels  27.4 us (23%)
  starting transfers between devices  25.3 us (22%)
  local copies, waits for them, and re-layouts  6.4 us (5%)
  other arithmetic  1.94 us (2%)
    ppermute x15, waiting for transfers between devices, send(): return lax.ppermute(array, 'qb', pairs)  54.9 us
    ppermute x15, starting transfers between devices, send(): return lax.ppermute(array, 'qb', pairs)  25.3 us
    pallas_call x3, Pallas kernels, visit(): pl.pallas_call(functools.partial(visit_kernel, plan), out_shape=outs, in_...  24.2 us
    unnamed x9, local copies, waits for them, and re-layouts  5.11 us
    pallas_call x1, Pallas kernels, pack(): pl.pallas_call(pack_kernel, out_shape=(jax.ShapeDtypeStruct((2 * count *...  3.26 us
  transfers between devices with their start and end apart: 15, of which 6 were waited for; matrix products, arithmetic and copies ran while one was open for 2% of the time, Pallas kernels for 12%

profile of v2, /device:TPU:0, one launch (start us, length us, event | category | flops | bytes accessed | tf_op | source)
XLA Modules:
  0.0 116.9 jit_solution(12430159441468636857)
XLA Ops:
  0.6 3.3 %pack.1 = (bf16[3168,128]{1,0:T(8,128)(2,1)}, bf16[3072,128]{1,0:T(8,128)(2,1)}) custom-call(bf16[1536,128]{1,0:T(8,128)(2,1)} %query.1, bf16[1536,128]{1,0:T(8,128)(2,1)} %grad.1, bf16[1536,128]{1,0:T(8,128)(2,1)} %output.1, bf16[1536,128]{1,0:T(8,128)(2,1)} %key.1, bf16[1536,128]{1,0:T(8,128)(2,1)} %value.1, f32[12,128]{1,0:T(8,128)} %bitcast.20), custom_call_target="tpu_custom_call" | custom-call | tf_op jit(solution)/shard_map/pack/pallas_call | solution.py:72
  3.9 1.3 %collective-permute-start.1 = (bf16[3168,128]{1,0:T(8,128)(2,1)}, bf16[3168,128]{1,0:T(8,128)(2,1)S(1)}, u32[]{:S(2)}, u32[]{:S(2)}) collective-permute-start(bf16[3168,128]{1,0:T(8,128)(2,1)} %get-tuple-element.29.refs_0_), channel_id=1, source_target_pairs={{4,0},{5,1},{6,2},{7,3},{8,4},{9,5},{10,6},{11,7},{12,8},{13,9},{1... | collective-permute-start | bytes 2433032 | tf_op jit(solution)/shard_map/ppermute | solution.py:404
  5.2 5.6 %collective-permute-start = (bf16[3168,128]{1,0:T(8,128)(2,1)}, bf16[3168,128]{1,0:T(8,128)(2,1)S(1)}, u32[]{:S(2)}, u32[]{:S(2)}) collective-permute-start(bf16[3168,128]{1,0:T(8,128)(2,1)} %get-tuple-element.29.refs_0_), channel_id=1, source_target_pairs={{0,4},{1,5},{2,6},{3,7},{4,8},{5,9},{6,10},{7,11},{8,12},{9,13},{1... | collective-permute-start | bytes 2433032 | tf_op jit(solution)/shard_map/ppermute | solution.py:404
  10.8 2.0 %collective-permute-start.3 = (bf16[3072,128]{1,0:T(8,128)(2,1)}, bf16[3072,128]{1,0:T(8,128)(2,1)}, u32[]{:S(2)}, u32[]{:S(2)}) collective-permute-start(bf16[3072,128]{1,0:T(8,128)(2,1)} %get-tuple-element.23.refs_1_), channel_id=1, source_target_pairs={{0,2},{1,3},{2,0},{3,1},{4,6},{5,7},{6,4},{7,5},{8,10},{9,11},{10,... | collective-permute-start | bytes 2359304 | tf_op jit(solution)/shard_map/ppermute | solution.py:404
  12.8 0.0 collective-permute-start.2
  12.8 17.4 %collective-permute-done.3.refs_3_ = bf16[3072,128]{1,0:T(8,128)(2,1)} collective-permute-done((bf16[3072,128]{1,0:T(8,128)(2,1)}, bf16[3072,128]{1,0:T(8,128)(2,1)}, u32[]{:S(2)}, u32[]{:S(2)}) %collective-permute-start.3) | collective-permute-done | bytes 786464 | tf_op jit(solution)/shard_map/ppermute | solution.py:404
  30.2 0.0 collective-permute-done.2.refs_2_
  30.2 0.9 copy-done.2
  31.1 0.0 collective-permute-done.1.refs_1_
  31.1 0.0 collective-permute-done.refs_0_
  31.1 3.8 %collective-permute-start.7 = (bf16[3168,128]{1,0:T(8,128)(2,1)}, bf16[3168,128]{1,0:T(8,128)(2,1)S(1)}, u32[]{:S(2)}, u32[]{:S(2)}) collective-permute-start(bf16[3168,128]{1,0:T(8,128)(2,1)} %get-tuple-element.29.refs_0_), channel_id=1, source_target_pairs={{12,0},{13,1},{14,2},{15,3},{0,12},{1,13},{2,14},{3,15},{28,16},{2... | collective-permute-start | bytes 2433032 | tf_op jit(solution)/shard_map/ppermute | solution.py:404
  34.9 0.7 collective-permute-start.5
  35.6 1.3 %collective-permute-start.6 = (bf16[3168,128]{1,0:T(8,128)(2,1)S(1)}, bf16[3168,128]{1,0:T(8,128)(2,1)}, u32[]{:S(2)}, u32[]{:S(2)}) collective-permute-start(bf16[3168,128]{1,0:T(8,128)(2,1)S(1)} %collective-permute-done.1.refs_1_), channel_id=1, source_target_pairs={{4,0},{5,1},{6,2},{7,3},{8,4},{9,5},{10,6},{11,7},{20,16},{21,17},... | collective-permute-start | bytes 2433032 | tf_op jit(solution)/shard_map/ppermute | solution.py:404
  36.9 0.1 collective-permute-start.4
  37.0 0.8 copy.13
  37.8 0.2 reshape.32.layout
  38.0 0.1 pad_add_fusion.me_ref
  38.1 1.5 %collective-permute-done.4.refs_4_ = bf16[3072,128]{1,0:T(8,128)(2,1)} collective-permute-done((bf16[3072,128]{1,0:T(8,128)(2,1)}, bf16[3072,128]{1,0:T(8,128)(2,1)}, u32[]{:S(2)}, u32[]{:S(2)}) %collective-permute-start.4) | collective-permute-done | bytes 786464 | tf_op jit(solution)/shard_map/ppermute | solution.py:404
  39.6 1.1 copy-done
  40.7 1.1 copy-done.1
  41.9 1.1 copy-done.3
  43.0 9.3 %visit.3 = (bf16[6144,128]{1,0:T(8,128)(2,1)S(1)}, bf16[6144,128]{1,0:T(8,128)(2,1)S(1)}, f32[48,2,128,128]{3,2,1,0:T(8,128)S(1)}, f32[12,128,128]{2,1,0:T(8,128)S(1)}) custom-call(s32[2]{0:T(128)S(1)} %pad_add_fusion.me_ref, s32[576]{0:T(1024)S(1)} %reshape.32.layout, bf16[3168,128]{1,0:T(8,128)(2,1)S(1)} %copy-done, bf16[3072,128]{1,0:T(8,128)(2,1)S(1)} %copy-done.1, ...), custom_call_target="tpu_custom_call" | custom-call | bytes 1048576 | tf_op jit(solution)/shard_map/visit/pallas_call | solution.py:366
  52.4 4.5 %visit.4 = (f32[48,2,128,128]{3,2,1,0:T(8,128)S(1)}, bf16[12,128,128]{2,1,0:T(8,128)(2,1)S(1)}, bf16[12,128,128]{2,1,0:T(8,128)(2,1)S(1)}) custom-call(s32[2]{0:T(128)S(1)} %pad_add_fusion.me_ref, s32[576]{0:T(1024)S(1)} %reshape.32.layout, bf16[3168,128]{1,0:T(8,128)(2,1)S(1)} %collective-permute-done.refs_0_, ...), custom_call_target="tpu_custom_call", output_to_operand_aliasing={{0}: (6, {})} | custom-call | bytes 1048576 | tf_op jit(solution)/shard_map/visit/pallas_call | solution.py:366
  56.9 0.0 collective-permute-done.7.refs_2_
  56.9 0.0 collective-permute-done.5.refs_0_
  56.9 14.2 %collective-permute-done.6.refs_1_ = bf16[3168,128]{1,0:T(8,128)(2,1)} collective-permute-done((bf16[3168,128]{1,0:T(8,128)(2,1)S(1)}, bf16[3168,128]{1,0:T(8,128)(2,1)}, u32[]{:S(2)}, u32[]{:S(2)}) %collective-permute-start.6) | collective-permute-done | bytes 811040 | tf_op jit(solution)/shard_map/ppermute | solution.py:404
  71.1 10.3 %visit.5 = (f32[48,2,128,128]{3,2,1,0:T(8,128)S(1)}, bf16[12,128,128]{2,1,0:T(8,128)(2,1)S(1)}, bf16[12,128,128]{2,1,0:T(8,128)(2,1)S(1)}, bf16[12,128,128]{2,1,...) custom-call(s32[2]{0:T(128)S(1)} %pad_add_fusion.me_ref, ...), custom_call_target="tpu_custom_call", output_to_operand_aliasing={{0}: (7, {})} | custom-call | bytes 1048576 | tf_op jit(solution)/shard_map/visit/pallas_call | solution.py:366
  81.4 0.1 collective-permute-start.13
  81.4 0.7 collective-permute-start.9
  82.1 1.9 %collective-permute-start.8 = (bf16[12,128,128]{2,1,0:T(8,128)(2,1)S(1)}, bf16[12,128,128]{2,1,0:T(8,128)(2,1)S(1)}, u32[]{:S(2)}, u32[]{:S(2)}) collective-permute-start(bf16[12,128,128]{2,1,0:T(8,128)(2,1)S(1)} %get-tuple-element.34), channel_id=1, source_target_pairs={{12,0},{13,1},{14,2},{15,3},{0,12},{1,13},{2,14},{3,15},{28,16},{2... | collective-permute-start | bytes 1179656 | tf_op jit(solution)/shard_map/ppermute | solution.py:404
  84.1 1.3 %collective-permute-start.11 = (bf16[12,128,128]{2,1,0:T(8,128)(2,1)S(1)}, bf16[12,128,128]{2,1,0:T(8,128)(2,1)S(1)}, u32[]{:S(2)}, u32[]{:S(2)}) collective-permute-start(bf16[12,128,128]{2,1,0:T(8,128)(2,1)S(1)} %get-tuple-element.38), channel_id=1, source_target_pairs={{0,4},{1,5},{2,6},{3,7},{4,8},{5,9},{6,10},{7,11},{16,20},{17,21},... | collective-permute-start | bytes 1179656 | tf_op jit(solution)/shard_map/ppermute | solution.py:404
  85.4 0.0 collective-permute-done.9
  85.4 0.1 add_convert_fusion.2
  85.5 1.3 %collective-permute-start.10 = (bf16[12,128,128]{2,1,0:T(8,128)(2,1)S(1)}, bf16[12,128,128]{2,1,0:T(8,128)(2,1)S(1)}, u32[]{:S(2)}, u32[]{:S(2)}) collective-permute-start(bf16[12,128,128]{2,1,0:T(8,128)(2,1)S(1)} %add_convert_fusion.2), channel_id=1, source_target_pairs={{4,0},{5,1},{6,2},{7,3},{8,4},{9,5},{10,6},{11,7},{12,8},{13,9},{1... | collective-permute-start | bytes 1179656 | tf_op jit(solution)/shard_map/ppermute | solution.py:404
  86.8 0.0 collective-permute-done.13
  86.8 0.5 add_bitcast_fusion
  87.3 0.1 fusion.2
  87.4 0.9 collective-permute-start.14
  88.4 13.5 %collective-permute-done.11 = bf16[12,128,128]{2,1,0:T(8,128)(2,1)S(1)} collective-permute-done((bf16[12,128,128]{2,1,0:T(8,128)(2,1)S(1)}, bf16[12,128,128]{2,1,0:T(8,128)(2,1)S(1)}, u32[]{:S(2)}, u32[]{:S(2)}) %collective-permute-start.11) | collective-permute-done | bytes 393248 | tf_op jit(solution)/shard_map/ppermute | solution.py:404
  101.8 0.1 add_convert_fusion.1
  101.9 4.4 %collective-permute-start.12 = (bf16[12,128,128]{2,1,0:T(8,128)(2,1)S(1)}, bf16[12,128,128]{2,1,0:T(8,128)(2,1)S(1)}, u32[]{:S(2)}, u32[]{:S(2)}) collective-permute-start(bf16[12,128,128]{2,1,0:T(8,128)(2,1)S(1)} %add_convert_fusion.1), channel_id=1, source_target_pairs={{0,4},{1,5},{2,6},{3,7},{4,8},{5,9},{6,10},{7,11},{8,12},{9,13},{1... | collective-permute-start | bytes 1179656 | tf_op jit(solution)/shard_map/ppermute | solution.py:404
  106.3 0.0 collective-permute-done.8
  106.4 0.7 collective-permute-done.10
  107.1 7.7 %collective-permute-done.12 = bf16[12,128,128]{2,1,0:T(8,128)(2,1)S(1)} collective-permute-done((bf16[12,128,128]{2,1,0:T(8,128)(2,1)S(1)}, bf16[12,128,128]{2,1,0:T(8,128)(2,1)S(1)}, u32[]{:S(2)}, u32[]{:S(2)}) %collective-permute-start.12) | collective-permute-done | bytes 393248 | tf_op jit(solution)/shard_map/ppermute | solution.py:404
  114.8 0.9 add_convert_fusion
  115.7 0.0 collective-permute-done.14
  115.7 0.2 fusion.1
  115.9 1.0 fusion.3
  (4 shorter events, 0.0 us)
Async XLA Ops:
  3.9 27.2 %collective-permute-start.1 = (bf16[3168,128]{1,0:T(8,128)(2,1)}, bf16[3168,128]{1,0:T(8,128)(2,1)S(1)}, u32[]{:S(2)}, u32[]{:S(2)}) collective-permute-start(bf16[3168,128]{1,0:T(8,128)(2,1)} %get-tuple-element.29.refs_0_), channel_id=1, source_target_pairs={{4,0},{5,1},{6,2},{7,3},{8,4},{9,5},{10,6},{11,7},{12,8},{13,9},{1... | collective-permute-start | bytes 2433032 | tf_op jit(solution)/shard_map/ppermute | solution.py:404
  5.2 25.9 %collective-permute-start = (bf16[3168,128]{1,0:T(8,128)(2,1)}, bf16[3168,128]{1,0:T(8,128)(2,1)S(1)}, u32[]{:S(2)}, u32[]{:S(2)}) collective-permute-start(bf16[3168,128]{1,0:T(8,128)(2,1)} %get-tuple-element.29.refs_0_), channel_id=1, source_target_pairs={{0,4},{1,5},{2,6},{3,7},{4,8},{5,9},{6,10},{7,11},{8,12},{9,13},{1... | collective-permute-start | bytes 2433032 | tf_op jit(solution)/shard_map/ppermute | solution.py:404
  10.8 19.4 %collective-permute-start.3 = (bf16[3072,128]{1,0:T(8,128)(2,1)}, bf16[3072,128]{1,0:T(8,128)(2,1)}, u32[]{:S(2)}, u32[]{:S(2)}) collective-permute-start(bf16[3072,128]{1,0:T(8,128)(2,1)} %get-tuple-element.23.refs_1_), channel_id=1, source_target_pairs={{0,2},{1,3},{2,0},{3,1},{4,6},{5,7},{6,4},{7,5},{8,10},{9,11},{10,... | collective-permute-start | bytes 2359304 | tf_op jit(solution)/shard_map/ppermute | solution.py:404
  12.8 17.4 %collective-permute-start.2 = (bf16[3072,128]{1,0:T(8,128)(2,1)}, bf16[3072,128]{1,0:T(8,128)(2,1)S(1)}, u32[]{:S(2)}, u32[]{:S(2)}) collective-permute-start(bf16[3072,128]{1,0:T(8,128)(2,1)} %get-tuple-element.23.refs_1_), channel_id=1, source_target_pairs={{0,1},{1,0},{2,3},{3,2},{4,5},{5,4},{6,7},{7,6},{8,9},{9,8},{10,11... | collective-permute-start | bytes 2359304 | tf_op jit(solution)/shard_map/ppermute | solution.py:404
  30.2 0.9 copy-start.2
  31.1 25.8 %collective-permute-start.7 = (bf16[3168,128]{1,0:T(8,128)(2,1)}, bf16[3168,128]{1,0:T(8,128)(2,1)S(1)}, u32[]{:S(2)}, u32[]{:S(2)}) collective-permute-start(bf16[3168,128]{1,0:T(8,128)(2,1)} %get-tuple-element.29.refs_0_), channel_id=1, source_target_pairs={{12,0},{13,1},{14,2},{15,3},{0,12},{1,13},{2,14},{3,15},{28,16},{2... | collective-permute-start | bytes 2433032 | tf_op jit(solution)/shard_map/ppermute | solution.py:404
  34.9 22.0 %collective-permute-start.5 = (bf16[3168,128]{1,0:T(8,128)(2,1)S(1)}, bf16[3168,128]{1,0:T(8,128)(2,1)S(1)}, u32[]{:S(2)}, u32[]{:S(2)}) collective-permute-start(bf16[3168,128]{1,0:T(8,128)(2,1)S(1)} %collective-permute-done.refs_0_), channel_id=1, source_target_pairs={{4,8},{5,9},{6,10},{7,11},{8,12},{9,13},{10,14},{11,15},{20,24},{2... | collective-permute-start | bytes 2433032 | tf_op jit(solution)/shard_map/ppermute | solution.py:404
  35.6 35.5 %collective-permute-start.6 = (bf16[3168,128]{1,0:T(8,128)(2,1)S(1)}, bf16[3168,128]{1,0:T(8,128)(2,1)}, u32[]{:S(2)}, u32[]{:S(2)}) collective-permute-start(bf16[3168,128]{1,0:T(8,128)(2,1)S(1)} %collective-permute-done.1.refs_1_), channel_id=1, source_target_pairs={{4,0},{5,1},{6,2},{7,3},{8,4},{9,5},{10,6},{11,7},{20,16},{21,17},... | collective-permute-start | bytes 2433032 | tf_op jit(solution)/shard_map/ppermute | solution.py:404
  36.9 2.7 %collective-permute-start.4 = (bf16[3072,128]{1,0:T(8,128)(2,1)}, bf16[3072,128]{1,0:T(8,128)(2,1)}, u32[]{:S(2)}, u32[]{:S(2)}) collective-permute-start(bf16[3072,128]{1,0:T(8,128)(2,1)} %collective-permute-done.3.refs_3_), channel_id=1, source_target_pairs={{0,1},{1,0},{2,3},{3,2},{4,5},{5,4},{6,7},{7,6},{8,9},{9,8},{10,11... | collective-permute-start | bytes 2359304 | tf_op jit(solution)/shard_map/ppermute | solution.py:404
  39.6 1.1 copy-start
  40.7 1.1 copy-start.1
  41.9 1.1 copy-start.3
  81.4 5.5 %collective-permute-start.13 = (bf16[2,2,12,128,128]{4,3,2,1,0:T(8,128)(2,1)S(1)}, bf16[2,2,12,128,128]{4,3,2,1,0:T(8,128)(2,1)S(1)}, u32[]{:S(2)}, u32[]{:S(2)}) collective-permute-start(bf16[2,2,12,128,128]{4,3,2,1,0:T(8,128)(2,1)S(1)} %get-tuple-element.40), channel_id=1, source_target_pairs={{0,1},{1,0},{2,3},{3,2},{4,5},{5,4},{6,7},{7,6},{8,9},{9,8},{10,11... | collective-permute-start | bytes 4718600 | tf_op jit(solution)/shard_map/ppermute | solution.py:404
  81.4 3.9 %collective-permute-start.9 = (bf16[12,128,128]{2,1,0:T(8,128)(2,1)S(1)}, bf16[12,128,128]{2,1,0:T(8,128)(2,1)S(1)}, u32[]{:S(2)}, u32[]{:S(2)}) collective-permute-start(bf16[12,128,128]{2,1,0:T(8,128)(2,1)S(1)} %get-tuple-element.36), channel_id=1, source_target_pairs={{8,4},{9,5},{10,6},{11,7},{12,8},{13,9},{14,10},{15,11},{24,20},{2... | collective-permute-start | bytes 1179656 | tf_op jit(solution)/shard_map/ppermute | solution.py:404
  82.1 24.2 %collective-permute-start.8 = (bf16[12,128,128]{2,1,0:T(8,128)(2,1)S(1)}, bf16[12,128,128]{2,1,0:T(8,128)(2,1)S(1)}, u32[]{:S(2)}, u32[]{:S(2)}) collective-permute-start(bf16[12,128,128]{2,1,0:T(8,128)(2,1)S(1)} %get-tuple-element.34), channel_id=1, source_target_pairs={{12,0},{13,1},{14,2},{15,3},{0,12},{1,13},{2,14},{3,15},{28,16},{2... | collective-permute-start | bytes 1179656 | tf_op jit(solution)/shard_map/ppermute | solution.py:404
  84.1 17.8 %collective-permute-start.11 = (bf16[12,128,128]{2,1,0:T(8,128)(2,1)S(1)}, bf16[12,128,128]{2,1,0:T(8,128)(2,1)S(1)}, u32[]{:S(2)}, u32[]{:S(2)}) collective-permute-start(bf16[12,128,128]{2,1,0:T(8,128)(2,1)S(1)} %get-tuple-element.38), channel_id=1, source_target_pairs={{0,4},{1,5},{2,6},{3,7},{4,8},{5,9},{6,10},{7,11},{16,20},{17,21},... | collective-permute-start | bytes 1179656 | tf_op jit(solution)/shard_map/ppermute | solution.py:404
  85.5 21.6 %collective-permute-start.10 = (bf16[12,128,128]{2,1,0:T(8,128)(2,1)S(1)}, bf16[12,128,128]{2,1,0:T(8,128)(2,1)S(1)}, u32[]{:S(2)}, u32[]{:S(2)}) collective-permute-start(bf16[12,128,128]{2,1,0:T(8,128)(2,1)S(1)} %add_convert_fusion.2), channel_id=1, source_target_pairs={{4,0},{5,1},{6,2},{7,3},{8,4},{9,5},{10,6},{11,7},{12,8},{13,9},{1... | collective-permute-start | bytes 1179656 | tf_op jit(solution)/shard_map/ppermute | solution.py:404
  87.4 28.3 %collective-permute-start.14 = (bf16[2,1,12,128,128]{4,3,2,0,1:T(8,128)(2,1)S(1)}, bf16[2,1,12,128,128]{4,3,2,0,1:T(8,128)(2,1)S(1)}, u32[]{:S(2)}, u32[]{:S(2)}) collective-permute-start(bf16[2,1,12,128,128]{4,3,2,0,1:T(8,128)(2,1)S(1)} %fusion.2), channel_id=1, source_target_pairs={{0,2},{1,3},{2,0},{3,1},{4,6},{5,7},{6,4},{7,5},{8,10},{9,11},{10,... | collective-permute-start | bytes 2359304 | tf_op jit(solution)/shard_map/ppermute | solution.py:404
  101.9 12.8 %collective-permute-start.12 = (bf16[12,128,128]{2,1,0:T(8,128)(2,1)S(1)}, bf16[12,128,128]{2,1,0:T(8,128)(2,1)S(1)}, u32[]{:S(2)}, u32[]{:S(2)}) collective-permute-start(bf16[12,128,128]{2,1,0:T(8,128)(2,1)S(1)} %add_convert_fusion.1), channel_id=1, source_target_pairs={{0,4},{1,5},{2,6},{3,7},{4,8},{5,9},{6,10},{7,11},{8,12},{9,13},{1... | collective-permute-start | bytes 1179656 | tf_op jit(solution)/shard_map/ppermute | solution.py:404

commit v3 on v2

--- a/solution.py
+++ b/solution.py
@@ -11,9 +11,10 @@
 GLOB = 2
 TILE = 16
 PAIRS = 3
+TURNS = 3
 FAR = 1e30
-COST = 0
-LIMIT = 24 * 2**20
+COST = 20
+LIMIT = 16 * 2**20
 
 
 def pieces(row):
@@ -28,56 +29,106 @@
     return -(-count // TILE) * TILE
 
 
-def pack_kernel(query, grad, output, key, value, lse, unit, keyval, delta_s):
+def placed(array, space):
+    return pltpu.with_memory_space_constraint(array, space)
+
+
+def groups_of(count):
+    return next(groups for groups in (3, 4, 2, 1) if count % groups == 0)
+
+
+def pack_kernel(query, grad, output, lse, unit, output_s, delta_s, sems):
     count, width = lse.shape
     rows = stat_rows(count)
-    group = 4 if count % 4 == 0 else 1
+    groups = groups_of(count)
+    group = count // groups
     ones = jnp.ones((TILE, width), jnp.bfloat16)
+    held = count * BLK
+    loads = []
+    for g in range(groups):
+        at = pl.ds(g * group * BLK, group * BLK)
+        after = pl.ds(held + g * group * BLK, group * BLK)
+        loads.append(
+            [
+                pltpu.make_async_copy(grad.at[at], unit.at[after], sems.at[0, g]),
+                pltpu.make_async_copy(output.at[at], output_s.at[at], sems.at[1, g]),
+                pltpu.make_async_copy(query.at[at], unit.at[at], sems.at[2, g]),
+            ]
+        )
+    for kind in range(3):
+        for load in loads:
+            load[kind].start()
 
     def total(part):
         return lax.dot_general(
             ones, part, (((1,), (1,)), ((), ())), preferred_element_type=jnp.float32
         )
 
-    def step(g, carry):
+    delta_s[...] = jnp.zeros(delta_s.shape, jnp.float32)
+    for g in range(groups):
+        loads[g][0].wait()
+        loads[g][1].wait()
         highs, lows = ([], [])
-        for k in range(group):
-            at = pl.ds(pl.multiple_of((g * group + k) * BLK, BLK), BLK)
-            after = pl.ds(pl.multiple_of((count + g * group + k) * BLK, BLK), BLK)
-            grads = grad[at, :]
-            unit[at, :] = query[at, :]
-            unit[after, :] = grads
-            keyval[at, :] = key[at, :]
-            keyval[after, :] = value[at, :]
-            product = grads.astype(jnp.float32) * output[at, :].astype(jnp.float32)
+        for k in range(g * group, (g + 1) * group):
+            grads = unit[held + k * BLK : held + (k + 1) * BLK, :].astype(jnp.float32)
+            product = grads * output_s[k * BLK : (k + 1) * BLK, :].astype(jnp.float32)
             highs.append(product.astype(jnp.bfloat16))
             lows.append((product - highs[-1].astype(jnp.float32)).astype(jnp.bfloat16))
         sums = [total(high) + total(low) for high, low in zip(highs, lows)]
         for k in range(group):
-            delta_s[pl.ds(g * group + k, 1), :] = sums[k][0:1]
-        return carry
-
-    delta_s[...] = jnp.zeros(delta_s.shape, jnp.float32)
-    lax.fori_loop(0, count // group, step, 0)
+            delta_s[g * group + k : g * group + k + 1, :] = sums[k][0:1]
     lines = lse[...]
     if rows > count:
         lines = jnp.concatenate([lines, jnp.zeros((rows - count, width), jnp.float32)], 0)
     stats = pieces(lines) + pieces(delta_s[...])
-    unit[2 * count * BLK :, :] = jnp.concatenate(stats, 0).astype(jnp.bfloat16)
-
-
-def pack(query, grad, output, key, value, lse):
+    unit[2 * held :, :] = jnp.concatenate(stats, 0).astype(jnp.bfloat16)
+    for load in loads:
+        load[2].wait()
+
+
+def pack(query, grad, output, lse):
     count, width = lse.shape
     rows = stat_rows(count)
+    hbm = pl.BlockSpec(memory_space=pltpu.HBM)
     return pl.pallas_call(
         pack_kernel,
-        out_shape=(
-            jax.ShapeDtypeStruct((2 * count * BLK + 6 * rows, width), jnp.bfloat16),
-            jax.ShapeDtypeStruct((2 * count * BLK, width), jnp.bfloat16),
-        ),
-        scratch_shapes=[pltpu.VMEM((rows, width), jnp.float32)],
+        out_shape=jax.ShapeDtypeStruct((2 * count * BLK + 6 * rows, width), jnp.bfloat16),
+        in_specs=[hbm, hbm, hbm, pl.BlockSpec(memory_space=pltpu.VMEM)],
+        out_specs=pl.BlockSpec(memory_space=pltpu.VMEM),
+        scratch_shapes=[
+            pltpu.VMEM(query.shape, jnp.bfloat16),
+            pltpu.VMEM((rows, width), jnp.float32),
+            pltpu.SemaphoreType.DMA((3, groups_of(count))),
+        ],
+        compiler_params=pltpu.CompilerParams(vmem_limit_bytes=LIMIT),
         name="pack",
-    )(query, grad, output, key, value, lse)
+    )(*[placed(array, pltpu.HBM) for array in (query, grad, output)], lse)
+
+
+def join_kernel(key, value, keyval, sems):
+    rows = key.shape[0]
+    copies = [
+        pltpu.make_async_copy(key, keyval.at[pl.ds(0, rows)], sems.at[0]),
+        pltpu.make_async_copy(value, keyval.at[pl.ds(rows, rows)], sems.at[1]),
+    ]
+    for copy in copies:
+        copy.start()
+    for copy in copies:
+        copy.wait()
+
+
+def join(key, value):
+    rows, width = key.shape
+    hbm = pl.BlockSpec(memory_space=pltpu.HBM)
+    return pl.pallas_call(
+        join_kernel,
+        out_shape=jax.ShapeDtypeStruct((2 * rows, width), key.dtype),
+        in_specs=[hbm, hbm],
+        out_specs=pl.BlockSpec(memory_space=pltpu.VMEM),
+        scratch_shapes=[pltpu.SemaphoreType.DMA((2,))],
+        compiler_params=pltpu.CompilerParams(vmem_limit_bytes=LIMIT),
+        name="join",
+    )(placed(key, pltpu.HBM), placed(value, pltpu.HBM))
 
 
 def pair_grads(pairs, scaling):
@@ -112,16 +163,18 @@
 
 
 class Visitor:
-    def __init__(self, count, unit, lse, delta, dq, keys, values, acc, layout, lists):
+    def __init__(
+        self, count, unit, lse, delta, dq, keys, values, acc, layout=None, lists=None, values_at=0
+    ):
         self.count = count
         self.unit, self.lse, self.delta = (unit, lse, delta)
         self.dq, self.keys, self.values, self.acc = (dq, keys, values, acc)
-        self.layout, self.lists = (layout, lists)
+        self.layout, self.lists, self.values_at = (layout, lists, values_at)
         self.width = unit.shape[1]
         self.scaling = self.width ** (-0.5)
         self.held = keys.shape[0] // BLK
 
-    def begin(self):
+    def begin(self, clear=True):
         count = self.count
         rows = stat_rows(count)
         stats = self.unit[2 * count * BLK :, :].astype(jnp.float32)
@@ -133,7 +186,8 @@
             self.dq[q] = jnp.zeros(self.dq.shape[1:], jnp.float32)
             return carry
 
-        lax.fori_loop(0, count, step, 0)
+        if clear:
+            lax.fori_loop(0, count, step, 0)
 
     def rows(self, array, block, blocks=1):
         return array[pl.ds(pl.multiple_of(block * BLK, BLK), blocks * BLK), :]
@@ -141,7 +195,7 @@
     def pair(self, q, j, keys=1, shift=0.0, mask=None):
         return (
             self.rows(self.keys, j, keys),
-            self.rows(self.values, j, keys),
+            self.rows(self.values, self.values_at + j, keys),
             self.rows(self.unit, q),
             self.rows(self.unit, self.count + q),
             self.lse[pl.ds(q, 1), :] + shift,
@@ -149,7 +203,7 @@
             mask,
         )
 
-    def window(self, base):
+    def window(self):
         count, width = (self.count, self.width)
         chunk = 2 if count % 2 == 0 else 1
 
@@ -157,9 +211,9 @@
             places, pairs = ([], [])
             for k in range(chunk):
                 q = c * chunk + k
-                start = jnp.clip(base + q - 1, 0, self.held - 3)
+                start = jnp.clip(q - 1, 0, count - 3)
                 block = lax.broadcasted_iota(jnp.int32, (3 * BLK, BLK), 0) // BLK
-                block = block + start - base - q
+                block = block + start - q
                 places.append((q, start))
                 pairs.append(self.pair(q, start, 3, 0.0, (block >= -1) & (block <= 1)))
             parts = pair_grads(pairs, self.scaling)
@@ -174,7 +228,7 @@
     def anchors(self):
         count, width = (self.count, self.width)
         chunk = 2 if count % 2 == 0 else 1
-        turns = 2 if count % (2 * chunk) == 0 else 1
+        turns = next(turns for turns in (TURNS, 2, 1) if count % (turns * chunk) == 0)
 
         def step(c, carry):
             places, pairs = ([], [])
@@ -257,8 +311,20 @@
         lax.fori_loop(0, self.count, step, 0)
 
 
+def own_kernel(unit, keyval, acc, dq, lse, delta):
+    def clear(b, carry):
+        acc[b] = jnp.zeros(acc.shape[1:], jnp.float32)
+        return carry
+
+    count = dq.shape[0]
+    lax.fori_loop(0, count, clear, 0)
+    own = Visitor(count, unit, lse, delta, dq, keyval, keyval, acc, values_at=count)
+    own.begin()
+    own.window()
+
+
 def visit_kernel(plan, me_ref, layout, *refs):
-    offsets, count, span, fanout, last = plan
+    offsets, count, span, fanout = plan
     refs = list(refs)
     first = offsets == (0,)
     guests = [refs.pop(0) for _ in offsets]
@@ -269,14 +335,13 @@
     low = row * span * count
     if first:
         parts = [refs.pop(0) for _ in range(span)]
+        acc_own, dq_own = (refs.pop(0), refs.pop(0))
         keys, values = (refs.pop(0), refs.pop(0))
     else:
         keys, values = (refs.pop(0), refs.pop(0))
         refs.pop(0)
     acc = refs.pop(0)
     outs = [refs.pop(0) for _ in offsets]
-    if last:
-        sent, kept = (refs.pop(0), refs.pop(0))
     sums = outs if first else [refs.pop(0) for _ in offsets]
     lse, delta = (refs.pop(0), refs.pop(0))
     lists = refs
@@ -285,7 +350,11 @@
         def lay(b, carry):
             for m in range(span):
                 there = jnp.bitwise_xor(seat, m) * count + b
-                acc[there] = jnp.zeros(acc.shape[1:], jnp.float32)
+                if m == 0:
+                    acc[there] = acc_own[b]
+                    sums[0][b] = dq_own[b]
+                else:
+                    acc[there] = jnp.zeros(acc.shape[1:], jnp.float32)
                 there = pl.ds(pl.multiple_of(there * BLK, BLK), BLK)
                 here = pl.ds(pl.multiple_of(b * BLK, BLK), BLK)
                 keys[there, :] = parts[m][here, :]
@@ -303,63 +372,172 @@
             guest = me + offset * span
             present = (guest >= 0) & (guest < shards)
         visitor = Visitor(count, guests[v], lse, delta, sums[v], keys, values, acc, layout, lists)
-        visitor.begin()
-        if offset == 0:
-            visitor.window(seat * count)
 
         @pl.when(present)
-        def _(visitor=visitor, near=offset in (-1, 1), guest=guest):
+        def _(visitor=visitor, offset=offset, guest=guest, out=outs[v]):
+            visitor.begin(offset != 0)
             @pl.when(row == 0)
             def _():
                 visitor.anchors()
 
-            visitor.scattered(guest, low, fanout, near)
-
-        visitor.finish(outs[v])
-
-    if last:
-        scaling = keys.shape[1] ** (-0.5)
-
-        def finish(b, carry):
-            for k in range(span // 2):
-                mine = jnp.bitwise_xor(seat, 2 * k) * count + b
-                theirs = jnp.bitwise_xor(seat, 2 * k + 1) * count + b
-                sent[0, k, b] = (acc[theirs, 0] * scaling).astype(jnp.bfloat16)
-                sent[1, k, b] = acc[theirs, 1].astype(jnp.bfloat16)
-                kept[0, k, b] = acc[mine, 0] * scaling
-                kept[1, k, b] = acc[mine, 1]
-            return carry
-
-        lax.fori_loop(0, count, finish, 0)
+            visitor.scattered(guest, low, fanout, offset in (-1, 0, 1))
+            visitor.finish(out)
+
+
+def sum_of(m, which, b, acc, place, scaling, parts, arrived):
+    total = acc[place, which]
+    if which == 0:
+        total = total * scaling
+    for part, units in zip(parts, arrived):
+        total = total + part[which, units.index(m), b].astype(jnp.float32)
+    return total.astype(jnp.bfloat16)
+
+
+def share_kernel(plan, me_ref, acc, *refs):
+    span, wanted, arrived = plan
+    parts, out = (refs[:-1], refs[-1])
+    count = acc.shape[0] // span
+    scaling = acc.shape[3] ** (-0.5)
+    seat = lax.rem(me_ref[0], span)
+
+    def step(b, carry):
+        for k, m in enumerate(wanted):
+            place = jnp.bitwise_xor(seat, m) * count + b
+            for which in range(2):
+                out[which, k, b] = sum_of(m, which, b, acc, place, scaling, parts, arrived)
+        return carry
+
+    lax.fori_loop(0, count, step, 0)
+
+
+def finish_kernel(plan, me_ref, acc, *refs):
+    span, arrived = plan
+    parts, outs = (refs[: len(arrived)], refs[len(arrived) : len(arrived) + 2])
+    held_s, sems = refs[len(arrived) + 2 :]
+    count = acc.shape[0] // span
+    scaling = acc.shape[3] ** (-0.5)
+    seat = lax.rem(me_ref[0], span)
+    groups = groups_of(count)
+    group = count // groups
+    copies = []
+    for g in range(groups):
+        for b in range(g * group, (g + 1) * group):
+            for which in range(2):
+                held_s[which, b * BLK : (b + 1) * BLK, :] = sum_of(
+                    0, which, b, acc, seat * count + b, scaling, parts, arrived
+                )
+        for which in range(2):
+            at = pl.ds(g * group * BLK, group * BLK)
+            copies.append(
+                pltpu.make_async_copy(
+                    held_s.at[which, at], outs[which].at[at], sems.at[which, g]
+                )
+            )
+            copies[-1].start()
+    for copy in copies:
+        copy.wait()
 
 
 SMEM = pl.BlockSpec(memory_space=pltpu.SMEM)
 VMEM = pl.BlockSpec(memory_space=pltpu.VMEM)
 
 
-def in_place(array):
-    return pltpu.with_memory_space_constraint(array, pltpu.VMEM)
-
-
-def visit(me, layout, units, offsets, keyvals, acc, last, count, span, fanout):
-    first = acc is None
+def own_visit(unit, keyval, count):
+    width = unit.shape[1]
+    stats = pltpu.VMEM((stat_rows(count), width), jnp.float32)
+    return pl.pallas_call(
+        own_kernel,
+        out_shape=(
+            jax.ShapeDtypeStruct((count, 2, BLK, width), jnp.float32),
+            jax.ShapeDtypeStruct((count, BLK, width), jnp.float32),
+        ),
+        scratch_shapes=[stats, stats],
+        compiler_params=pltpu.CompilerParams(vmem_limit_bytes=LIMIT),
+        name="own",
+    )(unit, keyval)
+
+
+def share(me, acc, span, wanted, arrived, parts):
+    held, _, _, width = acc.shape
+    return pl.pallas_call(
+        functools.partial(share_kernel, (span, wanted, arrived)),
+        out_shape=jax.ShapeDtypeStruct((2, len(wanted), held // span, BLK, width), jnp.bfloat16),
+        in_specs=[SMEM] + [VMEM] * (1 + len(parts)),
+        out_specs=VMEM,
+        compiler_params=pltpu.CompilerParams(vmem_limit_bytes=LIMIT),
+        name="share",
+    )(me, acc, *parts)
+
+
+def finish(me, acc, span, arrived, parts):
+    held, _, _, width = acc.shape
+    count = held // span
+    shape = (count * BLK, width)
+    hbm = pl.BlockSpec(memory_space=pltpu.HBM)
+    return pl.pallas_call(
+        functools.partial(finish_kernel, (span, arrived)),
+        out_shape=[jax.ShapeDtypeStruct(shape, jnp.bfloat16)] * 2,
+        in_specs=[SMEM] + [VMEM] * (1 + len(parts)),
+        out_specs=[hbm, hbm],
+        scratch_shapes=[
+            pltpu.VMEM((2,) + shape, jnp.bfloat16),
+            pltpu.SemaphoreType.DMA((2, groups_of(count))),
+        ],
+        compiler_params=pltpu.CompilerParams(vmem_limit_bytes=LIMIT),
+        name="finish",
+    )(me, acc, *parts)
+
+
+def add_kernel(base, *refs):
+    parts, out = (refs[:-1], refs[-1])
+
+    def step(b, carry):
+        total = base[b]
+        for part in parts:
+            total = total + part[b].astype(jnp.float32)
+        if len(out.shape) == 3:
+            out[b] = total
+        else:
+            out[pl.ds(pl.multiple_of(b * BLK, BLK), BLK), :] = total.astype(out.dtype)
+        return carry
+
+    lax.fori_loop(0, base.shape[0], step, 0)
+
+
+def add(base, parts, final, weight):
+    count, _, width = base.shape
+    if final:
+        out = jax.ShapeDtypeStruct((count * BLK, width), jnp.bfloat16)
+    else:
+        out = jax.ShapeDtypeStruct(base.shape, jnp.float32)
+    return pl.pallas_call(
+        add_kernel,
+        out_shape=out,
+        cost_estimate=pl.CostEstimate(
+            flops=weight * count * 10 * BLK * BLK * width, bytes_accessed=0, transcendentals=0
+        ),
+        compiler_params=pltpu.CompilerParams(vmem_limit_bytes=LIMIT),
+        name="add",
+    )(base, *parts)
+
+
+def visit(me, layout, units, offsets, keyvals, acc, query_acc, weight, count, span, fanout):
+    first = query_acc is not None
     width = units[0].shape[1]
     held = span * count
-    plan = (offsets, count, span, fanout, last)
+    plan = (offsets, count, span, fanout)
     operands = units + keyvals
     keys = jax.ShapeDtypeStruct((held * BLK, width), jnp.bfloat16)
     outs = [jax.ShapeDtypeStruct((held, 2, BLK, width), jnp.float32)]
-    aliases = {}
     if first:
         outs = [keys, keys] + outs
+        aliases = {}
+        operands = operands + [acc, query_acc]
     else:
-        aliases[len(operands) + 2] = 0
-        operands = operands + [in_place(acc)]
+        aliases = {len(operands) + 2: 0}
+        operands = operands + [placed(acc, pltpu.VMEM)]
     kind = jnp.float32 if first else jnp.bfloat16
     outs += [jax.ShapeDtypeStruct((count, BLK, width), kind)] * len(units)
-    if last:
-        outs.append(jax.ShapeDtypeStruct((2, span // 2, count, BLK, width), jnp.bfloat16))
-        outs.append(jax.ShapeDtypeStruct((2, span // 2, count, BLK, width), jnp.float32))
     entries = count * fanout + 2 + PAIRS
     stats = pltpu.VMEM((stat_rows(count), width), jnp.float32)
     return list(
@@ -380,8 +558,8 @@
             ],
             compiler_params=pltpu.CompilerParams(vmem_limit_bytes=LIMIT),
             cost_estimate=pl.CostEstimate(
-                flops=COST * len(offsets) * count * 10 * BLK * BLK * width,
-                bytes_accessed=2**20,
+                flops=weight * count * 10 * BLK * BLK * width,
+                bytes_accessed=0,
                 transcendentals=len(offsets) * count * BLK * BLK,
             ),
             name="visit",
@@ -418,75 +596,77 @@
 
     me = jnp.stack([myself, jnp.int32(shards)]).astype(jnp.int32)
     entries = layout.reshape(-1)
-    unit, keyval = pack(
-        query_rows, output_grad, output_rows, key_rows, value_rows, logsumexp.reshape(count, BLK)
-    )
+    unit = pack(query_rows, output_grad, output_rows, logsumexp.reshape(count, BLK))
+    keyval = join(key_rows, value_rows)
 
     def merge(one, two):
         return (one.astype(jnp.float32) + two.astype(jnp.float32)).astype(jnp.bfloat16)
 
-    def wide(array):
-        return array.astype(jnp.float32)
-
     def tie(*arrays):
         return lax.optimization_barrier(arrays)
 
     last = planes - 1
-    ends = [(last * span + e, e) for e in range(span)]
-    ends = ends + [(two, one) for one, two in ends]
     up, down = (shift(unit, 1, 0, last), shift(unit, -1, 1, planes))
     keyvals = {0: keyval}
     singles = [m for m in range(1, span) if m & (m - 1) == 0]
     for m in singles:
         keyvals[m] = swap(keyval, m)
-    up, down, far, *arrived = tie(up, down, unit, *[keyvals[m] for m in singles])
-    keyvals.update(zip(singles, arrived))
-    far = send(far, ends)
+    acc, query_acc = own_visit(unit, keyval, count)
+    up, down, query_acc = tie(up, down, query_acc)
     for m in range(1, span):
         if m & (m - 1):
             keyvals[m] = swap(keyvals[m & (m - 1)], m & -m)
     keyvals = [keyvals[m] for m in range(span)]
 
-    def meet(units, offsets, keyvals, acc, final=False):
-        return visit(me, entries, units, offsets, keyvals, acc, final, count, span, fanout)
-
-    keys, values, acc, query_acc = meet([unit], (0,), keyvals, None)
+    def meet(units, offsets, keyvals, acc, query_acc=None, weight=0):
+        return visit(
+            me, entries, units, offsets, keyvals, acc, query_acc, weight, count, span, fanout
+        )
+
+    keys, values, acc, query_acc = meet([unit], (0,), keyvals, acc, query_acc)
+    above = myself >= shards // 2
+    inward = [(p * span + e, q * span + e) for p, q in ((last - 1, last), (1, 0)) for e in range(span)]
+    ends = [(last * span + e, e) for e in range(span)]
+    ends = ends + [(two, one) for one, two in ends]
     up_parts, down_parts = ([], [])
     for s in range(1, last):
         if s + 1 < last:
             next_up, next_down = (shift(up, 1, s, last), shift(down, -1, 1, planes - s))
-        final = s + 1 == last
-        units, offsets = ([up, down], (-s, s))
-        if final:
-            units, offsets = (units + [far], offsets + (None,))
-        acc, up_part, down_part, *rest = meet(units, offsets, [keys, values], acc, final)
+        else:
+            up, down, query_acc = tie(up, down, query_acc)
+            far = send(jnp.where(above, up, down), inward)
+        acc, up_part, down_part = meet([up, down], (-s, s), [keys, values], acc)
         up_parts.append(up_part)
         down_parts.append(down_part)
-        if not final:
+        if s + 1 < last:
             up, down = (next_up, next_down)
-    far_part, sent, kept = rest
+
+    acc, far_part = meet([far], (None,), [keys, values], acc, None, COST)
 
     up_back, down_back = (up_parts[-1], down_parts[-1])
-    for t in range(last - 1, 0, -1):
-        up_back = shift(up_back, -1, t, planes)
-        down_back = shift(down_back, 1, 0, planes - t)
-        if t > 1:
-            up_back = merge(up_parts[t - 2], up_back)
-            down_back = merge(down_parts[t - 2], down_back)
-    query_acc = query_acc + wide(send(far_part, ends)) + wide(up_back) + wide(down_back)
-
+    for t in range(last - 1, 1, -1):
+        up_back, down_back = (shift(up_back, -1, t, planes), shift(down_back, 1, 0, planes - t))
+        if t == 2:
+            up_back, down_back, far_part = tie(up_back, down_back, far_part)
+        up_back = merge(up_parts[t - 2], up_back)
+        down_back = merge(down_parts[t - 2], down_back)
+    acc, up_back, down_back = tie(acc, up_back, down_back)
+    query_acc = add(query_acc, [send(far_part, ends)], False, COST)
+    query_grad = add(
+        query_acc, [shift(up_back, -1, 1, planes), shift(down_back, 1, 0, planes - 1)], True, 1
+    )
+
+    wanted = tuple(range(span))
+    arrived, parts = ((), ())
     bit = 1
-    while True:
-        kept = kept + swap(sent, bit).astype(jnp.float32)
+    while bit < span:
+        theirs = tuple(m for m in wanted if m & bit)
+        wanted = tuple(m for m in wanted if not m & bit)
+        sent = share(me, acc, span, theirs, arrived, parts)
+        arrived, parts = (arrived + (wanted,), parts + (swap(sent, bit),))
         bit = bit * 2
-        if bit == span:
-            break
-        halves = kept.reshape((2, kept.shape[1] // 2, 2) + kept.shape[2:])
-        kept = halves[:, :, 0]
-        sent = halves[:, :, 1].astype(jnp.bfloat16)
-    query_grad = query_acc.reshape(count * BLK, width).astype(jnp.bfloat16)
-    key_grad = kept[0, 0].reshape(count * BLK, width).astype(jnp.bfloat16)
-    value_grad = kept[1, 0].reshape(count * BLK, width).astype(jnp.bfloat16)
+    *parts, query_grad = tie(*parts, query_grad)
+    key_grad, value_grad = finish(me, acc, span, arrived, parts)
     return (query_grad, key_grad, value_grad)
 
 

time: 117 us -> 105 us (0.90)
  waiting for transfers between devices: 54.9 us -> 40.9 us
  Pallas kernels: 27.4 us -> 30 us
  other arithmetic: 1.94 us -> 0.45 us
  starting transfers between devices: 25.3 us -> 26.7 us
    ppermute x15, waiting for transfers between devices: 54.9 us -> 40.9 us  [send(): return lax.ppermute(array, 'qb', pairs)]
    pallas_call x1 -> x8, Pallas kernels: 3.26 us -> 10.9 us  [the longest x1 3.65 us: own_visit(): pl.pallas_call(own_kernel, out_shape=(jax.ShapeDtypeStruct((count, 2, BLK...]
    pallas_call x3 -> x4, Pallas kernels: 24.2 us -> 19.1 us  [visit(): pl.pallas_call(functools.partial(visit_kernel, plan), out_shape=outs, in_...]
    ppermute x15, starting transfers between devices: 25.3 us -> 26.7 us  [send(): return lax.ppermute(array, 'qb', pairs)]
    unnamed x9 -> x13, local copies, waits for them, and re-layouts: 5.11 us -> 5.42 us
  transfers between devices with their start and end apart: 15 -> 15, of which waited for: 6 -> 9; matrix products, arithmetic and copies ran while one was open for 2% -> 0% of each run, Pallas kernels for 12% -> 25%
where the time goes in v3:
time: 105 us; the launch traced here: 104 us
  waiting for transfers between devices  40.9 us (39%)
  Pallas kernels  30 us (29%)
  starting transfers between devices  26.7 us (25%)
  local copies, waits for them, and re-layouts  5.62 us (5%)
    ppermute x15, waiting for transfers between devices, send(): return lax.ppermute(array, 'qb', pairs)  40.9 us
    ppermute x15, starting transfers between devices, send(): return lax.ppermute(array, 'qb', pairs)  26.7 us
    pallas_call x4, Pallas kernels, visit(): pl.pallas_call(functools.partial(visit_kernel, plan), out_shape=outs, in_...  19.1 us
    unnamed x13, local copies, waits for them, and re-layouts  5.42 us
    pallas_call x1, Pallas kernels, own_visit(): pl.pallas_call(own_kernel, out_shape=(jax.ShapeDtypeStruct((count, 2, BLK...  3.65 us
  transfers between devices with their start and end apart: 15, of which 9 were waited for; matrix products, arithmetic and copies ran while one was open for 0% of the time, Pallas kernels for 25%

profile of v3, /device:TPU:0, one launch (start us, length us, event | category | flops | bytes accessed | tf_op | source)
XLA Modules:
  0.0 104.5 jit_solution(6872544995334851351)
XLA Ops:
  0.6 0.7 copy-done.4
  1.3 2.0 %pack.1.unit.refs_0_ = bf16[3168,128]{1,0:T(8,128)(2,1)S(1)} custom-call(bf16[1536,128]{1,0:T(8,128)(2,1)} %query.1, bf16[1536,128]{1,0:T(8,128)(2,1)} %grad.1, bf16[1536,128]{1,0:T(8,128)(2,1)} %output.1, f32[12,128]{1,0:T(8,128)S(1)} %bitcast.2), custom_call_target="tpu_custom_call" | custom-call | tf_op jit(solution)/shard_map/pack/pallas_call | solution.py:93
  3.3 0.0 copy-start.5
  3.3 5.8 %collective-permute-start = (bf16[3168,128]{1,0:T(8,128)(2,1)S(1)}, bf16[3168,128]{1,0:T(8,128)(2,1)}, u32[]{:S(2)}, u32[]{:S(2)}) collective-permute-start(bf16[3168,128]{1,0:T(8,128)(2,1)S(1)} %pack.1.unit.refs_0_), channel_id=1, source_target_pairs={{0,4},{1,5},{2,6},{3,7},{4,8},{5,9},{6,10},{7,11},{8,12},{9,13},{1... | collective-permute-start | bytes 2433032 | tf_op jit(solution)/shard_map/ppermute | solution.py:582
  9.2 1.3 %collective-permute-start.1 = (bf16[3168,128]{1,0:T(8,128)(2,1)S(1)}, bf16[3168,128]{1,0:T(8,128)(2,1)}, u32[]{:S(2)}, u32[]{:S(2)}) collective-permute-start(bf16[3168,128]{1,0:T(8,128)(2,1)S(1)} %pack.1.unit.refs_0_), channel_id=1, source_target_pairs={{4,0},{5,1},{6,2},{7,3},{8,4},{9,5},{10,6},{11,7},{12,8},{13,9},{1... | collective-permute-start | bytes 2433032 | tf_op jit(solution)/shard_map/ppermute | solution.py:582
  10.5 1.1 %join.1.keyval.refs_1_ = bf16[3072,128]{1,0:T(8,128)(2,1)S(1)} custom-call(bf16[1536,128]{1,0:T(8,128)(2,1)} %key.1, bf16[1536,128]{1,0:T(8,128)(2,1)} %value.1), custom_call_target="tpu_custom_call" | custom-call | tf_op jit(solution)/shard_map/join/pallas_call | solution.py:123
  11.6 1.6 %collective-permute-start.5 = (bf16[3072,128]{1,0:T(8,128)(2,1)S(1)}, bf16[3072,128]{1,0:T(8,128)(2,1)}, u32[]{:S(2)}, u32[]{:S(2)}) collective-permute-start(bf16[3072,128]{1,0:T(8,128)(2,1)S(1)} %join.1.keyval.refs_1_), channel_id=1, source_target_pairs={{0,2},{1,3},{2,0},{3,1},{4,6},{5,7},{6,4},{7,5},{8,10},{9,11},{10,... | collective-permute-start | bytes 2359304 | tf_op jit(solution)/shard_map/ppermute | solution.py:582
  13.2 3.7 %own.1 = (f32[12,2,128,128]{3,2,1,0:T(8,128)S(1)}, f32[12,128,128]{2,1,0:T(8,128)S(1)}) custom-call(bf16[3168,128]{1,0:T(8,128)(2,1)S(1)} %pack.1.unit.refs_0_, bf16[3072,128]{1,0:T(8,128)(2,1)S(1)} %join.1.keyval.refs_1_), custom_call_target="tpu_custom_call" | custom-call | tf_op jit(solution)/shard_map/own/pallas_call | solution.py:448
  16.8 1.2 %copy-done = f32[12,2,128,128]{3,2,1,0:T(8,128)} copy-done((f32[12,2,128,128]{3,2,1,0:T(8,128)}, f32[12,2,128,128]{3,2,1,0:T(8,128)S(1)}, u32[]{:S(2)}) %copy-start) | copy-done | bytes 1572888
  18.0 0.9 copy-done.2
  18.9 6.7 %collective-permute-done.refs_0_ = bf16[3168,128]{1,0:T(8,128)(2,1)} collective-permute-done((bf16[3168,128]{1,0:T(8,128)(2,1)S(1)}, bf16[3168,128]{1,0:T(8,128)(2,1)}, u32[]{:S(2)}, u32[]{:S(2)}) %collective-permute-start) | collective-permute-done | bytes 811040 | tf_op jit(solution)/shard_map/ppermute | solution.py:582
  25.6 5.1 %collective-permute-done.1.refs_1_ = bf16[3168,128]{1,0:T(8,128)(2,1)} collective-permute-done((bf16[3168,128]{1,0:T(8,128)(2,1)S(1)}, bf16[3168,128]{1,0:T(8,128)(2,1)}, u32[]{:S(2)}, u32[]{:S(2)}) %collective-permute-start.1) | collective-permute-done | bytes 811040 | tf_op jit(solution)/shard_map/ppermute | solution.py:582
  30.7 0.7 collective-permute-start.2
  31.4 1.3 %collective-permute-start.3 = (bf16[3168,128]{1,0:T(8,128)(2,1)}, bf16[3168,128]{1,0:T(8,128)(2,1)S(1)}, u32[]{:S(2)}, u32[]{:S(2)}) collective-permute-start(bf16[3168,128]{1,0:T(8,128)(2,1)} %collective-permute-done.1.refs_1_), channel_id=1, source_target_pairs={{4,0},{5,1},{6,2},{7,3},{8,4},{9,5},{10,6},{11,7},{20,16},{21,17},... | collective-permute-start | bytes 2433032 | tf_op jit(solution)/shard_map/ppermute | solution.py:582
  32.7 0.1 collective-permute-start.4
  32.8 0.0 collective-permute-done.5.refs_3_
  32.8 0.5 collective-permute-start.6
  33.3 0.1 copy.13
  33.4 0.2 reshape.12.layout
  33.6 0.1 pad_add_fusion.me_ref
  33.7 1.7 %collective-permute-done.4.refs_2_ = bf16[3072,128]{1,0:T(8,128)(2,1)} collective-permute-done((bf16[3072,128]{1,0:T(8,128)(2,1)S(1)}, bf16[3072,128]{1,0:T(8,128)(2,1)}, u32[]{:S(2)}, u32[]{:S(2)}) %collective-permute-start.4) | collective-permute-done | bytes 786464 | tf_op jit(solution)/shard_map/ppermute | solution.py:582
  35.4 1.1 %collective-permute-done.6.refs_4_ = bf16[3072,128]{1,0:T(8,128)(2,1)} collective-permute-done((bf16[3072,128]{1,0:T(8,128)(2,1)}, bf16[3072,128]{1,0:T(8,128)(2,1)}, u32[]{:S(2)}, u32[]{:S(2)}) %collective-permute-start.6) | collective-permute-done | bytes 786464 | tf_op jit(solution)/shard_map/ppermute | solution.py:582
  36.5 1.4 %copy-done.1 = f32[12,2,128,128]{3,2,1,0:T(8,128)S(1)} copy-done((f32[12,2,128,128]{3,2,1,0:T(8,128)S(1)}, f32[12,2,128,128]{3,2,1,0:T(8,128)}, u32[]{:S(2)}) %copy-start.1) | copy-done | bytes 1572888
  37.9 1.1 %copy-done.3 = f32[12,128,128]{2,1,0:T(8,128)S(1)} copy-done((f32[12,128,128]{2,1,0:T(8,128)S(1)}, f32[12,128,128]{2,1,0:T(8,128)}, u32[]{:S(2)}) %copy-start.3) | copy-done | bytes 786456
  39.1 6.1 %visit.4 = (bf16[6144,128]{1,0:T(8,128)(2,1)S(1)}, bf16[6144,128]{1,0:T(8,128)(2,1)S(1)}, f32[48,2,128,128]{3,2,1,0:T(8,128)S(1)}, f32[12,128,128]{2,1,0:T(8,128)S(1)}) custom-call(s32[2]{0:T(128)S(1)} %pad_add_fusion.me_ref, s32[576]{0:T(1024)S(1)} %reshape.12.layout, bf16[3168,128]{1,0:T(8,128)(2,1)S(1)} %pack.1.unit.refs_0_, ...), custom_call_target="tpu_custom_call" | custom-call | tf_op jit(solution)/shard_map/visit/pallas_call | solution.py:544
  45.2 8.4 %collective-permute-done.3.refs_1_ = bf16[3168,128]{1,0:T(8,128)(2,1)S(1)} collective-permute-done((bf16[3168,128]{1,0:T(8,128)(2,1)}, bf16[3168,128]{1,0:T(8,128)(2,1)S(1)}, u32[]{:S(2)}, u32[]{:S(2)}) %collective-permute-start.3) | collective-permute-done | bytes 811040 | tf_op jit(solution)/shard_map/ppermute | solution.py:582
  53.6 0.1 broadcast_select_fusion
  53.7 1.3 %collective-permute-start.7 = (bf16[3168,128]{1,0:T(8,128)(2,1)S(1)}, bf16[3168,128]{1,0:T(8,128)(2,1)S(1)}, u32[]{:S(2)}, u32[]{:S(2)}) collective-permute-start(bf16[3168,128]{1,0:T(8,128)(2,1)S(1)} %broadcast_select_fusion), channel_id=1, source_target_pairs={{8,12},{9,13},{10,14},{11,15},{4,0},{5,1},{6,2},{7,3},{24,28},{25,... | collective-permute-start | bytes 2433032 | tf_op jit(solution)/shard_map/ppermute | solution.py:582
  55.0 5.2 %visit.5 = (f32[48,2,128,128]{3,2,1,0:T(8,128)S(1)}, bf16[12,128,128]{2,1,0:T(8,128)(2,1)S(1)}, bf16[12,128,128]{2,1,0:T(8,128)(2,1)S(1)}) custom-call(s32[2]{0:T(128)S(1)} %pad_add_fusion.me_ref, s32[576]{0:T(1024)S(1)} %reshape.12.layout, bf16[3168,128]{1,0:T(8,128)(2,1)} %collective-permute-done.refs_0_, ...), custom_call_target="tpu_custom_call", output_to_operand_aliasing={{0}: (6, {})} | custom-call | tf_op jit(solution)/shard_map/visit/pallas_call | solution.py:544
  60.2 3.9 %visit.6 = (f32[48,2,128,128]{3,2,1,0:T(8,128)S(1)}, bf16[12,128,128]{2,1,0:T(8,128)(2,1)S(1)}, bf16[12,128,128]{2,1,0:T(8,128)(2,1)S(1)}) custom-call(s32[2]{0:T(128)S(1)} %pad_add_fusion.me_ref, s32[576]{0:T(1024)S(1)} %reshape.12.layout, bf16[3168,128]{1,0:T(8,128)(2,1)S(1)} %collective-permute-done.2.refs_0_, ...), custom_call_target="tpu_custom_call", output_to_operand_aliasing={{0}: (6, {})} | custom-call | tf_op jit(solution)/shard_map/visit/pallas_call | solution.py:544
  64.1 0.7 collective-permute-start.8
  64.8 3.7 %collective-permute-start.9 = (bf16[12,128,128]{2,1,0:T(8,128)(2,1)S(1)}, bf16[12,128,128]{2,1,0:T(8,128)(2,1)S(1)}, u32[]{:S(2)}, u32[]{:S(2)}) collective-permute-start(bf16[12,128,128]{2,1,0:T(8,128)(2,1)S(1)} %get-tuple-element.50), channel_id=1, source_target_pairs={{0,4},{1,5},{2,6},{3,7},{4,8},{5,9},{6,10},{7,11},{16,20},{17,21},... | collective-permute-start | bytes 1179656 | tf_op jit(solution)/shard_map/ppermute | solution.py:582
  68.5 4.8 %collective-permute-done.7.refs_0_ = bf16[3168,128]{1,0:T(8,128)(2,1)S(1)} collective-permute-done((bf16[3168,128]{1,0:T(8,128)(2,1)S(1)}, bf16[3168,128]{1,0:T(8,128)(2,1)S(1)}, u32[]{:S(2)}, u32[]{:S(2)}) %collective-permute-start.7) | collective-permute-done | bytes 811040 | tf_op jit(solution)/shard_map/ppermute | solution.py:582
  73.3 3.9 %visit.7 = (f32[48,2,128,128]{3,2,1,0:T(8,128)S(1)}, bf16[12,128,128]{2,1,0:T(8,128)(2,1)S(1)}) custom-call(s32[2]{0:T(128)S(1)} %pad_add_fusion.me_ref, s32[576]{0:T(1024)S(1)} %reshape.12.layout, bf16[3168,128]{1,0:T(8,128)(2,1)S(1)} %collective-permute-done.7.refs_0_, ...), custom_call_target="tpu_custom_call", output_to_operand_aliasing={{0}: (5, {})} | custom-call | flops 5033164800 | tf_op jit(solution)/shard_map/visit/pallas_call | solution.py:544
  77.2 0.3 add_convert_fusion
  77.5 0.8 share.2
  78.3 0.1 collective-permute-start.10
  78.4 1.9 %collective-permute-start.12 = (bf16[12,128,128]{2,1,0:T(8,128)(2,1)S(1)}, bf16[12,128,128]{2,1,0:T(8,128)(2,1)S(1)}, u32[]{:S(2)}, u32[]{:S(2)}) collective-permute-start(bf16[12,128,128]{2,1,0:T(8,128)(2,1)S(1)} %get-tuple-element.57), channel_id=1, source_target_pairs={{12,0},{13,1},{14,2},{15,3},{0,12},{1,13},{2,14},{3,15},{28,16},{2... | collective-permute-start | bytes 1179656 | tf_op jit(solution)/shard_map/ppermute | solution.py:582
  80.3 1.5 %collective-permute-done.10.refs_0_ = bf16[2,2,12,128,128]{4,3,2,1,0:T(8,128)(2,1)S(1)} collective-permute-done((bf16[2,2,12,128,128]{4,3,2,1,0:T(8,128)(2,1)S(1)}, bf16[2,2,12,128,128]{4,3,2,1,0:T(8,128)(2,1)S(1)}, u32[]{:S(2)}, u32[]{:S(2)}) %collective-permute-start.10) | collective-permute-done | bytes 1572896 | tf_op jit(solution)/shard_map/ppermute | solution.py:582
  81.8 0.8 share.3
  82.5 2.0 %collective-permute-start.11 = (bf16[2,1,12,128,128]{4,3,2,1,0:T(8,128)(2,1)S(1)}, bf16[2,1,12,128,128]{4,3,2,1,0:T(8,128)(2,1)S(1)}, u32[]{:S(2)}, u32[]{:S(2)}) collective-permute-start(bf16[2,1,12,128,128]{4,3,2,1,0:T(8,128)(2,1)S(1)} %share.3), channel_id=1, source_target_pairs={{0,2},{1,3},{2,0},{3,1},{4,6},{5,7},{6,4},{7,5},{8,10},{9,11},{10,... | collective-permute-start | bytes 2359304 | tf_op jit(solution)/shard_map/ppermute | solution.py:582
  84.5 1.3 %collective-permute-start.13 = (bf16[12,128,128]{2,1,0:T(8,128)(2,1)S(1)}, bf16[12,128,128]{2,1,0:T(8,128)(2,1)S(1)}, u32[]{:S(2)}, u32[]{:S(2)}) collective-permute-start(bf16[12,128,128]{2,1,0:T(8,128)(2,1)S(1)} %get-tuple-element.58), channel_id=1, source_target_pairs={{4,0},{5,1},{6,2},{7,3},{8,4},{9,5},{10,6},{11,7},{12,8},{13,9},{1... | collective-permute-start | bytes 1179656 | tf_op jit(solution)/shard_map/ppermute | solution.py:582
  85.8 4.6 %collective-permute-start.14 = (bf16[12,128,128]{2,1,0:T(8,128)(2,1)S(1)}, bf16[12,128,128]{2,1,0:T(8,128)(2,1)S(1)}, u32[]{:S(2)}, u32[]{:S(2)}) collective-permute-start(bf16[12,128,128]{2,1,0:T(8,128)(2,1)S(1)} %get-tuple-element.59), channel_id=1, source_target_pairs={{0,4},{1,5},{2,6},{3,7},{4,8},{5,9},{6,10},{7,11},{8,12},{9,13},{1... | collective-permute-start | bytes 1179656 | tf_op jit(solution)/shard_map/ppermute | solution.py:582
  90.4 3.6 %collective-permute-done.12.refs_0_ = bf16[12,128,128]{2,1,0:T(8,128)(2,1)S(1)} collective-permute-done((bf16[12,128,128]{2,1,0:T(8,128)(2,1)S(1)}, bf16[12,128,128]{2,1,0:T(8,128)(2,1)S(1)}, u32[]{:S(2)}, u32[]{:S(2)}) %collective-permute-start.12) | collective-permute-done | bytes 393248 | tf_op jit(solution)/shard_map/ppermute | solution.py:582
  94.0 0.1 add.14.base
  94.1 7.9 %collective-permute-done.13.refs_0_ = bf16[12,128,128]{2,1,0:T(8,128)(2,1)S(1)} collective-permute-done((bf16[12,128,128]{2,1,0:T(8,128)(2,1)S(1)}, bf16[12,128,128]{2,1,0:T(8,128)(2,1)S(1)}, u32[]{:S(2)}, u32[]{:S(2)}) %collective-permute-start.13) | collective-permute-done | bytes 393248 | tf_op jit(solution)/shard_map/ppermute | solution.py:582
  102.0 0.9 add.15
  102.9 1.6 %finish.1 = (bf16[1536,128]{1,0:T(8,128)(2,1)}, bf16[1536,128]{1,0:T(8,128)(2,1)}) custom-call(s32[2]{0:T(128)S(1)} %pad_add_fusion.me_ref, f32[48,2,128,128]{3,2,1,0:T(8,128)S(1)} %get-tuple-element.55.acc, bf16[2,2,12,128,128]{4,3,2,1,0:T(8,128)(2,1)S(1)} %collective-permute-done.10.refs_0_, bf16[2,1,12,128,128]{4,3,2,1,0:T(8,128)(2,1)S(1)} %collective-permute-done.11.refs_1_), custom_call_target="tpu_custom_call" | custom-call | tf_op jit(solution)/shard_map/finish/pallas_call | solution.py:477
  (11 shorter events, 0.0 us)
Async XLA Ops:
  0.6 0.7 copy-start.4
  3.3 30.0 %copy-start.5 = (s32[192,3]{0,1:T(4,128)S(1)}, s32[192,3]{0,1:T(4,128)}, u32[]{:S(2)}) copy-start(s32[192,3]{0,1:T(4,128)} %param.13) | copy-start | bytes 6916
  3.3 22.2 %collective-permute-start = (bf16[3168,128]{1,0:T(8,128)(2,1)S(1)}, bf16[3168,128]{1,0:T(8,128)(2,1)}, u32[]{:S(2)}, u32[]{:S(2)}) collective-permute-start(bf16[3168,128]{1,0:T(8,128)(2,1)S(1)} %pack.1.unit.refs_0_), channel_id=1, source_target_pairs={{0,4},{1,5},{2,6},{3,7},{4,8},{5,9},{6,10},{7,11},{8,12},{9,13},{1... | collective-permute-start | bytes 2433032 | tf_op jit(solution)/shard_map/ppermute | solution.py:582
  9.2 21.5 %collective-permute-start.1 = (bf16[3168,128]{1,0:T(8,128)(2,1)S(1)}, bf16[3168,128]{1,0:T(8,128)(2,1)}, u32[]{:S(2)}, u32[]{:S(2)}) collective-permute-start(bf16[3168,128]{1,0:T(8,128)(2,1)S(1)} %pack.1.unit.refs_0_), channel_id=1, source_target_pairs={{4,0},{5,1},{6,2},{7,3},{8,4},{9,5},{10,6},{11,7},{12,8},{13,9},{1... | collective-permute-start | bytes 2433032 | tf_op jit(solution)/shard_map/ppermute | solution.py:582
  11.6 21.2 %collective-permute-start.5 = (bf16[3072,128]{1,0:T(8,128)(2,1)S(1)}, bf16[3072,128]{1,0:T(8,128)(2,1)}, u32[]{:S(2)}, u32[]{:S(2)}) collective-permute-start(bf16[3072,128]{1,0:T(8,128)(2,1)S(1)} %join.1.keyval.refs_1_), channel_id=1, source_target_pairs={{0,2},{1,3},{2,0},{3,1},{4,6},{5,7},{6,4},{7,5},{8,10},{9,11},{10,... | collective-permute-start | bytes 2359304 | tf_op jit(solution)/shard_map/ppermute | solution.py:582
  16.8 1.2 %copy-start = (f32[12,2,128,128]{3,2,1,0:T(8,128)}, f32[12,2,128,128]{3,2,1,0:T(8,128)S(1)}, u32[]{:S(2)}) copy-start(f32[12,2,128,128]{3,2,1,0:T(8,128)S(1)} %get-tuple-element.37.refs_5_) | copy-start | bytes 4718596
  18.0 0.9 copy-start.2
  30.7 14.5 %collective-permute-start.2 = (bf16[3168,128]{1,0:T(8,128)(2,1)}, bf16[3168,128]{1,0:T(8,128)(2,1)S(1)}, u32[]{:S(2)}, u32[]{:S(2)}) collective-permute-start(bf16[3168,128]{1,0:T(8,128)(2,1)} %collective-permute-done.refs_0_), channel_id=1, source_target_pairs={{4,8},{5,9},{6,10},{7,11},{8,12},{9,13},{10,14},{11,15},{20,24},{2... | collective-permute-start | bytes 2433032 | tf_op jit(solution)/shard_map/ppermute | solution.py:582
  31.4 22.2 %collective-permute-start.3 = (bf16[3168,128]{1,0:T(8,128)(2,1)}, bf16[3168,128]{1,0:T(8,128)(2,1)S(1)}, u32[]{:S(2)}, u32[]{:S(2)}) collective-permute-start(bf16[3168,128]{1,0:T(8,128)(2,1)} %collective-permute-done.1.refs_1_), channel_id=1, source_target_pairs={{4,0},{5,1},{6,2},{7,3},{8,4},{9,5},{10,6},{11,7},{20,16},{21,17},... | collective-permute-start | bytes 2433032 | tf_op jit(solution)/shard_map/ppermute | solution.py:582
  32.7 2.7 %collective-permute-start.4 = (bf16[3072,128]{1,0:T(8,128)(2,1)S(1)}, bf16[3072,128]{1,0:T(8,128)(2,1)}, u32[]{:S(2)}, u32[]{:S(2)}) collective-permute-start(bf16[3072,128]{1,0:T(8,128)(2,1)S(1)} %join.1.keyval.refs_1_), channel_id=1, source_target_pairs={{0,1},{1,0},{2,3},{3,2},{4,5},{5,4},{6,7},{7,6},{8,9},{9,8},{10,11... | collective-permute-start | bytes 2359304 | tf_op jit(solution)/shard_map/ppermute | solution.py:582
  32.8 3.7 %collective-permute-start.6 = (bf16[3072,128]{1,0:T(8,128)(2,1)}, bf16[3072,128]{1,0:T(8,128)(2,1)}, u32[]{:S(2)}, u32[]{:S(2)}) collective-permute-start(bf16[3072,128]{1,0:T(8,128)(2,1)} %collective-permute-done.5.refs_3_), channel_id=1, source_target_pairs={{0,1},{1,0},{2,3},{3,2},{4,5},{5,4},{6,7},{7,6},{8,9},{9,8},{10,11... | collective-permute-start | bytes 2359304 | tf_op jit(solution)/shard_map/ppermute | solution.py:582
  36.5 1.4 %copy-start.1 = (f32[12,2,128,128]{3,2,1,0:T(8,128)S(1)}, f32[12,2,128,128]{3,2,1,0:T(8,128)}, u32[]{:S(2)}) copy-start(f32[12,2,128,128]{3,2,1,0:T(8,128)} %copy-done) | copy-start | bytes 4718596
  37.9 1.1 %copy-start.3 = (f32[12,128,128]{2,1,0:T(8,128)S(1)}, f32[12,128,128]{2,1,0:T(8,128)}, u32[]{:S(2)}) copy-start(f32[12,128,128]{2,1,0:T(8,128)} %copy-done.2) | copy-start | bytes 2359300
  53.7 19.6 %collective-permute-start.7 = (bf16[3168,128]{1,0:T(8,128)(2,1)S(1)}, bf16[3168,128]{1,0:T(8,128)(2,1)S(1)}, u32[]{:S(2)}, u32[]{:S(2)}) collective-permute-start(bf16[3168,128]{1,0:T(8,128)(2,1)S(1)} %broadcast_select_fusion), channel_id=1, source_target_pairs={{8,12},{9,13},{10,14},{11,15},{4,0},{5,1},{6,2},{7,3},{24,28},{25,... | collective-permute-start | bytes 2433032 | tf_op jit(solution)/shard_map/ppermute | solution.py:582
  64.1 13.1 %collective-permute-start.8 = (bf16[12,128,128]{2,1,0:T(8,128)(2,1)S(1)}, bf16[12,128,128]{2,1,0:T(8,128)(2,1)S(1)}, u32[]{:S(2)}, u32[]{:S(2)}) collective-permute-start(bf16[12,128,128]{2,1,0:T(8,128)(2,1)S(1)} %get-tuple-element.49), channel_id=1, source_target_pairs={{8,4},{9,5},{10,6},{11,7},{12,8},{13,9},{14,10},{15,11},{24,20},{2... | collective-permute-start | bytes 1179656 | tf_op jit(solution)/shard_map/ppermute | solution.py:582
  64.8 12.4 %collective-permute-start.9 = (bf16[12,128,128]{2,1,0:T(8,128)(2,1)S(1)}, bf16[12,128,128]{2,1,0:T(8,128)(2,1)S(1)}, u32[]{:S(2)}, u32[]{:S(2)}) collective-permute-start(bf16[12,128,128]{2,1,0:T(8,128)(2,1)S(1)} %get-tuple-element.50), channel_id=1, source_target_pairs={{0,4},{1,5},{2,6},{3,7},{4,8},{5,9},{6,10},{7,11},{16,20},{17,21},... | collective-permute-start | bytes 1179656 | tf_op jit(solution)/shard_map/ppermute | solution.py:582
  78.3 3.5 %collective-permute-start.10 = (bf16[2,2,12,128,128]{4,3,2,1,0:T(8,128)(2,1)S(1)}, bf16[2,2,12,128,128]{4,3,2,1,0:T(8,128)(2,1)S(1)}, u32[]{:S(2)}, u32[]{:S(2)}) collective-permute-start(bf16[2,2,12,128,128]{4,3,2,1,0:T(8,128)(2,1)S(1)} %share.2), channel_id=1, source_target_pairs={{0,1},{1,0},{2,3},{3,2},{4,5},{5,4},{6,7},{7,6},{8,9},{9,8},{10,11... | collective-permute-start | bytes 4718600 | tf_op jit(solution)/shard_map/ppermute | solution.py:582
  78.4 15.6 %collective-permute-start.12 = (bf16[12,128,128]{2,1,0:T(8,128)(2,1)S(1)}, bf16[12,128,128]{2,1,0:T(8,128)(2,1)S(1)}, u32[]{:S(2)}, u32[]{:S(2)}) collective-permute-start(bf16[12,128,128]{2,1,0:T(8,128)(2,1)S(1)} %get-tuple-element.57), channel_id=1, source_target_pairs={{12,0},{13,1},{14,2},{15,3},{0,12},{1,13},{2,14},{3,15},{28,16},{2... | collective-permute-start | bytes 1179656 | tf_op jit(solution)/shard_map/ppermute | solution.py:582
  82.5 20.4 %collective-permute-start.11 = (bf16[2,1,12,128,128]{4,3,2,1,0:T(8,128)(2,1)S(1)}, bf16[2,1,12,128,128]{4,3,2,1,0:T(8,128)(2,1)S(1)}, u32[]{:S(2)}, u32[]{:S(2)}) collective-permute-start(bf16[2,1,12,128,128]{4,3,2,1,0:T(8,128)(2,1)S(1)} %share.3), channel_id=1, source_target_pairs={{0,2},{1,3},{2,0},{3,1},{4,6},{5,7},{6,4},{7,5},{8,10},{9,11},{10,... | collective-permute-start | bytes 2359304 | tf_op jit(solution)/shard_map/ppermute | solution.py:582
  84.5 17.5 %collective-permute-start.13 = (bf16[12,128,128]{2,1,0:T(8,128)(2,1)S(1)}, bf16[12,128,128]{2,1,0:T(8,128)(2,1)S(1)}, u32[]{:S(2)}, u32[]{:S(2)}) collective-permute-start(bf16[12,128,128]{2,1,0:T(8,128)(2,1)S(1)} %get-tuple-element.58), channel_id=1, source_target_pairs={{4,0},{5,1},{6,2},{7,3},{8,4},{9,5},{10,6},{11,7},{12,8},{13,9},{1... | collective-permute-start | bytes 1179656 | tf_op jit(solution)/shard_map/ppermute | solution.py:582
  85.8 16.2 %collective-permute-start.14 = (bf16[12,128,128]{2,1,0:T(8,128)(2,1)S(1)}, bf16[12,128,128]{2,1,0:T(8,128)(2,1)S(1)}, u32[]{:S(2)}, u32[]{:S(2)}) collective-permute-start(bf16[12,128,128]{2,1,0:T(8,128)(2,1)S(1)} %get-tuple-element.59), channel_id=1, source_target_pairs={{0,4},{1,5},{2,6},{3,7},{4,8},{5,9},{6,10},{7,11},{8,12},{9,13},{1... | collective-permute-start | bytes 1179656 | tf_op jit(solution)/shard_map/ppermute | solution.py:582

commit v4 on v3

--- a/solution.py
+++ b/solution.py
@@ -10,7 +10,7 @@
 BLK = 128
 GLOB = 2
 TILE = 16
-PAIRS = 3
+PAIRS = 6
 TURNS = 3
 FAR = 1e30
 COST = 20
@@ -333,6 +333,7 @@
     seat = lax.rem(me, span)
     row = lax.div(me, span)
     low = row * span * count
+    side = 1 - 2 * lax.rem(row, 2)
     if first:
         parts = [refs.pop(0) for _ in range(span)]
         acc_own, dq_own = (refs.pop(0), refs.pop(0))
@@ -365,12 +366,8 @@
         lax.fori_loop(0, count, lay, 0)
 
     for v, offset in enumerate(offsets):
-        if offset is None:
-            guest = jnp.where(row == 0, me + shards - span, me + span - shards)
-            present = (row == 0) | (me + span >= shards)
-        else:
-            guest = me + offset * span
-            present = (guest >= 0) & (guest < shards)
+        guest = me + offset * span * side
+        present = (guest >= 0) & (guest < shards)
         visitor = Visitor(count, guests[v], lse, delta, sums[v], keys, values, acc, layout, lists)
 
         @pl.when(present)
@@ -584,15 +581,16 @@
     def swap(array, bit):
         return send(array, [(i, i ^ bit) for i in range(shards)])
 
-    def shift(array, planes_away, low, high):
-        return send(
-            array,
-            [
-                (p * span + e, (p + planes_away) * span + e)
-                for p in range(low, high)
-                for e in range(span)
-            ],
-        )
+    def hop(s, odd, back=False):
+        pairs = []
+        for p in range(odd, planes - 1, 2):
+            if p >= s - 1:
+                pairs.append((p, p + 1))
+            if p + 1 <= planes - s:
+                pairs.append((p + 1, p))
+        if back:
+            pairs = [(q, p) for p, q in pairs]
+        return [(p * span + e, q * span + e) for p, q in pairs for e in range(span)]
 
     me = jnp.stack([myself, jnp.int32(shards)]).astype(jnp.int32)
     entries = layout.reshape(-1)
@@ -606,13 +604,13 @@
         return lax.optimization_barrier(arrays)
 
     last = planes - 1
-    up, down = (shift(unit, 1, 0, last), shift(unit, -1, 1, planes))
+    odd, even = (send(unit, hop(1, 1)), send(unit, hop(1, 0)))
     keyvals = {0: keyval}
     singles = [m for m in range(1, span) if m & (m - 1) == 0]
     for m in singles:
         keyvals[m] = swap(keyval, m)
     acc, query_acc = own_visit(unit, keyval, count)
-    up, down, query_acc = tie(up, down, query_acc)
+    even, query_acc = tie(even, query_acc)
     for m in range(1, span):
         if m & (m - 1):
             keyvals[m] = swap(keyvals[m & (m - 1)], m & -m)
@@ -624,37 +622,37 @@
         )
 
     keys, values, acc, query_acc = meet([unit], (0,), keyvals, acc, query_acc)
-    above = myself >= shards // 2
-    inward = [(p * span + e, q * span + e) for p, q in ((last - 1, last), (1, 0)) for e in range(span)]
     ends = [(last * span + e, e) for e in range(span)]
     ends = ends + [(two, one) for one, two in ends]
-    up_parts, down_parts = ([], [])
+    even_parts, odd_parts = ([], [])
     for s in range(1, last):
         if s + 1 < last:
-            next_up, next_down = (shift(up, 1, s, last), shift(down, -1, 1, planes - s))
+            next_even, next_odd = (send(odd, hop(s + 1, 0)), send(even, hop(s + 1, 1)))
         else:
-            up, down, query_acc = tie(up, down, query_acc)
-            far = send(jnp.where(above, up, down), inward)
-        acc, up_part, down_part = meet([up, down], (-s, s), [keys, values], acc)
-        up_parts.append(up_part)
-        down_parts.append(down_part)
+            odd, query_acc = tie(odd, query_acc)
+            far = send(odd, hop(last, 0))
+        if s + 2 == last:
+            acc, next_even = tie(acc, next_even)
+        acc, even_part, odd_part = meet([even, odd], (s, -s), [keys, values], acc)
+        even_parts.append(even_part)
+        odd_parts.append(odd_part)
         if s + 1 < last:
-            up, down = (next_up, next_down)
-
-    acc, far_part = meet([far], (None,), [keys, values], acc, None, COST)
-
-    up_back, down_back = (up_parts[-1], down_parts[-1])
+            even, odd = (next_even, next_odd)
+    acc, far_part = meet([far], (last,), [keys, values], acc, None, COST)
+
+    even_back, odd_back = (even_parts[-1], odd_parts[-1])
     for t in range(last - 1, 1, -1):
-        up_back, down_back = (shift(up_back, -1, t, planes), shift(down_back, 1, 0, planes - t))
+        even_back, odd_back = (send(even_back, hop(t, 0, True)), send(odd_back, hop(t, 1, True)))
         if t == 2:
-            up_back, down_back, far_part = tie(up_back, down_back, far_part)
-        up_back = merge(up_parts[t - 2], up_back)
-        down_back = merge(down_parts[t - 2], down_back)
-    acc, up_back, down_back = tie(acc, up_back, down_back)
-    query_acc = add(query_acc, [send(far_part, ends)], False, COST)
-    query_grad = add(
-        query_acc, [shift(up_back, -1, 1, planes), shift(down_back, 1, 0, planes - 1)], True, 1
-    )
+            even_back, odd_back, far_part = tie(even_back, odd_back, far_part)
+        even_back, odd_back = (
+            merge(even_parts[t - 2], odd_back),
+            merge(odd_parts[t - 2], even_back),
+        )
+    acc, even_back, odd_back = tie(acc, even_back, odd_back)
+    backs = [send(even_back, hop(1, 0, True)), send(odd_back, hop(1, 1, True))]
+    query_acc = add(query_acc, backs, False, COST)
+    query_grad = add(query_acc, [send(far_part, ends)], True, 1)
 
     wanted = tuple(range(span))
     arrived, parts = ((), ())

time: 105 us -> 98.3 us (0.936)
  starting transfers between devices: 26.7 us -> 17.6 us
  waiting for transfers between devices: 40.9 us -> 46.7 us
  local copies, waits for them, and re-layouts: 5.62 us -> 3.05 us
    ppermute x15, starting transfers between devices: 26.7 us -> 17.6 us  [send(): return lax.ppermute(array, 'qb', pairs)]
    ppermute x15, waiting for transfers between devices: 40.9 us -> 46.7 us  [send(): return lax.ppermute(array, 'qb', pairs)]
    unnamed x13 -> x9, local copies, waits for them, and re-layouts: 5.42 us -> 2.84 us
  transfers between devices with their start and end apart: 15 -> 15, of which waited for: 9 -> 10; matrix products, arithmetic and copies ran while one was open for 0% -> 0% of each run, Pallas kernels for 25% -> 26%
where the time goes in v4:
time: 98.3 us; the launch traced here: 97.8 us
  waiting for transfers between devices  46.7 us (48%)
  Pallas kernels  29.3 us (30%)
  starting transfers between devices  17.6 us (18%)
  local copies, waits for them, and re-layouts  3.05 us (3%)
    ppermute x15, waiting for transfers between devices, send(): return lax.ppermute(array, 'qb', pairs)  46.7 us
    pallas_call x4, Pallas kernels, visit(): pl.pallas_call(functools.partial(visit_kernel, plan), out_shape=outs, in_...  18.4 us
    ppermute x15, starting transfers between devices, send(): return lax.ppermute(array, 'qb', pairs)  17.6 us
    pallas_call x1, Pallas kernels, own_visit(): pl.pallas_call(own_kernel, out_shape=(jax.ShapeDtypeStruct((count, 2, BLK...  3.67 us
    unnamed x9, local copies, waits for them, and re-layouts  2.84 us
    pallas_call x1, Pallas kernels, pack(): pl.pallas_call(pack_kernel, out_shape=jax.ShapeDtypeStruct((2 * count * B...  1.97 us
  transfers between devices with their start and end apart: 15, of which 10 were waited for; matrix products, arithmetic and copies ran while one was open for 0% of the time, Pallas kernels for 26%

profile of v4, /device:TPU:0, one launch (start us, length us, event | category | flops | bytes accessed | tf_op | source)
XLA Modules:
  0.0 97.8 jit_solution(9560769631886823169)
XLA Ops:
  0.6 0.7 copy-done.2
  1.3 2.0 %pack.1.unit.refs_0_ = bf16[3168,128]{1,0:T(8,128)(2,1)S(1)} custom-call(bf16[1536,128]{1,0:T(8,128)(2,1)} %query.1, bf16[1536,128]{1,0:T(8,128)(2,1)} %grad.1, bf16[1536,128]{1,0:T(8,128)(2,1)} %output.1, f32[12,128]{1,0:T(8,128)S(1)} %bitcast.2), custom_call_target="tpu_custom_call" | custom-call | tf_op jit(solution)/shard_map/pack/pallas_call | solution.py:93
  3.3 0.0 copy-start.3
  3.3 3.1 %collective-permute-start = (bf16[3168,128]{1,0:T(8,128)(2,1)S(1)}, bf16[3168,128]{1,0:T(8,128)(2,1)}, u32[]{:S(2)}, u32[]{:S(2)}) collective-permute-start(bf16[3168,128]{1,0:T(8,128)(2,1)S(1)} %pack.1.unit.refs_0_), channel_id=1, source_target_pairs={{0,4},{1,5},{2,6},{3,7},{4,0},{5,1},{6,2},{7,3},{8,12},{9,13},{10,... | collective-permute-start | bytes 2433032 | tf_op jit(solution)/shard_map/ppermute | solution.py:579
  6.4 1.1 %join.1.keyval.refs_1_ = bf16[3072,128]{1,0:T(8,128)(2,1)S(1)} custom-call(bf16[1536,128]{1,0:T(8,128)(2,1)} %key.1, bf16[1536,128]{1,0:T(8,128)(2,1)} %value.1), custom_call_target="tpu_custom_call" | custom-call | tf_op jit(solution)/shard_map/join/pallas_call | solution.py:123
  7.5 1.6 %collective-permute-start.3 = (bf16[3072,128]{1,0:T(8,128)(2,1)S(1)}, bf16[3072,128]{1,0:T(8,128)(2,1)}, u32[]{:S(2)}, u32[]{:S(2)}) collective-permute-start(bf16[3072,128]{1,0:T(8,128)(2,1)S(1)} %join.1.keyval.refs_1_), channel_id=1, source_target_pairs={{0,2},{1,3},{2,0},{3,1},{4,6},{5,7},{6,4},{7,5},{8,10},{9,11},{10,... | collective-permute-start | bytes 2359304 | tf_op jit(solution)/shard_map/ppermute | solution.py:579
  9.1 1.6 %collective-permute-start.6 = (bf16[3168,128]{1,0:T(8,128)(2,1)S(1)}, bf16[3168,128]{1,0:T(8,128)(2,1)}, u32[]{:S(2)}, u32[]{:S(2)}) collective-permute-start(bf16[3168,128]{1,0:T(8,128)(2,1)S(1)} %pack.1.unit.refs_0_), channel_id=1, source_target_pairs={{4,8},{5,9},{6,10},{7,11},{8,4},{9,5},{10,6},{11,7},{20,24},{21,25... | collective-permute-start | bytes 2433032 | tf_op jit(solution)/shard_map/ppermute | solution.py:579
  10.7 3.7 %own.1 = (f32[12,2,128,128]{3,2,1,0:T(8,128)S(1)}, f32[12,128,128]{2,1,0:T(8,128)S(1)}) custom-call(bf16[3168,128]{1,0:T(8,128)(2,1)S(1)} %pack.1.unit.refs_0_, bf16[3072,128]{1,0:T(8,128)(2,1)S(1)} %join.1.keyval.refs_1_), custom_call_target="tpu_custom_call" | custom-call | tf_op jit(solution)/shard_map/own/pallas_call | solution.py:445
  14.4 0.9 copy-done
  15.3 9.3 %collective-permute-done.refs_0_ = bf16[3168,128]{1,0:T(8,128)(2,1)} collective-permute-done((bf16[3168,128]{1,0:T(8,128)(2,1)S(1)}, bf16[3168,128]{1,0:T(8,128)(2,1)}, u32[]{:S(2)}, u32[]{:S(2)}) %collective-permute-start) | collective-permute-done | bytes 811040 | tf_op jit(solution)/shard_map/ppermute | solution.py:579
  24.6 1.6 %collective-permute-start.1 = (bf16[3168,128]{1,0:T(8,128)(2,1)}, bf16[3168,128]{1,0:T(8,128)(2,1)}, u32[]{:S(2)}, u32[]{:S(2)}) collective-permute-start(bf16[3168,128]{1,0:T(8,128)(2,1)} %collective-permute-done.refs_0_), channel_id=1, source_target_pairs={{4,8},{5,9},{6,10},{7,11},{8,4},{9,5},{10,6},{11,7},{20,24},{21,25... | collective-permute-start | bytes 2433032 | tf_op jit(solution)/shard_map/ppermute | solution.py:579
  26.2 0.0 collective-permute-start.2
  26.2 0.6 collective-permute-done.3.refs_3_
  26.7 0.0 collective-permute-start.4
  26.7 0.0 collective-permute-done.6.refs_1_
  26.7 1.3 %collective-permute-start.7 = (bf16[3168,128]{1,0:T(8,128)(2,1)}, bf16[3168,128]{1,0:T(8,128)(2,1)}, u32[]{:S(2)}, u32[]{:S(2)}) collective-permute-start(bf16[3168,128]{1,0:T(8,128)(2,1)} %collective-permute-done.6.refs_1_), channel_id=1, source_target_pairs={{4,0},{5,1},{6,2},{7,3},{8,12},{9,13},{10,14},{11,15},{20,16},{21,... | collective-permute-start | bytes 2433032 | tf_op jit(solution)/shard_map/ppermute | solution.py:579
  28.0 0.1 pad_add_fusion.me_ref
  28.1 0.1 copy.13
  28.2 0.2 reshape.12.layout
  28.4 0.2 collective-permute-done.2.refs_2_
  28.6 1.3 %collective-permute-done.4.refs_4_ = bf16[3072,128]{1,0:T(8,128)(2,1)} collective-permute-done((bf16[3072,128]{1,0:T(8,128)(2,1)}, bf16[3072,128]{1,0:T(8,128)(2,1)}, u32[]{:S(2)}, u32[]{:S(2)}) %collective-permute-start.4) | collective-permute-done | bytes 786464 | tf_op jit(solution)/shard_map/ppermute | solution.py:579
  29.9 1.1 %copy-done.1 = f32[12,128,128]{2,1,0:T(8,128)S(1)} copy-done((f32[12,128,128]{2,1,0:T(8,128)S(1)}, f32[12,128,128]{2,1,0:T(8,128)}, u32[]{:S(2)}) %copy-start.1) | copy-done | bytes 786456
  31.0 5.5 %visit.4 = (bf16[6144,128]{1,0:T(8,128)(2,1)S(1)}, bf16[6144,128]{1,0:T(8,128)(2,1)S(1)}, f32[48,2,128,128]{3,2,1,0:T(8,128)S(1)}, f32[12,128,128]{2,1,0:T(8,128)S(1)}) custom-call(s32[2]{0:T(128)S(1)} %pad_add_fusion.me_ref, s32[576]{0:T(1024)S(1)} %reshape.12.layout, bf16[3168,128]{1,0:T(8,128)(2,1)S(1)} %pack.1.unit.refs_0_, ...), custom_call_target="tpu_custom_call" | custom-call | tf_op jit(solution)/shard_map/visit/pallas_call | solution.py:541
  36.6 0.0 collective-permute-done.1.refs_1_
  36.6 1.3 %collective-permute-start.5 = (bf16[3168,128]{1,0:T(8,128)(2,1)}, bf16[3168,128]{1,0:T(8,128)(2,1)S(1)}, u32[]{:S(2)}, u32[]{:S(2)}) collective-permute-start(bf16[3168,128]{1,0:T(8,128)(2,1)} %collective-permute-done.1.refs_1_), channel_id=1, source_target_pairs={{4,0},{5,1},{6,2},{7,3},{8,12},{9,13},{10,14},{11,15},{20,16},{21,... | collective-permute-start | bytes 2433032 | tf_op jit(solution)/shard_map/ppermute | solution.py:579
  37.9 12.4 %collective-permute-done.7.refs_0_ = bf16[3168,128]{1,0:T(8,128)(2,1)} collective-permute-done((bf16[3168,128]{1,0:T(8,128)(2,1)}, bf16[3168,128]{1,0:T(8,128)(2,1)}, u32[]{:S(2)}, u32[]{:S(2)}) %collective-permute-start.7) | collective-permute-done | bytes 811040 | tf_op jit(solution)/shard_map/ppermute | solution.py:579
  50.3 4.6 %visit.5 = (f32[48,2,128,128]{3,2,1,0:T(8,128)S(1)}, bf16[12,128,128]{2,1,0:T(8,128)(2,1)S(1)}, bf16[12,128,128]{2,1,0:T(8,128)(2,1)S(1)}) custom-call(s32[2]{0:T(128)S(1)} %pad_add_fusion.me_ref, s32[576]{0:T(1024)S(1)} %reshape.12.layout, bf16[3168,128]{1,0:T(8,128)(2,1)} %collective-permute-done.refs_0_, ...), custom_call_target="tpu_custom_call", output_to_operand_aliasing={{0}: (6, {})} | custom-call | tf_op jit(solution)/shard_map/visit/pallas_call | solution.py:541
  54.9 4.6 %visit.6 = (f32[48,2,128,128]{3,2,1,0:T(8,128)S(1)}, bf16[12,128,128]{2,1,0:T(8,128)(2,1)S(1)}, bf16[12,128,128]{2,1,0:T(8,128)(2,1)S(1)}) custom-call(s32[2]{0:T(128)S(1)} %pad_add_fusion.me_ref, s32[576]{0:T(1024)S(1)} %reshape.12.layout, bf16[3168,128]{1,0:T(8,128)(2,1)} %collective-permute-done.7.refs_0_, ...), custom_call_target="tpu_custom_call", output_to_operand_aliasing={{0}: (6, {})} | custom-call | tf_op jit(solution)/shard_map/visit/pallas_call | solution.py:541
  59.5 1.3 %collective-permute-start.8 = (bf16[12,128,128]{2,1,0:T(8,128)(2,1)S(1)}, bf16[12,128,128]{2,1,0:T(8,128)(2,1)S(1)}, u32[]{:S(2)}, u32[]{:S(2)}) collective-permute-start(bf16[12,128,128]{2,1,0:T(8,128)(2,1)S(1)} %get-tuple-element.49), channel_id=1, source_target_pairs={{0,4},{1,5},{2,6},{3,7},{12,8},{13,9},{14,10},{15,11},{16,20},{17,... | collective-permute-start | bytes 1179656 | tf_op jit(solution)/shard_map/ppermute | solution.py:579
  60.8 0.7 collective-permute-start.9
  61.5 6.0 %collective-permute-done.5.refs_0_ = bf16[3168,128]{1,0:T(8,128)(2,1)S(1)} collective-permute-done((bf16[3168,128]{1,0:T(8,128)(2,1)}, bf16[3168,128]{1,0:T(8,128)(2,1)S(1)}, u32[]{:S(2)}, u32[]{:S(2)}) %collective-permute-start.5) | collective-permute-done | bytes 811040 | tf_op jit(solution)/shard_map/ppermute | solution.py:579
  67.6 3.7 %visit.7 = (f32[48,2,128,128]{3,2,1,0:T(8,128)S(1)}, bf16[12,128,128]{2,1,0:T(8,128)(2,1)S(1)}) custom-call(s32[2]{0:T(128)S(1)} %pad_add_fusion.me_ref, s32[576]{0:T(1024)S(1)} %reshape.12.layout, bf16[3168,128]{1,0:T(8,128)(2,1)S(1)} %collective-permute-done.5.refs_0_, ...), custom_call_target="tpu_custom_call", output_to_operand_aliasing={{0}: (5, {})} | custom-call | flops 5033164800 | tf_op jit(solution)/shard_map/visit/pallas_call | solution.py:541
  71.3 0.0 collective-permute-done.8
  71.3 0.2 add_convert_fusion
  71.6 0.8 share.2
  72.4 0.1 collective-permute-start.10
  72.5 0.1 collective-permute-start.12
  72.5 0.7 collective-permute-start.13
  73.2 2.6 %collective-permute-done.10.refs_0_ = bf16[2,2,12,128,128]{4,3,2,1,0:T(8,128)(2,1)S(1)} collective-permute-done((bf16[2,2,12,128,128]{4,3,2,1,0:T(8,128)(2,1)S(1)}, bf16[2,2,12,128,128]{4,3,2,1,0:T(8,128)(2,1)S(1)}, u32[]{:S(2)}, u32[]{:S(2)}) %collective-permute-start.10) | collective-permute-done | bytes 1572896 | tf_op jit(solution)/shard_map/ppermute | solution.py:579
  75.9 0.8 share.3
  76.6 1.6 %collective-permute-start.11 = (bf16[2,1,12,128,128]{4,3,2,1,0:T(8,128)(2,1)S(1)}, bf16[2,1,12,128,128]{4,3,2,1,0:T(8,128)(2,1)S(1)}, u32[]{:S(2)}, u32[]{:S(2)}) collective-permute-start(bf16[2,1,12,128,128]{4,3,2,1,0:T(8,128)(2,1)S(1)} %share.3), channel_id=1, source_target_pairs={{0,2},{1,3},{2,0},{3,1},{4,6},{5,7},{6,4},{7,5},{8,10},{9,11},{10,... | collective-permute-start | bytes 2359304 | tf_op jit(solution)/shard_map/ppermute | solution.py:579
  78.2 2.8 %collective-permute-start.14 = (bf16[12,128,128]{2,1,0:T(8,128)(2,1)S(1)}, bf16[12,128,128]{2,1,0:T(8,128)(2,1)S(1)}, u32[]{:S(2)}, u32[]{:S(2)}) collective-permute-start(bf16[12,128,128]{2,1,0:T(8,128)(2,1)S(1)} %get-tuple-element.59), channel_id=1, source_target_pairs={{12,0},{13,1},{14,2},{15,3},{0,12},{1,13},{2,14},{3,15},{28,16},{2... | collective-permute-start | bytes 1179656 | tf_op jit(solution)/shard_map/ppermute | solution.py:579
  81.0 3.0 %collective-permute-done.12.refs_0_ = bf16[12,128,128]{2,1,0:T(8,128)(2,1)S(1)} collective-permute-done((bf16[12,128,128]{2,1,0:T(8,128)(2,1)S(1)}, bf16[12,128,128]{2,1,0:T(8,128)(2,1)S(1)}, u32[]{:S(2)}, u32[]{:S(2)}) %collective-permute-start.12) | collective-permute-done | bytes 393248 | tf_op jit(solution)/shard_map/ppermute | solution.py:579
  84.0 0.1 add.14.base
  84.2 8.7 %collective-permute-done.14.refs_0_ = bf16[12,128,128]{2,1,0:T(8,128)(2,1)S(1)} collective-permute-done((bf16[12,128,128]{2,1,0:T(8,128)(2,1)S(1)}, bf16[12,128,128]{2,1,0:T(8,128)(2,1)S(1)}, u32[]{:S(2)}, u32[]{:S(2)}) %collective-permute-start.14) | collective-permute-done | bytes 393248 | tf_op jit(solution)/shard_map/ppermute | solution.py:579
  92.8 0.9 add.15
  93.7 2.6 %collective-permute-done.11.refs_1_ = bf16[2,1,12,128,128]{4,3,2,1,0:T(8,128)(2,1)S(1)} collective-permute-done((bf16[2,1,12,128,128]{4,3,2,1,0:T(8,128)(2,1)S(1)}, bf16[2,1,12,128,128]{4,3,2,1,0:T(8,128)(2,1)S(1)}, u32[]{:S(2)}, u32[]{:S(2)}) %collective-permute-start.11) | collective-permute-done | bytes 786464 | tf_op jit(solution)/shard_map/ppermute | solution.py:579
  96.3 1.6 %finish.1 = (bf16[1536,128]{1,0:T(8,128)(2,1)}, bf16[1536,128]{1,0:T(8,128)(2,1)}) custom-call(s32[2]{0:T(128)S(1)} %pad_add_fusion.me_ref, f32[48,2,128,128]{3,2,1,0:T(8,128)S(1)} %get-tuple-element.55.acc, bf16[2,2,12,128,128]{4,3,2,1,0:T(8,128)(2,1)S(1)} %collective-permute-done.10.refs_0_, bf16[2,1,12,128,128]{4,3,2,1,0:T(8,128)(2,1)S(1)} %collective-permute-done.11.refs_1_), custom_call_target="tpu_custom_call" | custom-call | tf_op jit(solution)/shard_map/finish/pallas_call | solution.py:474
  (6 shorter events, 0.0 us)
Async XLA Ops:
  0.6 0.7 copy-start.2
  3.3 24.8 %copy-start.3 = (s32[192,3]{0,1:T(4,128)S(1)}, s32[192,3]{0,1:T(4,128)}, u32[]{:S(2)}) copy-start(s32[192,3]{0,1:T(4,128)} %param.13) | copy-start | bytes 6916
  3.3 21.3 %collective-permute-start = (bf16[3168,128]{1,0:T(8,128)(2,1)S(1)}, bf16[3168,128]{1,0:T(8,128)(2,1)}, u32[]{:S(2)}, u32[]{:S(2)}) collective-permute-start(bf16[3168,128]{1,0:T(8,128)(2,1)S(1)} %pack.1.unit.refs_0_), channel_id=1, source_target_pairs={{0,4},{1,5},{2,6},{3,7},{4,0},{5,1},{6,2},{7,3},{8,12},{9,13},{10,... | collective-permute-start | bytes 2433032 | tf_op jit(solution)/shard_map/ppermute | solution.py:579
  7.5 19.2 %collective-permute-start.3 = (bf16[3072,128]{1,0:T(8,128)(2,1)S(1)}, bf16[3072,128]{1,0:T(8,128)(2,1)}, u32[]{:S(2)}, u32[]{:S(2)}) collective-permute-start(bf16[3072,128]{1,0:T(8,128)(2,1)S(1)} %join.1.keyval.refs_1_), channel_id=1, source_target_pairs={{0,2},{1,3},{2,0},{3,1},{4,6},{5,7},{6,4},{7,5},{8,10},{9,11},{10,... | collective-permute-start | bytes 2359304 | tf_op jit(solution)/shard_map/ppermute | solution.py:579
  9.1 17.6 %collective-permute-start.6 = (bf16[3168,128]{1,0:T(8,128)(2,1)S(1)}, bf16[3168,128]{1,0:T(8,128)(2,1)}, u32[]{:S(2)}, u32[]{:S(2)}) collective-permute-start(bf16[3168,128]{1,0:T(8,128)(2,1)S(1)} %pack.1.unit.refs_0_), channel_id=1, source_target_pairs={{4,8},{5,9},{6,10},{7,11},{8,4},{9,5},{10,6},{11,7},{20,24},{21,25... | collective-permute-start | bytes 2433032 | tf_op jit(solution)/shard_map/ppermute | solution.py:579
  14.4 0.9 copy-start
  24.6 12.0 %collective-permute-start.1 = (bf16[3168,128]{1,0:T(8,128)(2,1)}, bf16[3168,128]{1,0:T(8,128)(2,1)}, u32[]{:S(2)}, u32[]{:S(2)}) collective-permute-start(bf16[3168,128]{1,0:T(8,128)(2,1)} %collective-permute-done.refs_0_), channel_id=1, source_target_pairs={{4,8},{5,9},{6,10},{7,11},{8,4},{9,5},{10,6},{11,7},{20,24},{21,25... | collective-permute-start | bytes 2433032 | tf_op jit(solution)/shard_map/ppermute | solution.py:579
  26.2 2.4 %collective-permute-start.2 = (bf16[3072,128]{1,0:T(8,128)(2,1)S(1)}, bf16[3072,128]{1,0:T(8,128)(2,1)}, u32[]{:S(2)}, u32[]{:S(2)}) collective-permute-start(bf16[3072,128]{1,0:T(8,128)(2,1)S(1)} %join.1.keyval.refs_1_), channel_id=1, source_target_pairs={{0,1},{1,0},{2,3},{3,2},{4,5},{5,4},{6,7},{7,6},{8,9},{9,8},{10,11... | collective-permute-start | bytes 2359304 | tf_op jit(solution)/shard_map/ppermute | solution.py:579
  26.7 3.2 %collective-permute-start.4 = (bf16[3072,128]{1,0:T(8,128)(2,1)}, bf16[3072,128]{1,0:T(8,128)(2,1)}, u32[]{:S(2)}, u32[]{:S(2)}) collective-permute-start(bf16[3072,128]{1,0:T(8,128)(2,1)} %collective-permute-done.3.refs_3_), channel_id=1, source_target_pairs={{0,1},{1,0},{2,3},{3,2},{4,5},{5,4},{6,7},{7,6},{8,9},{9,8},{10,11... | collective-permute-start | bytes 2359304 | tf_op jit(solution)/shard_map/ppermute | solution.py:579
  26.7 23.6 %collective-permute-start.7 = (bf16[3168,128]{1,0:T(8,128)(2,1)}, bf16[3168,128]{1,0:T(8,128)(2,1)}, u32[]{:S(2)}, u32[]{:S(2)}) collective-permute-start(bf16[3168,128]{1,0:T(8,128)(2,1)} %collective-permute-done.6.refs_1_), channel_id=1, source_target_pairs={{4,0},{5,1},{6,2},{7,3},{8,12},{9,13},{10,14},{11,15},{20,16},{21,... | collective-permute-start | bytes 2433032 | tf_op jit(solution)/shard_map/ppermute | solution.py:579
  29.9 1.1 %copy-start.1 = (f32[12,128,128]{2,1,0:T(8,128)S(1)}, f32[12,128,128]{2,1,0:T(8,128)}, u32[]{:S(2)}) copy-start(f32[12,128,128]{2,1,0:T(8,128)} %copy-done) | copy-start | bytes 2359300
  36.6 31.0 %collective-permute-start.5 = (bf16[3168,128]{1,0:T(8,128)(2,1)}, bf16[3168,128]{1,0:T(8,128)(2,1)S(1)}, u32[]{:S(2)}, u32[]{:S(2)}) collective-permute-start(bf16[3168,128]{1,0:T(8,128)(2,1)} %collective-permute-done.1.refs_1_), channel_id=1, source_target_pairs={{4,0},{5,1},{6,2},{7,3},{8,12},{9,13},{10,14},{11,15},{20,16},{21,... | collective-permute-start | bytes 2433032 | tf_op jit(solution)/shard_map/ppermute | solution.py:579
  59.5 11.8 %collective-permute-start.8 = (bf16[12,128,128]{2,1,0:T(8,128)(2,1)S(1)}, bf16[12,128,128]{2,1,0:T(8,128)(2,1)S(1)}, u32[]{:S(2)}, u32[]{:S(2)}) collective-permute-start(bf16[12,128,128]{2,1,0:T(8,128)(2,1)S(1)} %get-tuple-element.49), channel_id=1, source_target_pairs={{0,4},{1,5},{2,6},{3,7},{12,8},{13,9},{14,10},{15,11},{16,20},{17,... | collective-permute-start | bytes 1179656 | tf_op jit(solution)/shard_map/ppermute | solution.py:579
  60.8 10.5 %collective-permute-start.9 = (bf16[12,128,128]{2,1,0:T(8,128)(2,1)S(1)}, bf16[12,128,128]{2,1,0:T(8,128)(2,1)S(1)}, u32[]{:S(2)}, u32[]{:S(2)}) collective-permute-start(bf16[12,128,128]{2,1,0:T(8,128)(2,1)S(1)} %get-tuple-element.50), channel_id=1, source_target_pairs={{8,4},{9,5},{10,6},{11,7},{4,8},{5,9},{6,10},{7,11},{24,20},{25,21... | collective-permute-start | bytes 1179656 | tf_op jit(solution)/shard_map/ppermute | solution.py:579
  72.4 3.5 %collective-permute-start.10 = (bf16[2,2,12,128,128]{4,3,2,1,0:T(8,128)(2,1)S(1)}, bf16[2,2,12,128,128]{4,3,2,1,0:T(8,128)(2,1)S(1)}, u32[]{:S(2)}, u32[]{:S(2)}) collective-permute-start(bf16[2,2,12,128,128]{4,3,2,1,0:T(8,128)(2,1)S(1)} %share.2), channel_id=1, source_target_pairs={{0,1},{1,0},{2,3},{3,2},{4,5},{5,4},{6,7},{7,6},{8,9},{9,8},{10,11... | collective-permute-start | bytes 4718600 | tf_op jit(solution)/shard_map/ppermute | solution.py:579
  72.5 11.5 %collective-permute-start.12 = (bf16[12,128,128]{2,1,0:T(8,128)(2,1)S(1)}, bf16[12,128,128]{2,1,0:T(8,128)(2,1)S(1)}, u32[]{:S(2)}, u32[]{:S(2)}) collective-permute-start(bf16[12,128,128]{2,1,0:T(8,128)(2,1)S(1)} %get-tuple-element.57), channel_id=1, source_target_pairs={{4,0},{5,1},{6,2},{7,3},{0,4},{1,5},{2,6},{3,7},{12,8},{13,9},{14,... | collective-permute-start | bytes 1179656 | tf_op jit(solution)/shard_map/ppermute | solution.py:579
  72.5 11.5 %collective-permute-start.13 = (bf16[12,128,128]{2,1,0:T(8,128)(2,1)S(1)}, bf16[12,128,128]{2,1,0:T(8,128)(2,1)S(1)}, u32[]{:S(2)}, u32[]{:S(2)}) collective-permute-start(bf16[12,128,128]{2,1,0:T(8,128)(2,1)S(1)} %get-tuple-element.58), channel_id=1, source_target_pairs={{8,4},{9,5},{10,6},{11,7},{4,8},{5,9},{6,10},{7,11},{24,20},{25,21... | collective-permute-start | bytes 1179656 | tf_op jit(solution)/shard_map/ppermute | solution.py:579
  76.6 19.6 %collective-permute-start.11 = (bf16[2,1,12,128,128]{4,3,2,1,0:T(8,128)(2,1)S(1)}, bf16[2,1,12,128,128]{4,3,2,1,0:T(8,128)(2,1)S(1)}, u32[]{:S(2)}, u32[]{:S(2)}) collective-permute-start(bf16[2,1,12,128,128]{4,3,2,1,0:T(8,128)(2,1)S(1)} %share.3), channel_id=1, source_target_pairs={{0,2},{1,3},{2,0},{3,1},{4,6},{5,7},{6,4},{7,5},{8,10},{9,11},{10,... | collective-permute-start | bytes 2359304 | tf_op jit(solution)/shard_map/ppermute | solution.py:579
  78.2 14.7 %collective-permute-start.14 = (bf16[12,128,128]{2,1,0:T(8,128)(2,1)S(1)}, bf16[12,128,128]{2,1,0:T(8,128)(2,1)S(1)}, u32[]{:S(2)}, u32[]{:S(2)}) collective-permute-start(bf16[12,128,128]{2,1,0:T(8,128)(2,1)S(1)} %get-tuple-element.59), channel_id=1, source_target_pairs={{12,0},{13,1},{14,2},{15,3},{0,12},{1,13},{2,14},{3,15},{28,16},{2... | collective-permute-start | bytes 1179656 | tf_op jit(solution)/shard_map/ppermute | solution.py:579

commit v5 on v4

--- a/solution.py
+++ b/solution.py
@@ -10,6 +10,7 @@
 BLK = 128
 GLOB = 2
 TILE = 16
+CODE = 256
 PAIRS = 6
 TURNS = 3
 FAR = 1e30
@@ -37,7 +38,7 @@
     return next(groups for groups in (3, 4, 2, 1) if count % groups == 0)
 
 
-def pack_kernel(query, grad, output, lse, unit, output_s, delta_s, sems):
+def pack_kernel(query, grad, output, lse_hbm, unit, output_s, lse, delta_s, sems):
     count, width = lse.shape
     rows = stat_rows(count)
     groups = groups_of(count)
@@ -55,6 +56,8 @@
                 pltpu.make_async_copy(query.at[at], unit.at[at], sems.at[2, g]),
             ]
         )
+    lines = pltpu.make_async_copy(lse_hbm, lse, sems.at[3, 0])
+    lines.start()
     for kind in range(3):
         for load in loads:
             load[kind].start()
@@ -77,6 +80,7 @@
         sums = [total(high) + total(low) for high, low in zip(highs, lows)]
         for k in range(group):
             delta_s[g * group + k : g * group + k + 1, :] = sums[k][0:1]
+    lines.wait()
     lines = lse[...]
     if rows > count:
         lines = jnp.concatenate([lines, jnp.zeros((rows - count, width), jnp.float32)], 0)
@@ -93,16 +97,17 @@
     return pl.pallas_call(
         pack_kernel,
         out_shape=jax.ShapeDtypeStruct((2 * count * BLK + 6 * rows, width), jnp.bfloat16),
-        in_specs=[hbm, hbm, hbm, pl.BlockSpec(memory_space=pltpu.VMEM)],
+        in_specs=[hbm] * 4,
         out_specs=pl.BlockSpec(memory_space=pltpu.VMEM),
         scratch_shapes=[
             pltpu.VMEM(query.shape, jnp.bfloat16),
+            pltpu.VMEM(lse.shape, jnp.float32),
             pltpu.VMEM((rows, width), jnp.float32),
-            pltpu.SemaphoreType.DMA((3, groups_of(count))),
+            pltpu.SemaphoreType.DMA((4, groups_of(count))),
         ],
         compiler_params=pltpu.CompilerParams(vmem_limit_bytes=LIMIT),
         name="pack",
-    )(*[placed(array, pltpu.HBM) for array in (query, grad, output)], lse)
+    )(*[placed(array, pltpu.HBM) for array in (query, grad, output, lse)])
 
 
 def join_kernel(key, value, keyval, sems):
@@ -172,7 +177,6 @@
         self.layout, self.lists, self.values_at = (layout, lists, values_at)
         self.width = unit.shape[1]
         self.scaling = self.width ** (-0.5)
-        self.held = keys.shape[0] // BLK
 
     def begin(self, clear=True):
         count = self.count
@@ -225,10 +229,11 @@
 
         lax.fori_loop(0, count // chunk, step, 0)
 
-    def anchors(self):
+    def anchors(self, base):
         count, width = (self.count, self.width)
         chunk = 2 if count % 2 == 0 else 1
         turns = next(turns for turns in (TURNS, 2, 1) if count % (turns * chunk) == 0)
+        globals_ = pl.ds(base, GLOB)
 
         def step(c, carry):
             places, pairs = ([], [])
@@ -237,8 +242,8 @@
                 places.append(pl.ds(at, chunk))
                 pairs.append(
                     (
-                        self.keys[0 : GLOB * BLK, :],
-                        self.values[0 : GLOB * BLK, :],
+                        self.rows(self.keys, base, GLOB),
+                        self.rows(self.values, base, GLOB),
                         self.rows(self.unit, at, chunk),
                         self.rows(self.unit, count + at, chunk),
                         jnp.concatenate(
@@ -255,34 +260,35 @@
                 self.dq[blocks] += query_part.reshape(chunk, BLK, width)
             key_part = sum(part[1] for part in parts)
             value_part = sum(part[2] for part in parts)
-            self.acc[0:GLOB, 0] += key_part.reshape(GLOB, BLK, width)
-            self.acc[0:GLOB, 1] += value_part.reshape(GLOB, BLK, width)
+            self.acc[globals_, 0] += key_part.reshape(GLOB, BLK, width)
+            self.acc[globals_, 1] += value_part.reshape(GLOB, BLK, width)
             return carry
 
         lax.fori_loop(0, count // (chunk * turns), step, 0)
 
-    def scattered(self, guest, low, fanout, near):
+    def scattered(self, guest, me, span, fanout, near):
         who, whom, far = self.lists
         count = self.count
 
-        def note(at, q, target):
-            local = target - low
-            hit = (local >= 0) & (local < self.held)
+        def note(at, q, owner, block):
+            unit = jnp.bitwise_xor(owner, me)
+            hit = (unit >= 0) & (unit < span)
             who[at] = q
-            whom[at] = local
+            whom[at] = unit * count + block
             far[at] = 0.0
             return at + hit.astype(jnp.int32)
 
         def gather(q, at):
-            block = guest * count + q
+            entry = (guest * count + q) * fanout
             for r in range(fanout):
-                at = note(at, q, self.layout[block * fanout + r])
+                code = self.layout[entry + r]
+                at = note(at, q, lax.shift_right_logical(code, CODE.bit_length() - 1), code & (CODE - 1))
             return at
 
         found = lax.fori_loop(0, count, gather, 0)
         if near:
-            found = note(found, 0, guest * count - 1)
-            found = note(found, count - 1, (guest + 1) * count)
+            found = note(found, 0, guest - 1, count - 1)
+            found = note(found, count - 1, guest + 1, 0)
         for k in range(PAIRS - 1):
             who[found + k] = 0
             whom[found + k] = 0
@@ -332,7 +338,6 @@
     shards = me_ref[1]
     seat = lax.rem(me, span)
     row = lax.div(me, span)
-    low = row * span * count
     side = 1 - 2 * lax.rem(row, 2)
     if first:
         parts = [refs.pop(0) for _ in range(span)]
@@ -350,7 +355,7 @@
 
         def lay(b, carry):
             for m in range(span):
-                there = jnp.bitwise_xor(seat, m) * count + b
+                there = m * count + b
                 if m == 0:
                     acc[there] = acc_own[b]
                     sums[0][b] = dq_own[b]
@@ -375,9 +380,9 @@
             visitor.begin(offset != 0)
             @pl.when(row == 0)
             def _():
-                visitor.anchors()
-
-            visitor.scattered(guest, low, fanout, offset in (-1, 0, 1))
+                visitor.anchors(seat * count)
+
+            visitor.scattered(guest, me, span, fanout, offset in (-1, 0, 1))
             visitor.finish(out)
 
 
@@ -390,16 +395,15 @@
     return total.astype(jnp.bfloat16)
 
 
-def share_kernel(plan, me_ref, acc, *refs):
+def share_kernel(plan, acc, *refs):
     span, wanted, arrived = plan
     parts, out = (refs[:-1], refs[-1])
     count = acc.shape[0] // span
     scaling = acc.shape[3] ** (-0.5)
-    seat = lax.rem(me_ref[0], span)
 
     def step(b, carry):
         for k, m in enumerate(wanted):
-            place = jnp.bitwise_xor(seat, m) * count + b
+            place = m * count + b
             for which in range(2):
                 out[which, k, b] = sum_of(m, which, b, acc, place, scaling, parts, arrived)
         return carry
@@ -407,13 +411,12 @@
     lax.fori_loop(0, count, step, 0)
 
 
-def finish_kernel(plan, me_ref, acc, *refs):
+def finish_kernel(plan, acc, *refs):
     span, arrived = plan
     parts, outs = (refs[: len(arrived)], refs[len(arrived) : len(arrived) + 2])
     held_s, sems = refs[len(arrived) + 2 :]
     count = acc.shape[0] // span
     scaling = acc.shape[3] ** (-0.5)
-    seat = lax.rem(me_ref[0], span)
     groups = groups_of(count)
     group = count // groups
     copies = []
@@ -421,7 +424,7 @@
         for b in range(g * group, (g + 1) * group):
             for which in range(2):
                 held_s[which, b * BLK : (b + 1) * BLK, :] = sum_of(
-                    0, which, b, acc, seat * count + b, scaling, parts, arrived
+                    0, which, b, acc, b, scaling, parts, arrived
                 )
         for which in range(2):
             at = pl.ds(g * group * BLK, group * BLK)
@@ -454,19 +457,19 @@
     )(unit, keyval)
 
 
-def share(me, acc, span, wanted, arrived, parts):
+def share(acc, span, wanted, arrived, parts):
     held, _, _, width = acc.shape
     return pl.pallas_call(
         functools.partial(share_kernel, (span, wanted, arrived)),
         out_shape=jax.ShapeDtypeStruct((2, len(wanted), held // span, BLK, width), jnp.bfloat16),
-        in_specs=[SMEM] + [VMEM] * (1 + len(parts)),
+        in_specs=[VMEM] * (1 + len(parts)),
         out_specs=VMEM,
         compiler_params=pltpu.CompilerParams(vmem_limit_bytes=LIMIT),
         name="share",
-    )(me, acc, *parts)
-
-
-def finish(me, acc, span, arrived, parts):
+    )(acc, *parts)
+
+
+def finish(acc, span, arrived, parts):
     held, _, _, width = acc.shape
     count = held // span
     shape = (count * BLK, width)
@@ -474,7 +477,7 @@
     return pl.pallas_call(
         functools.partial(finish_kernel, (span, arrived)),
         out_shape=[jax.ShapeDtypeStruct(shape, jnp.bfloat16)] * 2,
-        in_specs=[SMEM] + [VMEM] * (1 + len(parts)),
+        in_specs=[VMEM] * (1 + len(parts)),
         out_specs=[hbm, hbm],
         scratch_shapes=[
             pltpu.VMEM((2,) + shape, jnp.bfloat16),
@@ -482,7 +485,7 @@
         ],
         compiler_params=pltpu.CompilerParams(vmem_limit_bytes=LIMIT),
         name="finish",
-    )(me, acc, *parts)
+    )(acc, *parts)
 
 
 def add_kernel(base, *refs):
@@ -593,7 +596,7 @@
         return [(p * span + e, q * span + e) for p, q in pairs for e in range(span)]
 
     me = jnp.stack([myself, jnp.int32(shards)]).astype(jnp.int32)
-    entries = layout.reshape(-1)
+    entries = (layout // count * CODE + layout % count).reshape(-1)
     unit = pack(query_rows, output_grad, output_rows, logsumexp.reshape(count, BLK))
     keyval = join(key_rows, value_rows)
 
@@ -660,11 +663,11 @@
     while bit < span:
         theirs = tuple(m for m in wanted if m & bit)
         wanted = tuple(m for m in wanted if not m & bit)
-        sent = share(me, acc, span, theirs, arrived, parts)
+        sent = share(acc, span, theirs, arrived, parts)
         arrived, parts = (arrived + (wanted,), parts + (swap(sent, bit),))
         bit = bit * 2
     *parts, query_grad = tie(*parts, query_grad)
-    key_grad, value_grad = finish(me, acc, span, arrived, parts)
+    key_grad, value_grad = finish(acc, span, arrived, parts)
     return (query_grad, key_grad, value_grad)
 
 

time: 98.3 us -> 96 us (0.977)
  Pallas kernels: 29.3 us -> 27.6 us
    pallas_call x2, Pallas kernels: 1.55 us -> 0.43 us  [share(): pl.pallas_call(functools.partial(share_kernel, (span, wanted, arrived)),...]
    unnamed x9 -> x6, local copies, waits for them, and re-layouts: 2.84 us -> 2.03 us
  transfers between devices with their start and end apart: 15 -> 15, of which waited for: 10 -> 9; matrix products, arithmetic and copies ran while one was open for 0% -> 0% of each run, Pallas kernels for 26% -> 26%
where the time goes in v5:
time: 96 us; the launch traced here: 95.6 us
  waiting for transfers between devices  46.2 us (48%)
  Pallas kernels  27.6 us (29%)
  starting transfers between devices  18.1 us (19%)
  local copies, waits for them, and re-layouts  2.34 us (2%)
    ppermute x15, waiting for transfers between devices, send(): return lax.ppermute(array, 'qb', pairs)  46.2 us
    pallas_call x4, Pallas kernels, visit(): pl.pallas_call(functools.partial(visit_kernel, plan), out_shape=outs, in_...  18.4 us
    ppermute x15, starting transfers between devices, send(): return lax.ppermute(array, 'qb', pairs)  18.1 us
    pallas_call x1, Pallas kernels, own_visit(): pl.pallas_call(own_kernel, out_shape=(jax.ShapeDtypeStruct((count, 2, BLK...  3.66 us
    unnamed x6, local copies, waits for them, and re-layouts  2.03 us
    pallas_call x1, Pallas kernels, pack(): pl.pallas_call(pack_kernel, out_shape=jax.ShapeDtypeStruct((2 * count * B...  2.01 us
  transfers between devices with their start and end apart: 15, of which 9 were waited for; matrix products, arithmetic and copies ran while one was open for 0% of the time, Pallas kernels for 26%

profile of v5, /device:TPU:0, one launch (start us, length us, event | category | flops | bytes accessed | tf_op | source)
XLA Modules:
  0.0 95.6 jit_solution(7096912359338192865)
XLA Ops:
  0.6 2.0 %pack.1.unit.refs_0_ = bf16[3168,128]{1,0:T(8,128)(2,1)S(1)} custom-call(bf16[1536,128]{1,0:T(8,128)(2,1)} %query.1, bf16[1536,128]{1,0:T(8,128)(2,1)} %grad.1, bf16[1536,128]{1,0:T(8,128)(2,1)} %output.1, f32[12,128]{1,0:T(8,128)} %bitcast.2), custom_call_target="tpu_custom_call" | custom-call | tf_op jit(solution)/shard_map/pack/pallas_call | solution.py:97
  2.6 0.0 copy-start.2
  2.7 3.1 %collective-permute-start = (bf16[3168,128]{1,0:T(8,128)(2,1)S(1)}, bf16[3168,128]{1,0:T(8,128)(2,1)}, u32[]{:S(2)}, u32[]{:S(2)}) collective-permute-start(bf16[3168,128]{1,0:T(8,128)(2,1)S(1)} %pack.1.unit.refs_0_), channel_id=1, source_target_pairs={{0,4},{1,5},{2,6},{3,7},{4,0},{5,1},{6,2},{7,3},{8,12},{9,13},{10,... | collective-permute-start | bytes 2433032 | tf_op jit(solution)/shard_map/ppermute | solution.py:582
  5.8 1.1 %join.1.keyval.refs_1_ = bf16[3072,128]{1,0:T(8,128)(2,1)S(1)} custom-call(bf16[1536,128]{1,0:T(8,128)(2,1)} %key.1, bf16[1536,128]{1,0:T(8,128)(2,1)} %value.1), custom_call_target="tpu_custom_call" | custom-call | tf_op jit(solution)/shard_map/join/pallas_call | solution.py:128
  6.9 1.6 %collective-permute-start.3 = (bf16[3072,128]{1,0:T(8,128)(2,1)S(1)}, bf16[3072,128]{1,0:T(8,128)(2,1)}, u32[]{:S(2)}, u32[]{:S(2)}) collective-permute-start(bf16[3072,128]{1,0:T(8,128)(2,1)S(1)} %join.1.keyval.refs_1_), channel_id=1, source_target_pairs={{0,2},{1,3},{2,0},{3,1},{4,6},{5,7},{6,4},{7,5},{8,10},{9,11},{10,... | collective-permute-start | bytes 2359304 | tf_op jit(solution)/shard_map/ppermute | solution.py:582
  8.4 1.6 %collective-permute-start.6 = (bf16[3168,128]{1,0:T(8,128)(2,1)S(1)}, bf16[3168,128]{1,0:T(8,128)(2,1)}, u32[]{:S(2)}, u32[]{:S(2)}) collective-permute-start(bf16[3168,128]{1,0:T(8,128)(2,1)S(1)} %pack.1.unit.refs_0_), channel_id=1, source_target_pairs={{4,8},{5,9},{6,10},{7,11},{8,4},{9,5},{10,6},{11,7},{20,24},{21,25... | collective-permute-start | bytes 2433032 | tf_op jit(solution)/shard_map/ppermute | solution.py:582
  10.0 3.7 %own.1 = (f32[12,2,128,128]{3,2,1,0:T(8,128)S(1)}, f32[12,128,128]{2,1,0:T(8,128)S(1)}) custom-call(bf16[3168,128]{1,0:T(8,128)(2,1)S(1)} %pack.1.unit.refs_0_, bf16[3072,128]{1,0:T(8,128)(2,1)S(1)} %join.1.keyval.refs_1_), custom_call_target="tpu_custom_call" | custom-call | tf_op jit(solution)/shard_map/own/pallas_call | solution.py:448
  13.7 0.9 copy-done
  14.6 9.3 %collective-permute-done.refs_0_ = bf16[3168,128]{1,0:T(8,128)(2,1)} collective-permute-done((bf16[3168,128]{1,0:T(8,128)(2,1)S(1)}, bf16[3168,128]{1,0:T(8,128)(2,1)}, u32[]{:S(2)}, u32[]{:S(2)}) %collective-permute-start) | collective-permute-done | bytes 811040 | tf_op jit(solution)/shard_map/ppermute | solution.py:582
  23.9 1.6 %collective-permute-start.1 = (bf16[3168,128]{1,0:T(8,128)(2,1)}, bf16[3168,128]{1,0:T(8,128)(2,1)}, u32[]{:S(2)}, u32[]{:S(2)}) collective-permute-start(bf16[3168,128]{1,0:T(8,128)(2,1)} %collective-permute-done.refs_0_), channel_id=1, source_target_pairs={{4,8},{5,9},{6,10},{7,11},{8,4},{9,5},{10,6},{11,7},{20,24},{21,25... | collective-permute-start | bytes 2433032 | tf_op jit(solution)/shard_map/ppermute | solution.py:582
  25.5 0.0 collective-permute-start.2
  25.5 0.6 collective-permute-done.3.refs_3_
  26.1 0.0 collective-permute-start.4
  26.1 0.0 collective-permute-done.6.refs_1_
  26.1 1.3 %collective-permute-start.7 = (bf16[3168,128]{1,0:T(8,128)(2,1)}, bf16[3168,128]{1,0:T(8,128)(2,1)}, u32[]{:S(2)}, u32[]{:S(2)}) collective-permute-start(bf16[3168,128]{1,0:T(8,128)(2,1)} %collective-permute-done.6.refs_1_), channel_id=1, source_target_pairs={{4,0},{5,1},{6,2},{7,3},{8,12},{9,13},{10,14},{11,15},{20,16},{21,... | collective-permute-start | bytes 2433032 | tf_op jit(solution)/shard_map/ppermute | solution.py:582
  27.4 0.1 pad_add_fusion.me_ref
  27.5 0.1 copy.13
  27.6 0.2 reshape.12.layout
  27.8 0.1 collective-permute-done.2.refs_2_
  27.9 1.3 %collective-permute-done.4.refs_4_ = bf16[3072,128]{1,0:T(8,128)(2,1)} collective-permute-done((bf16[3072,128]{1,0:T(8,128)(2,1)}, bf16[3072,128]{1,0:T(8,128)(2,1)}, u32[]{:S(2)}, u32[]{:S(2)}) %collective-permute-start.4) | collective-permute-done | bytes 786464 | tf_op jit(solution)/shard_map/ppermute | solution.py:582
  29.2 1.1 %copy-done.1 = f32[12,128,128]{2,1,0:T(8,128)S(1)} copy-done((f32[12,128,128]{2,1,0:T(8,128)S(1)}, f32[12,128,128]{2,1,0:T(8,128)}, u32[]{:S(2)}) %copy-start.1) | copy-done | bytes 786456
  30.4 5.4 %visit.4 = (bf16[6144,128]{1,0:T(8,128)(2,1)S(1)}, bf16[6144,128]{1,0:T(8,128)(2,1)S(1)}, f32[48,2,128,128]{3,2,1,0:T(8,128)S(1)}, f32[12,128,128]{2,1,0:T(8,128)S(1)}) custom-call(s32[2]{0:T(128)S(1)} %pad_add_fusion.me_ref, s32[576]{0:T(1024)S(1)} %reshape.12.layout, bf16[3168,128]{1,0:T(8,128)(2,1)S(1)} %pack.1.unit.refs_0_, ...), custom_call_target="tpu_custom_call" | custom-call | tf_op jit(solution)/shard_map/visit/pallas_call | solution.py:544
  35.8 0.0 collective-permute-done.1.refs_1_
  35.8 1.3 %collective-permute-start.5 = (bf16[3168,128]{1,0:T(8,128)(2,1)}, bf16[3168,128]{1,0:T(8,128)(2,1)S(1)}, u32[]{:S(2)}, u32[]{:S(2)}) collective-permute-start(bf16[3168,128]{1,0:T(8,128)(2,1)} %collective-permute-done.1.refs_1_), channel_id=1, source_target_pairs={{4,0},{5,1},{6,2},{7,3},{8,12},{9,13},{10,14},{11,15},{20,16},{21,... | collective-permute-start | bytes 2433032 | tf_op jit(solution)/shard_map/ppermute | solution.py:582
  37.1 12.6 %collective-permute-done.7.refs_0_ = bf16[3168,128]{1,0:T(8,128)(2,1)} collective-permute-done((bf16[3168,128]{1,0:T(8,128)(2,1)}, bf16[3168,128]{1,0:T(8,128)(2,1)}, u32[]{:S(2)}, u32[]{:S(2)}) %collective-permute-start.7) | collective-permute-done | bytes 811040 | tf_op jit(solution)/shard_map/ppermute | solution.py:582
  49.7 4.6 %visit.5 = (f32[48,2,128,128]{3,2,1,0:T(8,128)S(1)}, bf16[12,128,128]{2,1,0:T(8,128)(2,1)S(1)}, bf16[12,128,128]{2,1,0:T(8,128)(2,1)S(1)}) custom-call(s32[2]{0:T(128)S(1)} %pad_add_fusion.me_ref, s32[576]{0:T(1024)S(1)} %reshape.12.layout, bf16[3168,128]{1,0:T(8,128)(2,1)} %collective-permute-done.refs_0_, ...), custom_call_target="tpu_custom_call", output_to_operand_aliasing={{0}: (6, {})} | custom-call | tf_op jit(solution)/shard_map/visit/pallas_call | solution.py:544
  54.3 4.6 %visit.6 = (f32[48,2,128,128]{3,2,1,0:T(8,128)S(1)}, bf16[12,128,128]{2,1,0:T(8,128)(2,1)S(1)}, bf16[12,128,128]{2,1,0:T(8,128)(2,1)S(1)}) custom-call(s32[2]{0:T(128)S(1)} %pad_add_fusion.me_ref, s32[576]{0:T(1024)S(1)} %reshape.12.layout, bf16[3168,128]{1,0:T(8,128)(2,1)} %collective-permute-done.7.refs_0_, ...), custom_call_target="tpu_custom_call", output_to_operand_aliasing={{0}: (6, {})} | custom-call | tf_op jit(solution)/shard_map/visit/pallas_call | solution.py:544
  58.9 1.3 %collective-permute-start.8 = (bf16[12,128,128]{2,1,0:T(8,128)(2,1)S(1)}, bf16[12,128,128]{2,1,0:T(8,128)(2,1)S(1)}, u32[]{:S(2)}, u32[]{:S(2)}) collective-permute-start(bf16[12,128,128]{2,1,0:T(8,128)(2,1)S(1)} %get-tuple-element.49), channel_id=1, source_target_pairs={{0,4},{1,5},{2,6},{3,7},{12,8},{13,9},{14,10},{15,11},{16,20},{17,... | collective-permute-start | bytes 1179656 | tf_op jit(solution)/shard_map/ppermute | solution.py:582
  60.2 0.7 collective-permute-start.9
  60.9 6.0 %collective-permute-done.5.refs_0_ = bf16[3168,128]{1,0:T(8,128)(2,1)S(1)} collective-permute-done((bf16[3168,128]{1,0:T(8,128)(2,1)}, bf16[3168,128]{1,0:T(8,128)(2,1)S(1)}, u32[]{:S(2)}, u32[]{:S(2)}) %collective-permute-start.5) | collective-permute-done | bytes 811040 | tf_op jit(solution)/shard_map/ppermute | solution.py:582
  66.9 3.8 %visit.7 = (f32[48,2,128,128]{3,2,1,0:T(8,128)S(1)}, bf16[12,128,128]{2,1,0:T(8,128)(2,1)S(1)}) custom-call(s32[2]{0:T(128)S(1)} %pad_add_fusion.me_ref, s32[576]{0:T(1024)S(1)} %reshape.12.layout, bf16[3168,128]{1,0:T(8,128)(2,1)S(1)} %collective-permute-done.5.refs_0_, ...), custom_call_target="tpu_custom_call", output_to_operand_aliasing={{0}: (5, {})} | custom-call | flops 5033164800 | tf_op jit(solution)/shard_map/visit/pallas_call | solution.py:544
  70.7 0.0 collective-permute-done.8
  70.7 0.3 add_convert_fusion
  71.0 0.2 share.2
  71.3 0.1 collective-permute-start.10
  71.3 0.7 collective-permute-start.12
  72.0 0.7 collective-permute-start.13
  72.7 2.1 %collective-permute-done.10.refs_0_ = bf16[2,2,12,128,128]{4,3,2,1,0:T(8,128)(2,1)S(1)} collective-permute-done((bf16[2,2,12,128,128]{4,3,2,1,0:T(8,128)(2,1)S(1)}, bf16[2,2,12,128,128]{4,3,2,1,0:T(8,128)(2,1)S(1)}, u32[]{:S(2)}, u32[]{:S(2)}) %collective-permute-start.10) | collective-permute-done | bytes 1572896 | tf_op jit(solution)/shard_map/ppermute | solution.py:582
  74.7 0.2 share.3
  74.9 1.6 %collective-permute-start.11 = (bf16[2,1,12,128,128]{4,3,2,1,0:T(8,128)(2,1)S(1)}, bf16[2,1,12,128,128]{4,3,2,1,0:T(8,128)(2,1)S(1)}, u32[]{:S(2)}, u32[]{:S(2)}) collective-permute-start(bf16[2,1,12,128,128]{4,3,2,1,0:T(8,128)(2,1)S(1)} %share.3), channel_id=1, source_target_pairs={{0,2},{1,3},{2,0},{3,1},{4,6},{5,7},{6,4},{7,5},{8,10},{9,11},{10,... | collective-permute-start | bytes 2359304 | tf_op jit(solution)/shard_map/ppermute | solution.py:582
  76.5 2.8 %collective-permute-start.14 = (bf16[12,128,128]{2,1,0:T(8,128)(2,1)S(1)}, bf16[12,128,128]{2,1,0:T(8,128)(2,1)S(1)}, u32[]{:S(2)}, u32[]{:S(2)}) collective-permute-start(bf16[12,128,128]{2,1,0:T(8,128)(2,1)S(1)} %get-tuple-element.59), channel_id=1, source_target_pairs={{12,0},{13,1},{14,2},{15,3},{0,12},{1,13},{2,14},{3,15},{28,16},{2... | collective-permute-start | bytes 1179656 | tf_op jit(solution)/shard_map/ppermute | solution.py:582
  79.3 12.0 %collective-permute-done.12.refs_0_ = bf16[12,128,128]{2,1,0:T(8,128)(2,1)S(1)} collective-permute-done((bf16[12,128,128]{2,1,0:T(8,128)(2,1)S(1)}, bf16[12,128,128]{2,1,0:T(8,128)(2,1)S(1)}, u32[]{:S(2)}, u32[]{:S(2)}) %collective-permute-start.12) | collective-permute-done | bytes 393248 | tf_op jit(solution)/shard_map/ppermute | solution.py:582
  91.3 0.0 collective-permute-done.13.refs_1_
  91.3 0.1 add.30.base
  91.5 0.0 collective-permute-done.14.refs_0_
  91.5 0.9 add.31
  92.3 2.2 %collective-permute-done.11.refs_1_ = bf16[2,1,12,128,128]{4,3,2,1,0:T(8,128)(2,1)S(1)} collective-permute-done((bf16[2,1,12,128,128]{4,3,2,1,0:T(8,128)(2,1)S(1)}, bf16[2,1,12,128,128]{4,3,2,1,0:T(8,128)(2,1)S(1)}, u32[]{:S(2)}, u32[]{:S(2)}) %collective-permute-start.11) | collective-permute-done | bytes 786464 | tf_op jit(solution)/shard_map/ppermute | solution.py:582
  94.6 1.0 %finish.1 = (bf16[1536,128]{1,0:T(8,128)(2,1)}, bf16[1536,128]{1,0:T(8,128)(2,1)}) custom-call(f32[48,2,128,128]{3,2,1,0:T(8,128)S(1)} %get-tuple-element.55.acc, bf16[2,2,12,128,128]{4,3,2,1,0:T(8,128)(2,1)S(1)} %collective-permute-done.10.refs_0_, bf16[2,1,12,128,128]{4,3,2,1,0:T(8,128)(2,1)S(1)} %collective-permute-done.11.refs_1_), custom_call_target="tpu_custom_call" | custom-call | tf_op jit(solution)/shard_map/finish/pallas_call | solution.py:477
  (5 shorter events, 0.0 us)
Async XLA Ops:
  2.6 23.4 %copy-start.2 = (s32[192,3]{0,1:T(4,128)S(1)}, s32[192,3]{0,1:T(4,128)}, u32[]{:S(2)}) copy-start(s32[192,3]{0,1:T(4,128)} %param.13) | copy-start | bytes 6916
  2.7 21.3 %collective-permute-start = (bf16[3168,128]{1,0:T(8,128)(2,1)S(1)}, bf16[3168,128]{1,0:T(8,128)(2,1)}, u32[]{:S(2)}, u32[]{:S(2)}) collective-permute-start(bf16[3168,128]{1,0:T(8,128)(2,1)S(1)} %pack.1.unit.refs_0_), channel_id=1, source_target_pairs={{0,4},{1,5},{2,6},{3,7},{4,0},{5,1},{6,2},{7,3},{8,12},{9,13},{10,... | collective-permute-start | bytes 2433032 | tf_op jit(solution)/shard_map/ppermute | solution.py:582
  6.9 19.2 %collective-permute-start.3 = (bf16[3072,128]{1,0:T(8,128)(2,1)S(1)}, bf16[3072,128]{1,0:T(8,128)(2,1)}, u32[]{:S(2)}, u32[]{:S(2)}) collective-permute-start(bf16[3072,128]{1,0:T(8,128)(2,1)S(1)} %join.1.keyval.refs_1_), channel_id=1, source_target_pairs={{0,2},{1,3},{2,0},{3,1},{4,6},{5,7},{6,4},{7,5},{8,10},{9,11},{10,... | collective-permute-start | bytes 2359304 | tf_op jit(solution)/shard_map/ppermute | solution.py:582
  8.4 17.6 %collective-permute-start.6 = (bf16[3168,128]{1,0:T(8,128)(2,1)S(1)}, bf16[3168,128]{1,0:T(8,128)(2,1)}, u32[]{:S(2)}, u32[]{:S(2)}) collective-permute-start(bf16[3168,128]{1,0:T(8,128)(2,1)S(1)} %pack.1.unit.refs_0_), channel_id=1, source_target_pairs={{4,8},{5,9},{6,10},{7,11},{8,4},{9,5},{10,6},{11,7},{20,24},{21,25... | collective-permute-start | bytes 2433032 | tf_op jit(solution)/shard_map/ppermute | solution.py:582
  13.7 0.9 copy-start
  23.9 11.9 %collective-permute-start.1 = (bf16[3168,128]{1,0:T(8,128)(2,1)}, bf16[3168,128]{1,0:T(8,128)(2,1)}, u32[]{:S(2)}, u32[]{:S(2)}) collective-permute-start(bf16[3168,128]{1,0:T(8,128)(2,1)} %collective-permute-done.refs_0_), channel_id=1, source_target_pairs={{4,8},{5,9},{6,10},{7,11},{8,4},{9,5},{10,6},{11,7},{20,24},{21,25... | collective-permute-start | bytes 2433032 | tf_op jit(solution)/shard_map/ppermute | solution.py:582
  25.5 2.4 %collective-permute-start.2 = (bf16[3072,128]{1,0:T(8,128)(2,1)S(1)}, bf16[3072,128]{1,0:T(8,128)(2,1)}, u32[]{:S(2)}, u32[]{:S(2)}) collective-permute-start(bf16[3072,128]{1,0:T(8,128)(2,1)S(1)} %join.1.keyval.refs_1_), channel_id=1, source_target_pairs={{0,1},{1,0},{2,3},{3,2},{4,5},{5,4},{6,7},{7,6},{8,9},{9,8},{10,11... | collective-permute-start | bytes 2359304 | tf_op jit(solution)/shard_map/ppermute | solution.py:582
  26.1 3.2 %collective-permute-start.4 = (bf16[3072,128]{1,0:T(8,128)(2,1)}, bf16[3072,128]{1,0:T(8,128)(2,1)}, u32[]{:S(2)}, u32[]{:S(2)}) collective-permute-start(bf16[3072,128]{1,0:T(8,128)(2,1)} %collective-permute-done.3.refs_3_), channel_id=1, source_target_pairs={{0,1},{1,0},{2,3},{3,2},{4,5},{5,4},{6,7},{7,6},{8,9},{9,8},{10,11... | collective-permute-start | bytes 2359304 | tf_op jit(solution)/shard_map/ppermute | solution.py:582
  26.1 23.6 %collective-permute-start.7 = (bf16[3168,128]{1,0:T(8,128)(2,1)}, bf16[3168,128]{1,0:T(8,128)(2,1)}, u32[]{:S(2)}, u32[]{:S(2)}) collective-permute-start(bf16[3168,128]{1,0:T(8,128)(2,1)} %collective-permute-done.6.refs_1_), channel_id=1, source_target_pairs={{4,0},{5,1},{6,2},{7,3},{8,12},{9,13},{10,14},{11,15},{20,16},{21,... | collective-permute-start | bytes 2433032 | tf_op jit(solution)/shard_map/ppermute | solution.py:582
  29.2 1.1 %copy-start.1 = (f32[12,128,128]{2,1,0:T(8,128)S(1)}, f32[12,128,128]{2,1,0:T(8,128)}, u32[]{:S(2)}) copy-start(f32[12,128,128]{2,1,0:T(8,128)} %copy-done) | copy-start | bytes 2359300
  35.8 31.1 %collective-permute-start.5 = (bf16[3168,128]{1,0:T(8,128)(2,1)}, bf16[3168,128]{1,0:T(8,128)(2,1)S(1)}, u32[]{:S(2)}, u32[]{:S(2)}) collective-permute-start(bf16[3168,128]{1,0:T(8,128)(2,1)} %collective-permute-done.1.refs_1_), channel_id=1, source_target_pairs={{4,0},{5,1},{6,2},{7,3},{8,12},{9,13},{10,14},{11,15},{20,16},{21,... | collective-permute-start | bytes 2433032 | tf_op jit(solution)/shard_map/ppermute | solution.py:582
  58.9 11.8 %collective-permute-start.8 = (bf16[12,128,128]{2,1,0:T(8,128)(2,1)S(1)}, bf16[12,128,128]{2,1,0:T(8,128)(2,1)S(1)}, u32[]{:S(2)}, u32[]{:S(2)}) collective-permute-start(bf16[12,128,128]{2,1,0:T(8,128)(2,1)S(1)} %get-tuple-element.49), channel_id=1, source_target_pairs={{0,4},{1,5},{2,6},{3,7},{12,8},{13,9},{14,10},{15,11},{16,20},{17,... | collective-permute-start | bytes 1179656 | tf_op jit(solution)/shard_map/ppermute | solution.py:582
  60.2 10.5 %collective-permute-start.9 = (bf16[12,128,128]{2,1,0:T(8,128)(2,1)S(1)}, bf16[12,128,128]{2,1,0:T(8,128)(2,1)S(1)}, u32[]{:S(2)}, u32[]{:S(2)}) collective-permute-start(bf16[12,128,128]{2,1,0:T(8,128)(2,1)S(1)} %get-tuple-element.50), channel_id=1, source_target_pairs={{8,4},{9,5},{10,6},{11,7},{4,8},{5,9},{6,10},{7,11},{24,20},{25,21... | collective-permute-start | bytes 1179656 | tf_op jit(solution)/shard_map/ppermute | solution.py:582
  71.3 3.5 %collective-permute-start.10 = (bf16[2,2,12,128,128]{4,3,2,1,0:T(8,128)(2,1)S(1)}, bf16[2,2,12,128,128]{4,3,2,1,0:T(8,128)(2,1)S(1)}, u32[]{:S(2)}, u32[]{:S(2)}) collective-permute-start(bf16[2,2,12,128,128]{4,3,2,1,0:T(8,128)(2,1)S(1)} %share.2), channel_id=1, source_target_pairs={{0,1},{1,0},{2,3},{3,2},{4,5},{5,4},{6,7},{7,6},{8,9},{9,8},{10,11... | collective-permute-start | bytes 4718600 | tf_op jit(solution)/shard_map/ppermute | solution.py:582
  71.3 20.0 %collective-permute-start.12 = (bf16[12,128,128]{2,1,0:T(8,128)(2,1)S(1)}, bf16[12,128,128]{2,1,0:T(8,128)(2,1)S(1)}, u32[]{:S(2)}, u32[]{:S(2)}) collective-permute-start(bf16[12,128,128]{2,1,0:T(8,128)(2,1)S(1)} %get-tuple-element.57), channel_id=1, source_target_pairs={{4,0},{5,1},{6,2},{7,3},{0,4},{1,5},{2,6},{3,7},{12,8},{13,9},{14,... | collective-permute-start | bytes 1179656 | tf_op jit(solution)/shard_map/ppermute | solution.py:582
  72.0 19.3 %collective-permute-start.13 = (bf16[12,128,128]{2,1,0:T(8,128)(2,1)S(1)}, bf16[12,128,128]{2,1,0:T(8,128)(2,1)S(1)}, u32[]{:S(2)}, u32[]{:S(2)}) collective-permute-start(bf16[12,128,128]{2,1,0:T(8,128)(2,1)S(1)} %get-tuple-element.58), channel_id=1, source_target_pairs={{8,4},{9,5},{10,6},{11,7},{4,8},{5,9},{6,10},{7,11},{24,20},{25,21... | collective-permute-start | bytes 1179656 | tf_op jit(solution)/shard_map/ppermute | solution.py:582
  74.9 19.6 %collective-permute-start.11 = (bf16[2,1,12,128,128]{4,3,2,1,0:T(8,128)(2,1)S(1)}, bf16[2,1,12,128,128]{4,3,2,1,0:T(8,128)(2,1)S(1)}, u32[]{:S(2)}, u32[]{:S(2)}) collective-permute-start(bf16[2,1,12,128,128]{4,3,2,1,0:T(8,128)(2,1)S(1)} %share.3), channel_id=1, source_target_pairs={{0,2},{1,3},{2,0},{3,1},{4,6},{5,7},{6,4},{7,5},{8,10},{9,11},{10,... | collective-permute-start | bytes 2359304 | tf_op jit(solution)/shard_map/ppermute | solution.py:582
  76.5 15.0 %collective-permute-start.14 = (bf16[12,128,128]{2,1,0:T(8,128)(2,1)S(1)}, bf16[12,128,128]{2,1,0:T(8,128)(2,1)S(1)}, u32[]{:S(2)}, u32[]{:S(2)}) collective-permute-start(bf16[12,128,128]{2,1,0:T(8,128)(2,1)S(1)} %get-tuple-element.59), channel_id=1, source_target_pairs={{12,0},{13,1},{14,2},{15,3},{0,12},{1,13},{2,14},{3,15},{28,16},{2... | collective-permute-start | bytes 1179656 | tf_op jit(solution)/shard_map/ppermute | solution.py:582

commit v6 on v5

--- a/solution.py
+++ b/solution.py
@@ -19,15 +19,12 @@
 
 
 def pieces(row):
-    high = row.astype(jnp.bfloat16)
-    rest = row - high.astype(jnp.float32)
-    middle = rest.astype(jnp.bfloat16)
-    low = (rest - middle.astype(jnp.float32)).astype(jnp.bfloat16)
-    return [high.astype(jnp.float32), middle.astype(jnp.float32), low.astype(jnp.float32)]
+    high = row.astype(jnp.bfloat16).astype(jnp.float32)
+    return [high, row - high]
 
 
 def stat_rows(count):
-    return -(-count // TILE) * TILE
+    return -(-4 * count // TILE) * TILE
 
 
 def placed(array, space):
@@ -38,9 +35,8 @@
     return next(groups for groups in (3, 4, 2, 1) if count % groups == 0)
 
 
-def pack_kernel(query, grad, output, lse_hbm, unit, output_s, lse, delta_s, sems):
+def pack_kernel(query, grad, output, lse_hbm, unit, output_s, lse, delta_s, stat_s, sems):
     count, width = lse.shape
-    rows = stat_rows(count)
     groups = groups_of(count)
     group = count // groups
     ones = jnp.ones((TILE, width), jnp.bfloat16)
@@ -67,7 +63,6 @@
             ones, part, (((1,), (1,)), ((), ())), preferred_element_type=jnp.float32
         )
 
-    delta_s[...] = jnp.zeros(delta_s.shape, jnp.float32)
     for g in range(groups):
         loads[g][0].wait()
         loads[g][1].wait()
@@ -81,11 +76,10 @@
         for k in range(group):
             delta_s[g * group + k : g * group + k + 1, :] = sums[k][0:1]
     lines.wait()
-    lines = lse[...]
-    if rows > count:
-        lines = jnp.concatenate([lines, jnp.zeros((rows - count, width), jnp.float32)], 0)
-    stats = pieces(lines) + pieces(delta_s[...])
-    unit[2 * held :, :] = jnp.concatenate(stats, 0).astype(jnp.bfloat16)
+    stat_s[...] = jnp.zeros(stat_s.shape, jnp.float32)
+    for k, line in enumerate(pieces(lse[...]) + pieces(delta_s[...])):
+        stat_s[k * count : (k + 1) * count, :] = line
+    unit[2 * held :, :] = stat_s[...].astype(jnp.bfloat16)
     for load in loads:
         load[2].wait()
 
@@ -96,11 +90,12 @@
     hbm = pl.BlockSpec(memory_space=pltpu.HBM)
     return pl.pallas_call(
         pack_kernel,
-        out_shape=jax.ShapeDtypeStruct((2 * count * BLK + 6 * rows, width), jnp.bfloat16),
+        out_shape=jax.ShapeDtypeStruct((2 * count * BLK + rows, width), jnp.bfloat16),
         in_specs=[hbm] * 4,
         out_specs=pl.BlockSpec(memory_space=pltpu.VMEM),
         scratch_shapes=[
             pltpu.VMEM(query.shape, jnp.bfloat16),
+            pltpu.VMEM(lse.shape, jnp.float32),
             pltpu.VMEM(lse.shape, jnp.float32),
             pltpu.VMEM((rows, width), jnp.float32),
             pltpu.SemaphoreType.DMA((4, groups_of(count))),
@@ -169,10 +164,10 @@
 
 class Visitor:
     def __init__(
-        self, count, unit, lse, delta, dq, keys, values, acc, layout=None, lists=None, values_at=0
+        self, count, unit, stat, dq, keys, values, acc, layout=None, lists=None, values_at=0
     ):
         self.count = count
-        self.unit, self.lse, self.delta = (unit, lse, delta)
+        self.unit, self.stat = (unit, stat)
         self.dq, self.keys, self.values, self.acc = (dq, keys, values, acc)
         self.layout, self.lists, self.values_at = (layout, lists, values_at)
         self.width = unit.shape[1]
@@ -180,11 +175,7 @@
 
     def begin(self, clear=True):
         count = self.count
-        rows = stat_rows(count)
-        stats = self.unit[2 * count * BLK :, :].astype(jnp.float32)
-        lines = [stats[k * rows : (k + 1) * rows] for k in range(6)]
-        self.lse[...] = lines[0] + lines[1] + lines[2]
-        self.delta[...] = lines[3] + lines[4] + lines[5]
+        self.stat[...] = self.unit[2 * count * BLK :, :].astype(jnp.float32)
 
         def step(q, carry):
             self.dq[q] = jnp.zeros(self.dq.shape[1:], jnp.float32)
@@ -195,6 +186,10 @@
 
     def rows(self, array, block, blocks=1):
         return array[pl.ds(pl.multiple_of(block * BLK, BLK), blocks * BLK), :]
+
+    def line(self, q, kind):
+        at = 2 * kind * self.count + q
+        return self.stat[pl.ds(at, 1), :] + self.stat[pl.ds(at + self.count, 1), :]
 
     def pair(self, q, j, keys=1, shift=0.0, mask=None):
         return (
@@ -202,8 +197,8 @@
             self.rows(self.values, self.values_at + j, keys),
             self.rows(self.unit, q),
             self.rows(self.unit, self.count + q),
-            self.lse[pl.ds(q, 1), :] + shift,
-            self.delta[pl.ds(q, 1), :],
+            self.line(q, 0) + shift,
+            self.line(q, 1),
             mask,
         )
 
@@ -247,10 +242,10 @@
                         self.rows(self.unit, at, chunk),
                         self.rows(self.unit, count + at, chunk),
                         jnp.concatenate(
-                            [self.lse[pl.ds(at + i, 1), :] for i in range(chunk)], 1
+                            [self.line(at + i, 0) for i in range(chunk)], 1
                         ),
                         jnp.concatenate(
-                            [self.delta[pl.ds(at + i, 1), :] for i in range(chunk)], 1
+                            [self.line(at + i, 1) for i in range(chunk)], 1
                         ),
                         None,
                     )
@@ -317,14 +312,14 @@
         lax.fori_loop(0, self.count, step, 0)
 
 
-def own_kernel(unit, keyval, acc, dq, lse, delta):
+def own_kernel(unit, keyval, acc, dq, stat):
     def clear(b, carry):
         acc[b] = jnp.zeros(acc.shape[1:], jnp.float32)
         return carry
 
     count = dq.shape[0]
     lax.fori_loop(0, count, clear, 0)
-    own = Visitor(count, unit, lse, delta, dq, keyval, keyval, acc, values_at=count)
+    own = Visitor(count, unit, stat, dq, keyval, keyval, acc, values_at=count)
     own.begin()
     own.window()
 
@@ -349,7 +344,7 @@
     acc = refs.pop(0)
     outs = [refs.pop(0) for _ in offsets]
     sums = outs if first else [refs.pop(0) for _ in offsets]
-    lse, delta = (refs.pop(0), refs.pop(0))
+    stat = refs.pop(0)
     lists = refs
     if first:
 
@@ -373,7 +368,7 @@
     for v, offset in enumerate(offsets):
         guest = me + offset * span * side
         present = (guest >= 0) & (guest < shards)
-        visitor = Visitor(count, guests[v], lse, delta, sums[v], keys, values, acc, layout, lists)
+        visitor = Visitor(count, guests[v], stat, sums[v], keys, values, acc, layout, lists)
 
         @pl.when(present)
         def _(visitor=visitor, offset=offset, guest=guest, out=outs[v]):
@@ -451,7 +446,7 @@
             jax.ShapeDtypeStruct((count, 2, BLK, width), jnp.float32),
             jax.ShapeDtypeStruct((count, BLK, width), jnp.float32),
         ),
-        scratch_shapes=[stats, stats],
+        scratch_shapes=[stats],
         compiler_params=pltpu.CompilerParams(vmem_limit_bytes=LIMIT),
         name="own",
     )(unit, keyval)
@@ -551,7 +546,6 @@
             * (0 if first else len(units))
             + [
                 stats,
-                stats,
                 pltpu.SMEM((entries,), jnp.int32),
                 pltpu.SMEM((entries,), jnp.int32),
                 pltpu.SMEM((entries,), jnp.float32),

time: 96 us -> 95.3 us (level)
  transfers between devices with their start and end apart: 15 -> 15, of which waited for: 9 -> 9; matrix products, arithmetic and copies ran while one was open for 0% -> 0% of each run, Pallas kernels for 26% -> 25%
where the time goes in v6:
time: 95.3 us; the launch traced here: 94.9 us
  waiting for transfers between devices  45.9 us (48%)
  Pallas kernels  27.3 us (29%)
  starting transfers between devices  18.2 us (19%)
  local copies, waits for them, and re-layouts  2.34 us (2%)
    ppermute x15, waiting for transfers between devices, send(): return lax.ppermute(array, 'qb', pairs)  45.9 us
    ppermute x15, starting transfers between devices, send(): return lax.ppermute(array, 'qb', pairs)  18.2 us
    pallas_call x4, Pallas kernels, visit(): pl.pallas_call(functools.partial(visit_kernel, plan), out_shape=outs, in_...  17.9 us
    pallas_call x1, Pallas kernels, own_visit(): pl.pallas_call(own_kernel, out_shape=(jax.ShapeDtypeStruct((count, 2, BLK...  3.67 us
    unnamed x6, local copies, waits for them, and re-layouts  2.02 us
    pallas_call x1, Pallas kernels, pack(): pl.pallas_call(pack_kernel, out_shape=jax.ShapeDtypeStruct((2 * count * B...  2.01 us
  transfers between devices with their start and end apart: 15, of which 9 were waited for; matrix products, arithmetic and copies ran while one was open for 0% of the time, Pallas kernels for 25%

profile of v6, /device:TPU:0, one launch (start us, length us, event | category | flops | bytes accessed | tf_op | source)
XLA Modules:
  0.0 94.9 jit_solution(18368200673577383718)
XLA Ops:
  0.6 2.0 %pack.1.unit.refs_0_ = bf16[3120,128]{1,0:T(8,128)(2,1)S(1)} custom-call(bf16[1536,128]{1,0:T(8,128)(2,1)} %query.1, bf16[1536,128]{1,0:T(8,128)(2,1)} %grad.1, bf16[1536,128]{1,0:T(8,128)(2,1)} %output.1, f32[12,128]{1,0:T(8,128)} %bitcast.2), custom_call_target="tpu_custom_call" | custom-call | tf_op jit(solution)/shard_map/pack/pallas_call | solution.py:91
  2.7 0.0 copy-start.2
  2.7 3.1 %collective-permute-start = (bf16[3120,128]{1,0:T(8,128)(2,1)S(1)}, bf16[3120,128]{1,0:T(8,128)(2,1)}, u32[]{:S(2)}, u32[]{:S(2)}) collective-permute-start(bf16[3120,128]{1,0:T(8,128)(2,1)S(1)} %pack.1.unit.refs_0_), channel_id=1, source_target_pairs={{0,4},{1,5},{2,6},{3,7},{4,0},{5,1},{6,2},{7,3},{8,12},{9,13},{10,... | collective-permute-start | bytes 2396168 | tf_op jit(solution)/shard_map/ppermute | solution.py:576
  5.8 1.1 %join.1.keyval.refs_1_ = bf16[3072,128]{1,0:T(8,128)(2,1)S(1)} custom-call(bf16[1536,128]{1,0:T(8,128)(2,1)} %key.1, bf16[1536,128]{1,0:T(8,128)(2,1)} %value.1), custom_call_target="tpu_custom_call" | custom-call | tf_op jit(solution)/shard_map/join/pallas_call | solution.py:123
  6.9 1.6 %collective-permute-start.3 = (bf16[3072,128]{1,0:T(8,128)(2,1)S(1)}, bf16[3072,128]{1,0:T(8,128)(2,1)}, u32[]{:S(2)}, u32[]{:S(2)}) collective-permute-start(bf16[3072,128]{1,0:T(8,128)(2,1)S(1)} %join.1.keyval.refs_1_), channel_id=1, source_target_pairs={{0,2},{1,3},{2,0},{3,1},{4,6},{5,7},{6,4},{7,5},{8,10},{9,11},{10,... | collective-permute-start | bytes 2359304 | tf_op jit(solution)/shard_map/ppermute | solution.py:576
  8.4 1.6 %collective-permute-start.6 = (bf16[3120,128]{1,0:T(8,128)(2,1)S(1)}, bf16[3120,128]{1,0:T(8,128)(2,1)}, u32[]{:S(2)}, u32[]{:S(2)}) collective-permute-start(bf16[3120,128]{1,0:T(8,128)(2,1)S(1)} %pack.1.unit.refs_0_), channel_id=1, source_target_pairs={{4,8},{5,9},{6,10},{7,11},{8,4},{9,5},{10,6},{11,7},{20,24},{21,25... | collective-permute-start | bytes 2396168 | tf_op jit(solution)/shard_map/ppermute | solution.py:576
  10.1 3.7 %own.1 = (f32[12,2,128,128]{3,2,1,0:T(8,128)S(1)}, f32[12,128,128]{2,1,0:T(8,128)S(1)}) custom-call(bf16[3120,128]{1,0:T(8,128)(2,1)S(1)} %pack.1.unit.refs_0_, bf16[3072,128]{1,0:T(8,128)(2,1)S(1)} %join.1.keyval.refs_1_), custom_call_target="tpu_custom_call" | custom-call | tf_op jit(solution)/shard_map/own/pallas_call | solution.py:443
  13.7 0.9 copy-done
  14.6 9.0 %collective-permute-done.refs_0_ = bf16[3120,128]{1,0:T(8,128)(2,1)} collective-permute-done((bf16[3120,128]{1,0:T(8,128)(2,1)S(1)}, bf16[3120,128]{1,0:T(8,128)(2,1)}, u32[]{:S(2)}, u32[]{:S(2)}) %collective-permute-start) | collective-permute-done | bytes 798752 | tf_op jit(solution)/shard_map/ppermute | solution.py:576
  23.7 1.6 %collective-permute-start.1 = (bf16[3120,128]{1,0:T(8,128)(2,1)}, bf16[3120,128]{1,0:T(8,128)(2,1)}, u32[]{:S(2)}, u32[]{:S(2)}) collective-permute-start(bf16[3120,128]{1,0:T(8,128)(2,1)} %collective-permute-done.refs_0_), channel_id=1, source_target_pairs={{4,8},{5,9},{6,10},{7,11},{8,4},{9,5},{10,6},{11,7},{20,24},{21,25... | collective-permute-start | bytes 2396168 | tf_op jit(solution)/shard_map/ppermute | solution.py:576
  25.2 0.0 collective-permute-start.2
  25.2 0.8 collective-permute-done.3.refs_3_
  26.1 0.0 collective-permute-start.4
  26.1 0.0 collective-permute-done.6.refs_1_
  26.1 1.3 %collective-permute-start.7 = (bf16[3120,128]{1,0:T(8,128)(2,1)}, bf16[3120,128]{1,0:T(8,128)(2,1)}, u32[]{:S(2)}, u32[]{:S(2)}) collective-permute-start(bf16[3120,128]{1,0:T(8,128)(2,1)} %collective-permute-done.6.refs_1_), channel_id=1, source_target_pairs={{4,0},{5,1},{6,2},{7,3},{8,12},{9,13},{10,14},{11,15},{20,16},{21,... | collective-permute-start | bytes 2396168 | tf_op jit(solution)/shard_map/ppermute | solution.py:576
  27.4 0.1 pad_add_fusion.me_ref
  27.5 0.1 copy.13
  27.6 0.2 reshape.12.layout
  27.8 0.0 collective-permute-done.2.refs_2_
  27.8 1.2 %collective-permute-done.4.refs_4_ = bf16[3072,128]{1,0:T(8,128)(2,1)} collective-permute-done((bf16[3072,128]{1,0:T(8,128)(2,1)}, bf16[3072,128]{1,0:T(8,128)(2,1)}, u32[]{:S(2)}, u32[]{:S(2)}) %collective-permute-start.4) | collective-permute-done | bytes 786464 | tf_op jit(solution)/shard_map/ppermute | solution.py:576
  29.0 1.1 %copy-done.1 = f32[12,128,128]{2,1,0:T(8,128)S(1)} copy-done((f32[12,128,128]{2,1,0:T(8,128)S(1)}, f32[12,128,128]{2,1,0:T(8,128)}, u32[]{:S(2)}) %copy-start.1) | copy-done | bytes 786456
  30.1 5.5 %visit.4 = (bf16[6144,128]{1,0:T(8,128)(2,1)S(1)}, bf16[6144,128]{1,0:T(8,128)(2,1)S(1)}, f32[48,2,128,128]{3,2,1,0:T(8,128)S(1)}, f32[12,128,128]{2,1,0:T(8,128)S(1)}) custom-call(s32[2]{0:T(128)S(1)} %pad_add_fusion.me_ref, s32[576]{0:T(1024)S(1)} %reshape.12.layout, bf16[3120,128]{1,0:T(8,128)(2,1)S(1)} %pack.1.unit.refs_0_, ...), custom_call_target="tpu_custom_call" | custom-call | tf_op jit(solution)/shard_map/visit/pallas_call | solution.py:539
  35.6 0.0 collective-permute-done.1.refs_1_
  35.6 1.3 %collective-permute-start.5 = (bf16[3120,128]{1,0:T(8,128)(2,1)}, bf16[3120,128]{1,0:T(8,128)(2,1)S(1)}, u32[]{:S(2)}, u32[]{:S(2)}) collective-permute-start(bf16[3120,128]{1,0:T(8,128)(2,1)} %collective-permute-done.1.refs_1_), channel_id=1, source_target_pairs={{4,0},{5,1},{6,2},{7,3},{8,12},{9,13},{10,14},{11,15},{20,16},{21,... | collective-permute-start | bytes 2396168 | tf_op jit(solution)/shard_map/ppermute | solution.py:576
  36.9 12.3 %collective-permute-done.7.refs_0_ = bf16[3120,128]{1,0:T(8,128)(2,1)} collective-permute-done((bf16[3120,128]{1,0:T(8,128)(2,1)}, bf16[3120,128]{1,0:T(8,128)(2,1)}, u32[]{:S(2)}, u32[]{:S(2)}) %collective-permute-start.7) | collective-permute-done | bytes 798752 | tf_op jit(solution)/shard_map/ppermute | solution.py:576
  49.2 4.6 %visit.5 = (f32[48,2,128,128]{3,2,1,0:T(8,128)S(1)}, bf16[12,128,128]{2,1,0:T(8,128)(2,1)S(1)}, bf16[12,128,128]{2,1,0:T(8,128)(2,1)S(1)}) custom-call(s32[2]{0:T(128)S(1)} %pad_add_fusion.me_ref, s32[576]{0:T(1024)S(1)} %reshape.12.layout, bf16[3120,128]{1,0:T(8,128)(2,1)} %collective-permute-done.refs_0_, ...), custom_call_target="tpu_custom_call", output_to_operand_aliasing={{0}: (6, {})} | custom-call | tf_op jit(solution)/shard_map/visit/pallas_call | solution.py:539
  53.8 4.0 %visit.6 = (f32[48,2,128,128]{3,2,1,0:T(8,128)S(1)}, bf16[12,128,128]{2,1,0:T(8,128)(2,1)S(1)}, bf16[12,128,128]{2,1,0:T(8,128)(2,1)S(1)}) custom-call(s32[2]{0:T(128)S(1)} %pad_add_fusion.me_ref, s32[576]{0:T(1024)S(1)} %reshape.12.layout, bf16[3120,128]{1,0:T(8,128)(2,1)} %collective-permute-done.7.refs_0_, ...), custom_call_target="tpu_custom_call", output_to_operand_aliasing={{0}: (6, {})} | custom-call | tf_op jit(solution)/shard_map/visit/pallas_call | solution.py:539
  57.8 2.0 %collective-permute-start.8 = (bf16[12,128,128]{2,1,0:T(8,128)(2,1)S(1)}, bf16[12,128,128]{2,1,0:T(8,128)(2,1)S(1)}, u32[]{:S(2)}, u32[]{:S(2)}) collective-permute-start(bf16[12,128,128]{2,1,0:T(8,128)(2,1)S(1)} %get-tuple-element.49), channel_id=1, source_target_pairs={{0,4},{1,5},{2,6},{3,7},{12,8},{13,9},{14,10},{15,11},{16,20},{17,... | collective-permute-start | bytes 1179656 | tf_op jit(solution)/shard_map/ppermute | solution.py:576
  59.8 0.7 collective-permute-start.9
  60.5 5.6 %collective-permute-done.5.refs_0_ = bf16[3120,128]{1,0:T(8,128)(2,1)S(1)} collective-permute-done((bf16[3120,128]{1,0:T(8,128)(2,1)}, bf16[3120,128]{1,0:T(8,128)(2,1)S(1)}, u32[]{:S(2)}, u32[]{:S(2)}) %collective-permute-start.5) | collective-permute-done | bytes 798752 | tf_op jit(solution)/shard_map/ppermute | solution.py:576
  66.2 3.8 %visit.7 = (f32[48,2,128,128]{3,2,1,0:T(8,128)S(1)}, bf16[12,128,128]{2,1,0:T(8,128)(2,1)S(1)}) custom-call(s32[2]{0:T(128)S(1)} %pad_add_fusion.me_ref, s32[576]{0:T(1024)S(1)} %reshape.12.layout, bf16[3120,128]{1,0:T(8,128)(2,1)S(1)} %collective-permute-done.5.refs_0_, ...), custom_call_target="tpu_custom_call", output_to_operand_aliasing={{0}: (5, {})} | custom-call | flops 5033164800 | tf_op jit(solution)/shard_map/visit/pallas_call | solution.py:539
  70.0 0.0 collective-permute-done.8
  70.0 0.0 collective-permute-done.9
  70.0 0.2 add_convert_fusion
  70.2 0.2 share.2
  70.5 0.1 collective-permute-start.10
  70.6 0.1 collective-permute-start.12
  70.6 0.7 collective-permute-start.13
  71.3 2.6 %collective-permute-done.10.refs_0_ = bf16[2,2,12,128,128]{4,3,2,1,0:T(8,128)(2,1)S(1)} collective-permute-done((bf16[2,2,12,128,128]{4,3,2,1,0:T(8,128)(2,1)S(1)}, bf16[2,2,12,128,128]{4,3,2,1,0:T(8,128)(2,1)S(1)}, u32[]{:S(2)}, u32[]{:S(2)}) %collective-permute-start.10) | collective-permute-done | bytes 1572896 | tf_op jit(solution)/shard_map/ppermute | solution.py:576
  74.0 0.3 share.3
  74.2 1.6 %collective-permute-start.11 = (bf16[2,1,12,128,128]{4,3,2,1,0:T(8,128)(2,1)S(1)}, bf16[2,1,12,128,128]{4,3,2,1,0:T(8,128)(2,1)S(1)}, u32[]{:S(2)}, u32[]{:S(2)}) collective-permute-start(bf16[2,1,12,128,128]{4,3,2,1,0:T(8,128)(2,1)S(1)} %share.3), channel_id=1, source_target_pairs={{0,2},{1,3},{2,0},{3,1},{4,6},{5,7},{6,4},{7,5},{8,10},{9,11},{10,... | collective-permute-start | bytes 2359304 | tf_op jit(solution)/shard_map/ppermute | solution.py:576
  75.8 2.7 %collective-permute-start.14 = (bf16[12,128,128]{2,1,0:T(8,128)(2,1)S(1)}, bf16[12,128,128]{2,1,0:T(8,128)(2,1)S(1)}, u32[]{:S(2)}, u32[]{:S(2)}) collective-permute-start(bf16[12,128,128]{2,1,0:T(8,128)(2,1)S(1)} %get-tuple-element.59), channel_id=1, source_target_pairs={{12,0},{13,1},{14,2},{15,3},{0,12},{1,13},{2,14},{3,15},{28,16},{2... | collective-permute-start | bytes 1179656 | tf_op jit(solution)/shard_map/ppermute | solution.py:576
  78.5 3.8 %collective-permute-done.12.refs_0_ = bf16[12,128,128]{2,1,0:T(8,128)(2,1)S(1)} collective-permute-done((bf16[12,128,128]{2,1,0:T(8,128)(2,1)S(1)}, bf16[12,128,128]{2,1,0:T(8,128)(2,1)S(1)}, u32[]{:S(2)}, u32[]{:S(2)}) %collective-permute-start.12) | collective-permute-done | bytes 393248 | tf_op jit(solution)/shard_map/ppermute | solution.py:576
  82.3 0.1 add.30.base
  82.5 8.1 %collective-permute-done.14.refs_0_ = bf16[12,128,128]{2,1,0:T(8,128)(2,1)S(1)} collective-permute-done((bf16[12,128,128]{2,1,0:T(8,128)(2,1)S(1)}, bf16[12,128,128]{2,1,0:T(8,128)(2,1)S(1)}, u32[]{:S(2)}, u32[]{:S(2)}) %collective-permute-start.14) | collective-permute-done | bytes 393248 | tf_op jit(solution)/shard_map/ppermute | solution.py:576
  90.5 0.9 add.31
  91.4 2.5 %collective-permute-done.11.refs_1_ = bf16[2,1,12,128,128]{4,3,2,1,0:T(8,128)(2,1)S(1)} collective-permute-done((bf16[2,1,12,128,128]{4,3,2,1,0:T(8,128)(2,1)S(1)}, bf16[2,1,12,128,128]{4,3,2,1,0:T(8,128)(2,1)S(1)}, u32[]{:S(2)}, u32[]{:S(2)}) %collective-permute-start.11) | collective-permute-done | bytes 786464 | tf_op jit(solution)/shard_map/ppermute | solution.py:576
  93.9 1.1 %finish.1 = (bf16[1536,128]{1,0:T(8,128)(2,1)}, bf16[1536,128]{1,0:T(8,128)(2,1)}) custom-call(f32[48,2,128,128]{3,2,1,0:T(8,128)S(1)} %get-tuple-element.55.acc, bf16[2,2,12,128,128]{4,3,2,1,0:T(8,128)(2,1)S(1)} %collective-permute-done.10.refs_0_, bf16[2,1,12,128,128]{4,3,2,1,0:T(8,128)(2,1)S(1)} %collective-permute-done.11.refs_1_), custom_call_target="tpu_custom_call" | custom-call | tf_op jit(solution)/shard_map/finish/pallas_call | solution.py:472
  (5 shorter events, 0.0 us)
Async XLA Ops:
  2.7 23.4 %copy-start.2 = (s32[192,3]{0,1:T(4,128)S(1)}, s32[192,3]{0,1:T(4,128)}, u32[]{:S(2)}) copy-start(s32[192,3]{0,1:T(4,128)} %param.13) | copy-start | bytes 6916
  2.7 21.0 %collective-permute-start = (bf16[3120,128]{1,0:T(8,128)(2,1)S(1)}, bf16[3120,128]{1,0:T(8,128)(2,1)}, u32[]{:S(2)}, u32[]{:S(2)}) collective-permute-start(bf16[3120,128]{1,0:T(8,128)(2,1)S(1)} %pack.1.unit.refs_0_), channel_id=1, source_target_pairs={{0,4},{1,5},{2,6},{3,7},{4,0},{5,1},{6,2},{7,3},{8,12},{9,13},{10,... | collective-permute-start | bytes 2396168 | tf_op jit(solution)/shard_map/ppermute | solution.py:576
  6.9 19.2 %collective-permute-start.3 = (bf16[3072,128]{1,0:T(8,128)(2,1)S(1)}, bf16[3072,128]{1,0:T(8,128)(2,1)}, u32[]{:S(2)}, u32[]{:S(2)}) collective-permute-start(bf16[3072,128]{1,0:T(8,128)(2,1)S(1)} %join.1.keyval.refs_1_), channel_id=1, source_target_pairs={{0,2},{1,3},{2,0},{3,1},{4,6},{5,7},{6,4},{7,5},{8,10},{9,11},{10,... | collective-permute-start | bytes 2359304 | tf_op jit(solution)/shard_map/ppermute | solution.py:576
  8.4 17.6 %collective-permute-start.6 = (bf16[3120,128]{1,0:T(8,128)(2,1)S(1)}, bf16[3120,128]{1,0:T(8,128)(2,1)}, u32[]{:S(2)}, u32[]{:S(2)}) collective-permute-start(bf16[3120,128]{1,0:T(8,128)(2,1)S(1)} %pack.1.unit.refs_0_), channel_id=1, source_target_pairs={{4,8},{5,9},{6,10},{7,11},{8,4},{9,5},{10,6},{11,7},{20,24},{21,25... | collective-permute-start | bytes 2396168 | tf_op jit(solution)/shard_map/ppermute | solution.py:576
  13.7 0.9 copy-start
  23.7 11.9 %collective-permute-start.1 = (bf16[3120,128]{1,0:T(8,128)(2,1)}, bf16[3120,128]{1,0:T(8,128)(2,1)}, u32[]{:S(2)}, u32[]{:S(2)}) collective-permute-start(bf16[3120,128]{1,0:T(8,128)(2,1)} %collective-permute-done.refs_0_), channel_id=1, source_target_pairs={{4,8},{5,9},{6,10},{7,11},{8,4},{9,5},{10,6},{11,7},{20,24},{21,25... | collective-permute-start | bytes 2396168 | tf_op jit(solution)/shard_map/ppermute | solution.py:576
  25.2 2.6 %collective-permute-start.2 = (bf16[3072,128]{1,0:T(8,128)(2,1)S(1)}, bf16[3072,128]{1,0:T(8,128)(2,1)}, u32[]{:S(2)}, u32[]{:S(2)}) collective-permute-start(bf16[3072,128]{1,0:T(8,128)(2,1)S(1)} %join.1.keyval.refs_1_), channel_id=1, source_target_pairs={{0,1},{1,0},{2,3},{3,2},{4,5},{5,4},{6,7},{7,6},{8,9},{9,8},{10,11... | collective-permute-start | bytes 2359304 | tf_op jit(solution)/shard_map/ppermute | solution.py:576
  26.1 2.9 %collective-permute-start.4 = (bf16[3072,128]{1,0:T(8,128)(2,1)}, bf16[3072,128]{1,0:T(8,128)(2,1)}, u32[]{:S(2)}, u32[]{:S(2)}) collective-permute-start(bf16[3072,128]{1,0:T(8,128)(2,1)} %collective-permute-done.3.refs_3_), channel_id=1, source_target_pairs={{0,1},{1,0},{2,3},{3,2},{4,5},{5,4},{6,7},{7,6},{8,9},{9,8},{10,11... | collective-permute-start | bytes 2359304 | tf_op jit(solution)/shard_map/ppermute | solution.py:576
  26.1 23.1 %collective-permute-start.7 = (bf16[3120,128]{1,0:T(8,128)(2,1)}, bf16[3120,128]{1,0:T(8,128)(2,1)}, u32[]{:S(2)}, u32[]{:S(2)}) collective-permute-start(bf16[3120,128]{1,0:T(8,128)(2,1)} %collective-permute-done.6.refs_1_), channel_id=1, source_target_pairs={{4,0},{5,1},{6,2},{7,3},{8,12},{9,13},{10,14},{11,15},{20,16},{21,... | collective-permute-start | bytes 2396168 | tf_op jit(solution)/shard_map/ppermute | solution.py:576
  29.0 1.1 %copy-start.1 = (f32[12,128,128]{2,1,0:T(8,128)S(1)}, f32[12,128,128]{2,1,0:T(8,128)}, u32[]{:S(2)}) copy-start(f32[12,128,128]{2,1,0:T(8,128)} %copy-done) | copy-start | bytes 2359300
  35.6 30.5 %collective-permute-start.5 = (bf16[3120,128]{1,0:T(8,128)(2,1)}, bf16[3120,128]{1,0:T(8,128)(2,1)S(1)}, u32[]{:S(2)}, u32[]{:S(2)}) collective-permute-start(bf16[3120,128]{1,0:T(8,128)(2,1)} %collective-permute-done.1.refs_1_), channel_id=1, source_target_pairs={{4,0},{5,1},{6,2},{7,3},{8,12},{9,13},{10,14},{11,15},{20,16},{21,... | collective-permute-start | bytes 2396168 | tf_op jit(solution)/shard_map/ppermute | solution.py:576
  57.8 12.1 %collective-permute-start.8 = (bf16[12,128,128]{2,1,0:T(8,128)(2,1)S(1)}, bf16[12,128,128]{2,1,0:T(8,128)(2,1)S(1)}, u32[]{:S(2)}, u32[]{:S(2)}) collective-permute-start(bf16[12,128,128]{2,1,0:T(8,128)(2,1)S(1)} %get-tuple-element.49), channel_id=1, source_target_pairs={{0,4},{1,5},{2,6},{3,7},{12,8},{13,9},{14,10},{15,11},{16,20},{17,... | collective-permute-start | bytes 1179656 | tf_op jit(solution)/shard_map/ppermute | solution.py:576
  59.8 10.1 %collective-permute-start.9 = (bf16[12,128,128]{2,1,0:T(8,128)(2,1)S(1)}, bf16[12,128,128]{2,1,0:T(8,128)(2,1)S(1)}, u32[]{:S(2)}, u32[]{:S(2)}) collective-permute-start(bf16[12,128,128]{2,1,0:T(8,128)(2,1)S(1)} %get-tuple-element.50), channel_id=1, source_target_pairs={{8,4},{9,5},{10,6},{11,7},{4,8},{5,9},{6,10},{7,11},{24,20},{25,21... | collective-permute-start | bytes 1179656 | tf_op jit(solution)/shard_map/ppermute | solution.py:576
  70.5 3.5 %collective-permute-start.10 = (bf16[2,2,12,128,128]{4,3,2,1,0:T(8,128)(2,1)S(1)}, bf16[2,2,12,128,128]{4,3,2,1,0:T(8,128)(2,1)S(1)}, u32[]{:S(2)}, u32[]{:S(2)}) collective-permute-start(bf16[2,2,12,128,128]{4,3,2,1,0:T(8,128)(2,1)S(1)} %share.2), channel_id=1, source_target_pairs={{0,1},{1,0},{2,3},{3,2},{4,5},{5,4},{6,7},{7,6},{8,9},{9,8},{10,11... | collective-permute-start | bytes 4718600 | tf_op jit(solution)/shard_map/ppermute | solution.py:576
  70.6 11.7 %collective-permute-start.12 = (bf16[12,128,128]{2,1,0:T(8,128)(2,1)S(1)}, bf16[12,128,128]{2,1,0:T(8,128)(2,1)S(1)}, u32[]{:S(2)}, u32[]{:S(2)}) collective-permute-start(bf16[12,128,128]{2,1,0:T(8,128)(2,1)S(1)} %get-tuple-element.57), channel_id=1, source_target_pairs={{4,0},{5,1},{6,2},{7,3},{0,4},{1,5},{2,6},{3,7},{12,8},{13,9},{14,... | collective-permute-start | bytes 1179656 | tf_op jit(solution)/shard_map/ppermute | solution.py:576
  70.6 11.7 %collective-permute-start.13 = (bf16[12,128,128]{2,1,0:T(8,128)(2,1)S(1)}, bf16[12,128,128]{2,1,0:T(8,128)(2,1)S(1)}, u32[]{:S(2)}, u32[]{:S(2)}) collective-permute-start(bf16[12,128,128]{2,1,0:T(8,128)(2,1)S(1)} %get-tuple-element.58), channel_id=1, source_target_pairs={{8,4},{9,5},{10,6},{11,7},{4,8},{5,9},{6,10},{7,11},{24,20},{25,21... | collective-permute-start | bytes 1179656 | tf_op jit(solution)/shard_map/ppermute | solution.py:576
  74.2 19.6 %collective-permute-start.11 = (bf16[2,1,12,128,128]{4,3,2,1,0:T(8,128)(2,1)S(1)}, bf16[2,1,12,128,128]{4,3,2,1,0:T(8,128)(2,1)S(1)}, u32[]{:S(2)}, u32[]{:S(2)}) collective-permute-start(bf16[2,1,12,128,128]{4,3,2,1,0:T(8,128)(2,1)S(1)} %share.3), channel_id=1, source_target_pairs={{0,2},{1,3},{2,0},{3,1},{4,6},{5,7},{6,4},{7,5},{8,10},{9,11},{10,... | collective-permute-start | bytes 2359304 | tf_op jit(solution)/shard_map/ppermute | solution.py:576
  75.8 14.7 %collective-permute-start.14 = (bf16[12,128,128]{2,1,0:T(8,128)(2,1)S(1)}, bf16[12,128,128]{2,1,0:T(8,128)(2,1)S(1)}, u32[]{:S(2)}, u32[]{:S(2)}) collective-permute-start(bf16[12,128,128]{2,1,0:T(8,128)(2,1)S(1)} %get-tuple-element.59), channel_id=1, source_target_pairs={{12,0},{13,1},{14,2},{15,3},{0,12},{1,13},{2,14},{3,15},{28,16},{2... | collective-permute-start | bytes 1179656 | tf_op jit(solution)/shard_map/ppermute | solution.py:576

commit v7 on v6

--- a/solution.py
+++ b/solution.py
@@ -11,8 +11,8 @@
 GLOB = 2
 TILE = 16
 CODE = 256
-PAIRS = 6
-TURNS = 3
+PAIRS = 5
+TURNS = 6
 FAR = 1e30
 COST = 20
 LIMIT = 16 * 2**20
@@ -32,7 +32,7 @@
 
 
 def groups_of(count):
-    return next(groups for groups in (3, 4, 2, 1) if count % groups == 0)
+    return next(groups for groups in (2, 3, 1) if count % groups == 0)
 
 
 def pack_kernel(query, grad, output, lse_hbm, unit, output_s, lse, delta_s, stat_s, sems):
@@ -273,14 +273,17 @@
             far[at] = 0.0
             return at + hit.astype(jnp.int32)
 
-        def gather(q, at):
-            entry = (guest * count + q) * fanout
-            for r in range(fanout):
-                code = self.layout[entry + r]
-                at = note(at, q, lax.shift_right_logical(code, CODE.bit_length() - 1), code & (CODE - 1))
+        group = count // groups_of(count)
+
+        def gather(g, at):
+            first = (guest * count + g * group) * fanout
+            codes = [self.layout[first + k] for k in range(group * fanout)]
+            for k, code in enumerate(codes):
+                owner = lax.shift_right_logical(code, CODE.bit_length() - 1)
+                at = note(at, g * group + k // fanout, owner, code & (CODE - 1))
             return at
 
-        found = lax.fori_loop(0, count, gather, 0)
+        found = lax.fori_loop(0, count // group, gather, 0)
         if near:
             found = note(found, 0, guest - 1, count - 1)
             found = note(found, count - 1, guest + 1, 0)

time: 95.3 us -> 95.1 us (level)
  Pallas kernels: 27.3 us -> 26.2 us
    pallas_call x4, Pallas kernels: 17.9 us -> 16.9 us  [visit(): pl.pallas_call(functools.partial(visit_kernel, plan), out_shape=outs, in_...]
  transfers between devices with their start and end apart: 15 -> 15, of which waited for: 9 -> 9; matrix products, arithmetic and copies ran while one was open for 0% -> 0% of each run, Pallas kernels for 25% -> 24%
where the time goes in v7:
time: 95.1 us; the launch traced here: 94.4 us
  waiting for transfers between devices  45.9 us (48%)
  Pallas kernels  26.2 us (28%)
  starting transfers between devices  18.7 us (20%)
  local copies, waits for them, and re-layouts  2.34 us (2%)
    ppermute x15, waiting for transfers between devices, send(): return lax.ppermute(array, 'qb', pairs)  45.9 us
    ppermute x15, starting transfers between devices, send(): return lax.ppermute(array, 'qb', pairs)  18.7 us
    pallas_call x4, Pallas kernels, visit(): pl.pallas_call(functools.partial(visit_kernel, plan), out_shape=outs, in_...  16.9 us
    pallas_call x1, Pallas kernels, own_visit(): pl.pallas_call(own_kernel, out_shape=(jax.ShapeDtypeStruct((count, 2, BLK...  3.67 us
    unnamed x6, local copies, waits for them, and re-layouts  2.02 us
  transfers between devices with their start and end apart: 15, of which 9 were waited for; matrix products, arithmetic and copies ran while one was open for 0% of the time, Pallas kernels for 24%

profile of v7, /device:TPU:0, one launch (start us, length us, event | category | flops | bytes accessed | tf_op | source)
XLA Modules:
  0.0 94.4 jit_solution(4827155179471548629)
XLA Ops:
  0.6 1.9 %pack.1.unit.refs_0_ = bf16[3120,128]{1,0:T(8,128)(2,1)S(1)} custom-call(bf16[1536,128]{1,0:T(8,128)(2,1)} %query.1, bf16[1536,128]{1,0:T(8,128)(2,1)} %grad.1, bf16[1536,128]{1,0:T(8,128)(2,1)} %output.1, f32[12,128]{1,0:T(8,128)} %bitcast.2), custom_call_target="tpu_custom_call" | custom-call | tf_op jit(solution)/shard_map/pack/pallas_call | solution.py:91
  2.5 0.0 copy-start.2
  2.5 3.1 %collective-permute-start = (bf16[3120,128]{1,0:T(8,128)(2,1)S(1)}, bf16[3120,128]{1,0:T(8,128)(2,1)}, u32[]{:S(2)}, u32[]{:S(2)}) collective-permute-start(bf16[3120,128]{1,0:T(8,128)(2,1)S(1)} %pack.1.unit.refs_0_), channel_id=1, source_target_pairs={{0,4},{1,5},{2,6},{3,7},{4,0},{5,1},{6,2},{7,3},{8,12},{9,13},{10,... | collective-permute-start | bytes 2396168 | tf_op jit(solution)/shard_map/ppermute | solution.py:579
  5.6 1.1 %join.1.keyval.refs_1_ = bf16[3072,128]{1,0:T(8,128)(2,1)S(1)} custom-call(bf16[1536,128]{1,0:T(8,128)(2,1)} %key.1, bf16[1536,128]{1,0:T(8,128)(2,1)} %value.1), custom_call_target="tpu_custom_call" | custom-call | tf_op jit(solution)/shard_map/join/pallas_call | solution.py:123
  6.8 1.6 %collective-permute-start.3 = (bf16[3072,128]{1,0:T(8,128)(2,1)S(1)}, bf16[3072,128]{1,0:T(8,128)(2,1)}, u32[]{:S(2)}, u32[]{:S(2)}) collective-permute-start(bf16[3072,128]{1,0:T(8,128)(2,1)S(1)} %join.1.keyval.refs_1_), channel_id=1, source_target_pairs={{0,2},{1,3},{2,0},{3,1},{4,6},{5,7},{6,4},{7,5},{8,10},{9,11},{10,... | collective-permute-start | bytes 2359304 | tf_op jit(solution)/shard_map/ppermute | solution.py:579
  8.3 1.6 %collective-permute-start.6 = (bf16[3120,128]{1,0:T(8,128)(2,1)S(1)}, bf16[3120,128]{1,0:T(8,128)(2,1)}, u32[]{:S(2)}, u32[]{:S(2)}) collective-permute-start(bf16[3120,128]{1,0:T(8,128)(2,1)S(1)} %pack.1.unit.refs_0_), channel_id=1, source_target_pairs={{4,8},{5,9},{6,10},{7,11},{8,4},{9,5},{10,6},{11,7},{20,24},{21,25... | collective-permute-start | bytes 2396168 | tf_op jit(solution)/shard_map/ppermute | solution.py:579
  9.9 3.7 %own.1 = (f32[12,2,128,128]{3,2,1,0:T(8,128)S(1)}, f32[12,128,128]{2,1,0:T(8,128)S(1)}) custom-call(bf16[3120,128]{1,0:T(8,128)(2,1)S(1)} %pack.1.unit.refs_0_, bf16[3072,128]{1,0:T(8,128)(2,1)S(1)} %join.1.keyval.refs_1_), custom_call_target="tpu_custom_call" | custom-call | tf_op jit(solution)/shard_map/own/pallas_call | solution.py:446
  13.6 0.9 copy-done
  14.5 9.0 %collective-permute-done.refs_0_ = bf16[3120,128]{1,0:T(8,128)(2,1)} collective-permute-done((bf16[3120,128]{1,0:T(8,128)(2,1)S(1)}, bf16[3120,128]{1,0:T(8,128)(2,1)}, u32[]{:S(2)}, u32[]{:S(2)}) %collective-permute-start) | collective-permute-done | bytes 798752 | tf_op jit(solution)/shard_map/ppermute | solution.py:579
  23.5 1.6 %collective-permute-start.1 = (bf16[3120,128]{1,0:T(8,128)(2,1)}, bf16[3120,128]{1,0:T(8,128)(2,1)}, u32[]{:S(2)}, u32[]{:S(2)}) collective-permute-start(bf16[3120,128]{1,0:T(8,128)(2,1)} %collective-permute-done.refs_0_), channel_id=1, source_target_pairs={{4,8},{5,9},{6,10},{7,11},{8,4},{9,5},{10,6},{11,7},{20,24},{21,25... | collective-permute-start | bytes 2396168 | tf_op jit(solution)/shard_map/ppermute | solution.py:579
  25.1 0.0 collective-permute-start.2
  25.1 0.8 collective-permute-done.3.refs_3_
  25.9 0.0 collective-permute-start.4
  25.9 0.0 collective-permute-done.6.refs_1_
  26.0 1.3 %collective-permute-start.7 = (bf16[3120,128]{1,0:T(8,128)(2,1)}, bf16[3120,128]{1,0:T(8,128)(2,1)}, u32[]{:S(2)}, u32[]{:S(2)}) collective-permute-start(bf16[3120,128]{1,0:T(8,128)(2,1)} %collective-permute-done.6.refs_1_), channel_id=1, source_target_pairs={{4,0},{5,1},{6,2},{7,3},{8,12},{9,13},{10,14},{11,15},{20,16},{21,... | collective-permute-start | bytes 2396168 | tf_op jit(solution)/shard_map/ppermute | solution.py:579
  27.3 0.1 pad_add_fusion.me_ref
  27.3 0.1 copy.13
  27.5 0.2 reshape.12.layout
  27.7 0.0 collective-permute-done.2.refs_2_
  27.7 1.2 %collective-permute-done.4.refs_4_ = bf16[3072,128]{1,0:T(8,128)(2,1)} collective-permute-done((bf16[3072,128]{1,0:T(8,128)(2,1)}, bf16[3072,128]{1,0:T(8,128)(2,1)}, u32[]{:S(2)}, u32[]{:S(2)}) %collective-permute-start.4) | collective-permute-done | bytes 786464 | tf_op jit(solution)/shard_map/ppermute | solution.py:579
  28.8 1.1 %copy-done.1 = f32[12,128,128]{2,1,0:T(8,128)S(1)} copy-done((f32[12,128,128]{2,1,0:T(8,128)S(1)}, f32[12,128,128]{2,1,0:T(8,128)}, u32[]{:S(2)}) %copy-start.1) | copy-done | bytes 786456
  30.0 5.1 %visit.4 = (bf16[6144,128]{1,0:T(8,128)(2,1)S(1)}, bf16[6144,128]{1,0:T(8,128)(2,1)S(1)}, f32[48,2,128,128]{3,2,1,0:T(8,128)S(1)}, f32[12,128,128]{2,1,0:T(8,128)S(1)}) custom-call(s32[2]{0:T(128)S(1)} %pad_add_fusion.me_ref, s32[576]{0:T(1024)S(1)} %reshape.12.layout, bf16[3120,128]{1,0:T(8,128)(2,1)S(1)} %pack.1.unit.refs_0_, ...), custom_call_target="tpu_custom_call" | custom-call | tf_op jit(solution)/shard_map/visit/pallas_call | solution.py:542
  35.1 1.3 %collective-permute-start.5 = (bf16[3120,128]{1,0:T(8,128)(2,1)}, bf16[3120,128]{1,0:T(8,128)(2,1)S(1)}, u32[]{:S(2)}, u32[]{:S(2)}) collective-permute-start(bf16[3120,128]{1,0:T(8,128)(2,1)} %collective-permute-done.1.refs_1_), channel_id=1, source_target_pairs={{4,0},{5,1},{6,2},{7,3},{8,12},{9,13},{10,14},{11,15},{20,16},{21,... | collective-permute-start | bytes 2396168 | tf_op jit(solution)/shard_map/ppermute | solution.py:579
  36.4 12.7 %collective-permute-done.7.refs_0_ = bf16[3120,128]{1,0:T(8,128)(2,1)} collective-permute-done((bf16[3120,128]{1,0:T(8,128)(2,1)}, bf16[3120,128]{1,0:T(8,128)(2,1)}, u32[]{:S(2)}, u32[]{:S(2)}) %collective-permute-start.7) | collective-permute-done | bytes 798752 | tf_op jit(solution)/shard_map/ppermute | solution.py:579
  49.0 4.2 %visit.5 = (f32[48,2,128,128]{3,2,1,0:T(8,128)S(1)}, bf16[12,128,128]{2,1,0:T(8,128)(2,1)S(1)}, bf16[12,128,128]{2,1,0:T(8,128)(2,1)S(1)}) custom-call(s32[2]{0:T(128)S(1)} %pad_add_fusion.me_ref, s32[576]{0:T(1024)S(1)} %reshape.12.layout, bf16[3120,128]{1,0:T(8,128)(2,1)} %collective-permute-done.refs_0_, ...), custom_call_target="tpu_custom_call", output_to_operand_aliasing={{0}: (6, {})} | custom-call | tf_op jit(solution)/shard_map/visit/pallas_call | solution.py:542
  53.3 4.2 %visit.6 = (f32[48,2,128,128]{3,2,1,0:T(8,128)S(1)}, bf16[12,128,128]{2,1,0:T(8,128)(2,1)S(1)}, bf16[12,128,128]{2,1,0:T(8,128)(2,1)S(1)}) custom-call(s32[2]{0:T(128)S(1)} %pad_add_fusion.me_ref, s32[576]{0:T(1024)S(1)} %reshape.12.layout, bf16[3120,128]{1,0:T(8,128)(2,1)} %collective-permute-done.7.refs_0_, ...), custom_call_target="tpu_custom_call", output_to_operand_aliasing={{0}: (6, {})} | custom-call | tf_op jit(solution)/shard_map/visit/pallas_call | solution.py:542
  57.5 1.7 %collective-permute-start.8 = (bf16[12,128,128]{2,1,0:T(8,128)(2,1)S(1)}, bf16[12,128,128]{2,1,0:T(8,128)(2,1)S(1)}, u32[]{:S(2)}, u32[]{:S(2)}) collective-permute-start(bf16[12,128,128]{2,1,0:T(8,128)(2,1)S(1)} %get-tuple-element.49), channel_id=1, source_target_pairs={{0,4},{1,5},{2,6},{3,7},{12,8},{13,9},{14,10},{15,11},{16,20},{17,... | collective-permute-start | bytes 1179656 | tf_op jit(solution)/shard_map/ppermute | solution.py:579
  59.2 0.7 collective-permute-start.9
  59.9 6.1 %collective-permute-done.5.refs_0_ = bf16[3120,128]{1,0:T(8,128)(2,1)S(1)} collective-permute-done((bf16[3120,128]{1,0:T(8,128)(2,1)}, bf16[3120,128]{1,0:T(8,128)(2,1)S(1)}, u32[]{:S(2)}, u32[]{:S(2)}) %collective-permute-start.5) | collective-permute-done | bytes 798752 | tf_op jit(solution)/shard_map/ppermute | solution.py:579
  66.0 3.4 %visit.7 = (f32[48,2,128,128]{3,2,1,0:T(8,128)S(1)}, bf16[12,128,128]{2,1,0:T(8,128)(2,1)S(1)}) custom-call(s32[2]{0:T(128)S(1)} %pad_add_fusion.me_ref, s32[576]{0:T(1024)S(1)} %reshape.12.layout, bf16[3120,128]{1,0:T(8,128)(2,1)S(1)} %collective-permute-done.5.refs_0_, ...), custom_call_target="tpu_custom_call", output_to_operand_aliasing={{0}: (5, {})} | custom-call | flops 5033164800 | tf_op jit(solution)/shard_map/visit/pallas_call | solution.py:542
  69.4 0.0 collective-permute-done.8
  69.4 0.0 collective-permute-done.9
  69.4 0.2 add_convert_fusion
  69.7 0.2 share.2
  69.9 0.1 collective-permute-start.10
  70.0 0.7 collective-permute-start.12
  70.8 0.7 collective-permute-start.13
  71.4 2.0 %collective-permute-done.10.refs_0_ = bf16[2,2,12,128,128]{4,3,2,1,0:T(8,128)(2,1)S(1)} collective-permute-done((bf16[2,2,12,128,128]{4,3,2,1,0:T(8,128)(2,1)S(1)}, bf16[2,2,12,128,128]{4,3,2,1,0:T(8,128)(2,1)S(1)}, u32[]{:S(2)}, u32[]{:S(2)}) %collective-permute-start.10) | collective-permute-done | bytes 1572896 | tf_op jit(solution)/shard_map/ppermute | solution.py:579
  73.4 0.3 share.3
  73.7 1.5 %collective-permute-start.11 = (bf16[2,1,12,128,128]{4,3,2,1,0:T(8,128)(2,1)S(1)}, bf16[2,1,12,128,128]{4,3,2,1,0:T(8,128)(2,1)S(1)}, u32[]{:S(2)}, u32[]{:S(2)}) collective-permute-start(bf16[2,1,12,128,128]{4,3,2,1,0:T(8,128)(2,1)S(1)} %share.3), channel_id=1, source_target_pairs={{0,2},{1,3},{2,0},{3,1},{4,6},{5,7},{6,4},{7,5},{8,10},{9,11},{10,... | collective-permute-start | bytes 2359304 | tf_op jit(solution)/shard_map/ppermute | solution.py:579
  75.2 3.0 %collective-permute-start.14 = (bf16[12,128,128]{2,1,0:T(8,128)(2,1)S(1)}, bf16[12,128,128]{2,1,0:T(8,128)(2,1)S(1)}, u32[]{:S(2)}, u32[]{:S(2)}) collective-permute-start(bf16[12,128,128]{2,1,0:T(8,128)(2,1)S(1)} %get-tuple-element.59), channel_id=1, source_target_pairs={{12,0},{13,1},{14,2},{15,3},{0,12},{1,13},{2,14},{3,15},{28,16},{2... | collective-permute-start | bytes 1179656 | tf_op jit(solution)/shard_map/ppermute | solution.py:579
  78.2 3.4 %collective-permute-done.12.refs_0_ = bf16[12,128,128]{2,1,0:T(8,128)(2,1)S(1)} collective-permute-done((bf16[12,128,128]{2,1,0:T(8,128)(2,1)S(1)}, bf16[12,128,128]{2,1,0:T(8,128)(2,1)S(1)}, u32[]{:S(2)}, u32[]{:S(2)}) %collective-permute-start.12) | collective-permute-done | bytes 393248 | tf_op jit(solution)/shard_map/ppermute | solution.py:579
  81.6 0.0 collective-permute-done.13.refs_1_
  81.6 0.1 add.30.base
  81.7 8.8 %collective-permute-done.14.refs_0_ = bf16[12,128,128]{2,1,0:T(8,128)(2,1)S(1)} collective-permute-done((bf16[12,128,128]{2,1,0:T(8,128)(2,1)S(1)}, bf16[12,128,128]{2,1,0:T(8,128)(2,1)S(1)}, u32[]{:S(2)}, u32[]{:S(2)}) %collective-permute-start.14) | collective-permute-done | bytes 393248 | tf_op jit(solution)/shard_map/ppermute | solution.py:579
  90.5 0.9 add.31
  91.4 1.9 %collective-permute-done.11.refs_1_ = bf16[2,1,12,128,128]{4,3,2,1,0:T(8,128)(2,1)S(1)} collective-permute-done((bf16[2,1,12,128,128]{4,3,2,1,0:T(8,128)(2,1)S(1)}, bf16[2,1,12,128,128]{4,3,2,1,0:T(8,128)(2,1)S(1)}, u32[]{:S(2)}, u32[]{:S(2)}) %collective-permute-start.11) | collective-permute-done | bytes 786464 | tf_op jit(solution)/shard_map/ppermute | solution.py:579
  93.3 1.1 %finish.1 = (bf16[1536,128]{1,0:T(8,128)(2,1)}, bf16[1536,128]{1,0:T(8,128)(2,1)}) custom-call(f32[48,2,128,128]{3,2,1,0:T(8,128)S(1)} %get-tuple-element.55.acc, bf16[2,2,12,128,128]{4,3,2,1,0:T(8,128)(2,1)S(1)} %collective-permute-done.10.refs_0_, bf16[2,1,12,128,128]{4,3,2,1,0:T(8,128)(2,1)S(1)} %collective-permute-done.11.refs_1_), custom_call_target="tpu_custom_call" | custom-call | tf_op jit(solution)/shard_map/finish/pallas_call | solution.py:475
  (5 shorter events, 0.0 us)
Async XLA Ops:
  2.5 23.4 %copy-start.2 = (s32[192,3]{0,1:T(4,128)S(1)}, s32[192,3]{0,1:T(4,128)}, u32[]{:S(2)}) copy-start(s32[192,3]{0,1:T(4,128)} %param.13) | copy-start | bytes 6916
  2.5 21.0 %collective-permute-start = (bf16[3120,128]{1,0:T(8,128)(2,1)S(1)}, bf16[3120,128]{1,0:T(8,128)(2,1)}, u32[]{:S(2)}, u32[]{:S(2)}) collective-permute-start(bf16[3120,128]{1,0:T(8,128)(2,1)S(1)} %pack.1.unit.refs_0_), channel_id=1, source_target_pairs={{0,4},{1,5},{2,6},{3,7},{4,0},{5,1},{6,2},{7,3},{8,12},{9,13},{10,... | collective-permute-start | bytes 2396168 | tf_op jit(solution)/shard_map/ppermute | solution.py:579
  6.8 19.2 %collective-permute-start.3 = (bf16[3072,128]{1,0:T(8,128)(2,1)S(1)}, bf16[3072,128]{1,0:T(8,128)(2,1)}, u32[]{:S(2)}, u32[]{:S(2)}) collective-permute-start(bf16[3072,128]{1,0:T(8,128)(2,1)S(1)} %join.1.keyval.refs_1_), channel_id=1, source_target_pairs={{0,2},{1,3},{2,0},{3,1},{4,6},{5,7},{6,4},{7,5},{8,10},{9,11},{10,... | collective-permute-start | bytes 2359304 | tf_op jit(solution)/shard_map/ppermute | solution.py:579
  8.3 17.6 %collective-permute-start.6 = (bf16[3120,128]{1,0:T(8,128)(2,1)S(1)}, bf16[3120,128]{1,0:T(8,128)(2,1)}, u32[]{:S(2)}, u32[]{:S(2)}) collective-permute-start(bf16[3120,128]{1,0:T(8,128)(2,1)S(1)} %pack.1.unit.refs_0_), channel_id=1, source_target_pairs={{4,8},{5,9},{6,10},{7,11},{8,4},{9,5},{10,6},{11,7},{20,24},{21,25... | collective-permute-start | bytes 2396168 | tf_op jit(solution)/shard_map/ppermute | solution.py:579
  13.6 0.9 copy-start
  23.5 11.5 %collective-permute-start.1 = (bf16[3120,128]{1,0:T(8,128)(2,1)}, bf16[3120,128]{1,0:T(8,128)(2,1)}, u32[]{:S(2)}, u32[]{:S(2)}) collective-permute-start(bf16[3120,128]{1,0:T(8,128)(2,1)} %collective-permute-done.refs_0_), channel_id=1, source_target_pairs={{4,8},{5,9},{6,10},{7,11},{8,4},{9,5},{10,6},{11,7},{20,24},{21,25... | collective-permute-start | bytes 2396168 | tf_op jit(solution)/shard_map/ppermute | solution.py:579
  25.1 2.6 %collective-permute-start.2 = (bf16[3072,128]{1,0:T(8,128)(2,1)S(1)}, bf16[3072,128]{1,0:T(8,128)(2,1)}, u32[]{:S(2)}, u32[]{:S(2)}) collective-permute-start(bf16[3072,128]{1,0:T(8,128)(2,1)S(1)} %join.1.keyval.refs_1_), channel_id=1, source_target_pairs={{0,1},{1,0},{2,3},{3,2},{4,5},{5,4},{6,7},{7,6},{8,9},{9,8},{10,11... | collective-permute-start | bytes 2359304 | tf_op jit(solution)/shard_map/ppermute | solution.py:579
  25.9 2.9 %collective-permute-start.4 = (bf16[3072,128]{1,0:T(8,128)(2,1)}, bf16[3072,128]{1,0:T(8,128)(2,1)}, u32[]{:S(2)}, u32[]{:S(2)}) collective-permute-start(bf16[3072,128]{1,0:T(8,128)(2,1)} %collective-permute-done.3.refs_3_), channel_id=1, source_target_pairs={{0,1},{1,0},{2,3},{3,2},{4,5},{5,4},{6,7},{7,6},{8,9},{9,8},{10,11... | collective-permute-start | bytes 2359304 | tf_op jit(solution)/shard_map/ppermute | solution.py:579
  26.0 23.1 %collective-permute-start.7 = (bf16[3120,128]{1,0:T(8,128)(2,1)}, bf16[3120,128]{1,0:T(8,128)(2,1)}, u32[]{:S(2)}, u32[]{:S(2)}) collective-permute-start(bf16[3120,128]{1,0:T(8,128)(2,1)} %collective-permute-done.6.refs_1_), channel_id=1, source_target_pairs={{4,0},{5,1},{6,2},{7,3},{8,12},{9,13},{10,14},{11,15},{20,16},{21,... | collective-permute-start | bytes 2396168 | tf_op jit(solution)/shard_map/ppermute | solution.py:579
  28.8 1.1 %copy-start.1 = (f32[12,128,128]{2,1,0:T(8,128)S(1)}, f32[12,128,128]{2,1,0:T(8,128)}, u32[]{:S(2)}) copy-start(f32[12,128,128]{2,1,0:T(8,128)} %copy-done) | copy-start | bytes 2359300
  35.1 30.9 %collective-permute-start.5 = (bf16[3120,128]{1,0:T(8,128)(2,1)}, bf16[3120,128]{1,0:T(8,128)(2,1)S(1)}, u32[]{:S(2)}, u32[]{:S(2)}) collective-permute-start(bf16[3120,128]{1,0:T(8,128)(2,1)} %collective-permute-done.1.refs_1_), channel_id=1, source_target_pairs={{4,0},{5,1},{6,2},{7,3},{8,12},{9,13},{10,14},{11,15},{20,16},{21,... | collective-permute-start | bytes 2396168 | tf_op jit(solution)/shard_map/ppermute | solution.py:579
  57.5 11.9 %collective-permute-start.8 = (bf16[12,128,128]{2,1,0:T(8,128)(2,1)S(1)}, bf16[12,128,128]{2,1,0:T(8,128)(2,1)S(1)}, u32[]{:S(2)}, u32[]{:S(2)}) collective-permute-start(bf16[12,128,128]{2,1,0:T(8,128)(2,1)S(1)} %get-tuple-element.49), channel_id=1, source_target_pairs={{0,4},{1,5},{2,6},{3,7},{12,8},{13,9},{14,10},{15,11},{16,20},{17,... | collective-permute-start | bytes 1179656 | tf_op jit(solution)/shard_map/ppermute | solution.py:579
  59.2 10.3 %collective-permute-start.9 = (bf16[12,128,128]{2,1,0:T(8,128)(2,1)S(1)}, bf16[12,128,128]{2,1,0:T(8,128)(2,1)S(1)}, u32[]{:S(2)}, u32[]{:S(2)}) collective-permute-start(bf16[12,128,128]{2,1,0:T(8,128)(2,1)S(1)} %get-tuple-element.50), channel_id=1, source_target_pairs={{8,4},{9,5},{10,6},{11,7},{4,8},{5,9},{6,10},{7,11},{24,20},{25,21... | collective-permute-start | bytes 1179656 | tf_op jit(solution)/shard_map/ppermute | solution.py:579
  69.9 3.5 %collective-permute-start.10 = (bf16[2,2,12,128,128]{4,3,2,1,0:T(8,128)(2,1)S(1)}, bf16[2,2,12,128,128]{4,3,2,1,0:T(8,128)(2,1)S(1)}, u32[]{:S(2)}, u32[]{:S(2)}) collective-permute-start(bf16[2,2,12,128,128]{4,3,2,1,0:T(8,128)(2,1)S(1)} %share.2), channel_id=1, source_target_pairs={{0,1},{1,0},{2,3},{3,2},{4,5},{5,4},{6,7},{7,6},{8,9},{9,8},{10,11... | collective-permute-start | bytes 4718600 | tf_op jit(solution)/shard_map/ppermute | solution.py:579
  70.0 11.5 %collective-permute-start.12 = (bf16[12,128,128]{2,1,0:T(8,128)(2,1)S(1)}, bf16[12,128,128]{2,1,0:T(8,128)(2,1)S(1)}, u32[]{:S(2)}, u32[]{:S(2)}) collective-permute-start(bf16[12,128,128]{2,1,0:T(8,128)(2,1)S(1)} %get-tuple-element.57), channel_id=1, source_target_pairs={{4,0},{5,1},{6,2},{7,3},{0,4},{1,5},{2,6},{3,7},{12,8},{13,9},{14,... | collective-permute-start | bytes 1179656 | tf_op jit(solution)/shard_map/ppermute | solution.py:579
  70.8 10.8 %collective-permute-start.13 = (bf16[12,128,128]{2,1,0:T(8,128)(2,1)S(1)}, bf16[12,128,128]{2,1,0:T(8,128)(2,1)S(1)}, u32[]{:S(2)}, u32[]{:S(2)}) collective-permute-start(bf16[12,128,128]{2,1,0:T(8,128)(2,1)S(1)} %get-tuple-element.58), channel_id=1, source_target_pairs={{8,4},{9,5},{10,6},{11,7},{4,8},{5,9},{6,10},{7,11},{24,20},{25,21... | collective-permute-start | bytes 1179656 | tf_op jit(solution)/shard_map/ppermute | solution.py:579
  73.7 19.6 %collective-permute-start.11 = (bf16[2,1,12,128,128]{4,3,2,1,0:T(8,128)(2,1)S(1)}, bf16[2,1,12,128,128]{4,3,2,1,0:T(8,128)(2,1)S(1)}, u32[]{:S(2)}, u32[]{:S(2)}) collective-permute-start(bf16[2,1,12,128,128]{4,3,2,1,0:T(8,128)(2,1)S(1)} %share.3), channel_id=1, source_target_pairs={{0,2},{1,3},{2,0},{3,1},{4,6},{5,7},{6,4},{7,5},{8,10},{9,11},{10,... | collective-permute-start | bytes 2359304 | tf_op jit(solution)/shard_map/ppermute | solution.py:579
  75.2 15.3 %collective-permute-start.14 = (bf16[12,128,128]{2,1,0:T(8,128)(2,1)S(1)}, bf16[12,128,128]{2,1,0:T(8,128)(2,1)S(1)}, u32[]{:S(2)}, u32[]{:S(2)}) collective-permute-start(bf16[12,128,128]{2,1,0:T(8,128)(2,1)S(1)} %get-tuple-element.59), channel_id=1, source_target_pairs={{12,0},{13,1},{14,2},{15,3},{0,12},{1,13},{2,14},{3,15},{28,16},{2... | collective-permute-start | bytes 1179656 | tf_op jit(solution)/shard_map/ppermute | solution.py:579

commit v8 on v7

--- a/solution.py
+++ b/solution.py
@@ -35,7 +35,9 @@
     return next(groups for groups in (2, 3, 1) if count % groups == 0)
 
 
-def pack_kernel(query, grad, output, lse_hbm, unit, output_s, lse, delta_s, stat_s, sems):
+def pack_kernel(
+    query, grad, output, lse_hbm, key, value, unit, keyval, output_s, lse, delta_s, stat_s, sems
+):
     count, width = lse.shape
     groups = groups_of(count)
     group = count // groups
@@ -57,6 +59,12 @@
     for kind in range(3):
         for load in loads:
             load[kind].start()
+    joins = [
+        pltpu.make_async_copy(key, keyval.at[pl.ds(0, held)], sems.at[4, 0]),
+        pltpu.make_async_copy(value, keyval.at[pl.ds(held, held)], sems.at[5, 0]),
+    ]
+    for join in joins:
+        join.start()
 
     def total(part):
         return lax.dot_general(
@@ -82,53 +90,32 @@
     unit[2 * held :, :] = stat_s[...].astype(jnp.bfloat16)
     for load in loads:
         load[2].wait()
-
-
-def pack(query, grad, output, lse):
+    for join in joins:
+        join.wait()
+
+
+def pack(query, grad, output, lse, key, value):
     count, width = lse.shape
     rows = stat_rows(count)
     hbm = pl.BlockSpec(memory_space=pltpu.HBM)
     return pl.pallas_call(
         pack_kernel,
-        out_shape=jax.ShapeDtypeStruct((2 * count * BLK + rows, width), jnp.bfloat16),
-        in_specs=[hbm] * 4,
-        out_specs=pl.BlockSpec(memory_space=pltpu.VMEM),
+        out_shape=(
+            jax.ShapeDtypeStruct((2 * count * BLK + rows, width), jnp.bfloat16),
+            jax.ShapeDtypeStruct((2 * count * BLK, width), jnp.bfloat16),
+        ),
+        in_specs=[hbm] * 6,
+        out_specs=[pl.BlockSpec(memory_space=pltpu.VMEM)] * 2,
         scratch_shapes=[
             pltpu.VMEM(query.shape, jnp.bfloat16),
             pltpu.VMEM(lse.shape, jnp.float32),
             pltpu.VMEM(lse.shape, jnp.float32),
             pltpu.VMEM((rows, width), jnp.float32),
-            pltpu.SemaphoreType.DMA((4, groups_of(count))),
+            pltpu.SemaphoreType.DMA((6, groups_of(count))),
         ],
         compiler_params=pltpu.CompilerParams(vmem_limit_bytes=LIMIT),
         name="pack",
-    )(*[placed(array, pltpu.HBM) for array in (query, grad, output, lse)])
-
-
-def join_kernel(key, value, keyval, sems):
-    rows = key.shape[0]
-    copies = [
-        pltpu.make_async_copy(key, keyval.at[pl.ds(0, rows)], sems.at[0]),
-        pltpu.make_async_copy(value, keyval.at[pl.ds(rows, rows)], sems.at[1]),
-    ]
-    for copy in copies:
-        copy.start()
-    for copy in copies:
-        copy.wait()
-
-
-def join(key, value):
-    rows, width = key.shape
-    hbm = pl.BlockSpec(memory_space=pltpu.HBM)
-    return pl.pallas_call(
-        join_kernel,
-        out_shape=jax.ShapeDtypeStruct((2 * rows, width), key.dtype),
-        in_specs=[hbm, hbm],
-        out_specs=pl.BlockSpec(memory_space=pltpu.VMEM),
-        scratch_shapes=[pltpu.SemaphoreType.DMA((2,))],
-        compiler_params=pltpu.CompilerParams(vmem_limit_bytes=LIMIT),
-        name="join",
-    )(placed(key, pltpu.HBM), placed(value, pltpu.HBM))
+    )(*[placed(array, pltpu.HBM) for array in (query, grad, output, lse, key, value)])
 
 
 def pair_grads(pairs, scaling):
@@ -594,8 +581,9 @@
 
     me = jnp.stack([myself, jnp.int32(shards)]).astype(jnp.int32)
     entries = (layout // count * CODE + layout % count).reshape(-1)
-    unit = pack(query_rows, output_grad, output_rows, logsumexp.reshape(count, BLK))
-    keyval = join(key_rows, value_rows)
+    unit, keyval = pack(
+        query_rows, output_grad, output_rows, logsumexp.reshape(count, BLK), key_rows, value_rows
+    )
 
     def merge(one, two):
         return (one.astype(jnp.float32) + two.astype(jnp.float32)).astype(jnp.bfloat16)

time: 95.1 us -> 95.1 us (level)
    pallas_call x2 -> x1, Pallas kernels: 3.01 us -> 1.92 us  [pack(): pl.pallas_call(pack_kernel, out_shape=(jax.ShapeDtypeStruct((2 * count *...]
  transfers between devices with their start and end apart: 15 -> 15, of which waited for: 9 -> 8; matrix products, arithmetic and copies ran while one was open for 0% -> 0% of each run, Pallas kernels for 24% -> 24%
where the time goes in v8:
time: 95.1 us; the launch traced here: 94.4 us
  waiting for transfers between devices  46.4 us (49%)
  Pallas kernels  25.7 us (27%)
  starting transfers between devices  18.8 us (20%)
  local copies, waits for them, and re-layouts  2.34 us (2%)
    ppermute x15, waiting for transfers between devices, send(): return lax.ppermute(array, 'qb', pairs)  46.4 us
    ppermute x15, starting transfers between devices, send(): return lax.ppermute(array, 'qb', pairs)  18.8 us
    pallas_call x4, Pallas kernels, visit(): pl.pallas_call(functools.partial(visit_kernel, plan), out_shape=outs, in_...  17.5 us
    pallas_call x1, Pallas kernels, own_visit(): pl.pallas_call(own_kernel, out_shape=(jax.ShapeDtypeStruct((count, 2, BLK...  3.67 us
    unnamed x6, local copies, waits for them, and re-layouts  2.03 us
    pallas_call x1, Pallas kernels, pack(): pl.pallas_call(pack_kernel, out_shape=(jax.ShapeDtypeStruct((2 * count *...  1.92 us
  transfers between devices with their start and end apart: 15, of which 8 were waited for; matrix products, arithmetic and copies ran while one was open for 0% of the time, Pallas kernels for 24%

profile of v8, /device:TPU:0, one launch (start us, length us, event | category | flops | bytes accessed | tf_op | source)
XLA Modules:
  0.0 94.4 jit_solution(4576028813507430136)
XLA Ops:
  0.6 1.9 %pack.1 = (bf16[3120,128]{1,0:T(8,128)(2,1)S(1)}, bf16[3072,128]{1,0:T(8,128)(2,1)S(1)}) custom-call(bf16[1536,128]{1,0:T(8,128)(2,1)} %query.1, bf16[1536,128]{1,0:T(8,128)(2,1)} %grad.1, bf16[1536,128]{1,0:T(8,128)(2,1)} %output.1, f32[12,128]{1,0:T(8,128)} %bitcast.2, bf16[1536,128]{1,0:T(8,128)(2,1)} %key.1, bf16[1536,128]{1,0:T(8,128)(2,1)} %value.1), custom_call_target="tpu_custom_call" | custom-call | tf_op jit(solution)/shard_map/pack/pallas_call | solution.py:101
  2.6 3.1 %collective-permute-start = (bf16[3120,128]{1,0:T(8,128)(2,1)S(1)}, bf16[3120,128]{1,0:T(8,128)(2,1)}, u32[]{:S(2)}, u32[]{:S(2)}) collective-permute-start(bf16[3120,128]{1,0:T(8,128)(2,1)S(1)} %get-tuple-element.36.unit.refs_0_), channel_id=1, source_target_pairs={{0,4},{1,5},{2,6},{3,7},{4,0},{5,1},{6,2},{7,3},{8,12},{9,13},{10,... | collective-permute-start | bytes 2396168 | tf_op jit(solution)/shard_map/ppermute | solution.py:566
  5.7 1.5 %collective-permute-start.3 = (bf16[3072,128]{1,0:T(8,128)(2,1)S(1)}, bf16[3072,128]{1,0:T(8,128)(2,1)}, u32[]{:S(2)}, u32[]{:S(2)}) collective-permute-start(bf16[3072,128]{1,0:T(8,128)(2,1)S(1)} %get-tuple-element.37.keyval.refs_1_), channel_id=1, source_target_pairs={{0,2},{1,3},{2,0},{3,1},{4,6},{5,7},{6,4},{7,5},{8,10},{9,11},{10,... | collective-permute-start | bytes 2359304 | tf_op jit(solution)/shard_map/ppermute | solution.py:566
  7.2 1.6 %collective-permute-start.6 = (bf16[3120,128]{1,0:T(8,128)(2,1)S(1)}, bf16[3120,128]{1,0:T(8,128)(2,1)}, u32[]{:S(2)}, u32[]{:S(2)}) collective-permute-start(bf16[3120,128]{1,0:T(8,128)(2,1)S(1)} %get-tuple-element.36.unit.refs_0_), channel_id=1, source_target_pairs={{4,8},{5,9},{6,10},{7,11},{8,4},{9,5},{10,6},{11,7},{20,24},{21,25... | collective-permute-start | bytes 2396168 | tf_op jit(solution)/shard_map/ppermute | solution.py:566
  8.8 3.7 %own.1 = (f32[12,2,128,128]{3,2,1,0:T(8,128)S(1)}, f32[12,128,128]{2,1,0:T(8,128)S(1)}) custom-call(bf16[3120,128]{1,0:T(8,128)(2,1)S(1)} %get-tuple-element.36.unit.refs_0_, bf16[3072,128]{1,0:T(8,128)(2,1)S(1)} %get-tuple-element.37.keyval.refs_1_), custom_call_target="tpu_custom_call" | custom-call | tf_op jit(solution)/shard_map/own/pallas_call | solution.py:433
  12.4 0.9 copy-done
  13.3 10.2 %collective-permute-done.refs_0_ = bf16[3120,128]{1,0:T(8,128)(2,1)} collective-permute-done((bf16[3120,128]{1,0:T(8,128)(2,1)S(1)}, bf16[3120,128]{1,0:T(8,128)(2,1)}, u32[]{:S(2)}, u32[]{:S(2)}) %collective-permute-start) | collective-permute-done | bytes 798752 | tf_op jit(solution)/shard_map/ppermute | solution.py:566
  23.6 1.6 %collective-permute-start.1 = (bf16[3120,128]{1,0:T(8,128)(2,1)}, bf16[3120,128]{1,0:T(8,128)(2,1)}, u32[]{:S(2)}, u32[]{:S(2)}) collective-permute-start(bf16[3120,128]{1,0:T(8,128)(2,1)} %collective-permute-done.refs_0_), channel_id=1, source_target_pairs={{4,8},{5,9},{6,10},{7,11},{8,4},{9,5},{10,6},{11,7},{20,24},{21,25... | collective-permute-start | bytes 2396168 | tf_op jit(solution)/shard_map/ppermute | solution.py:566
  25.1 0.0 collective-permute-start.2
  25.1 0.0 collective-permute-done.3.refs_3_
  25.1 0.5 collective-permute-start.4
  25.6 0.0 copy-done.2
  25.7 0.0 collective-permute-done.6.refs_1_
  25.7 1.3 %collective-permute-start.7 = (bf16[3120,128]{1,0:T(8,128)(2,1)}, bf16[3120,128]{1,0:T(8,128)(2,1)}, u32[]{:S(2)}, u32[]{:S(2)}) collective-permute-start(bf16[3120,128]{1,0:T(8,128)(2,1)} %collective-permute-done.6.refs_1_), channel_id=1, source_target_pairs={{4,0},{5,1},{6,2},{7,3},{8,12},{9,13},{10,14},{11,15},{20,16},{21,... | collective-permute-start | bytes 2396168 | tf_op jit(solution)/shard_map/ppermute | solution.py:566
  27.0 0.1 pad_add_fusion.me_ref
  27.0 0.1 copy.13
  27.2 0.2 reshape.12.layout
  27.4 1.2 %collective-permute-done.2.refs_2_ = bf16[3072,128]{1,0:T(8,128)(2,1)} collective-permute-done((bf16[3072,128]{1,0:T(8,128)(2,1)S(1)}, bf16[3072,128]{1,0:T(8,128)(2,1)}, u32[]{:S(2)}, u32[]{:S(2)}) %collective-permute-start.2) | collective-permute-done | bytes 786464 | tf_op jit(solution)/shard_map/ppermute | solution.py:566
  28.6 0.3 collective-permute-done.4.refs_4_
  28.9 1.1 %copy-done.1 = f32[12,128,128]{2,1,0:T(8,128)S(1)} copy-done((f32[12,128,128]{2,1,0:T(8,128)S(1)}, f32[12,128,128]{2,1,0:T(8,128)}, u32[]{:S(2)}) %copy-start.1) | copy-done | bytes 786456
  30.0 5.6 %visit.4 = (bf16[6144,128]{1,0:T(8,128)(2,1)S(1)}, bf16[6144,128]{1,0:T(8,128)(2,1)S(1)}, f32[48,2,128,128]{3,2,1,0:T(8,128)S(1)}, f32[12,128,128]{2,1,0:T(8,128)S(1)}) custom-call(s32[2]{0:T(128)S(1)} %pad_add_fusion.me_ref, s32[576]{0:T(1024)S(1)} %reshape.12.layout, bf16[3120,128]{1,0:T(8,128)(2,1)S(1)} %get-tuple-element.36.unit.refs_0_, ...), custom_call_target="tpu_custom_call" | custom-call | tf_op jit(solution)/shard_map/visit/pallas_call | solution.py:529
  35.7 0.0 collective-permute-done.1.refs_1_
  35.7 1.3 %collective-permute-start.5 = (bf16[3120,128]{1,0:T(8,128)(2,1)}, bf16[3120,128]{1,0:T(8,128)(2,1)S(1)}, u32[]{:S(2)}, u32[]{:S(2)}) collective-permute-start(bf16[3120,128]{1,0:T(8,128)(2,1)} %collective-permute-done.1.refs_1_), channel_id=1, source_target_pairs={{4,0},{5,1},{6,2},{7,3},{8,12},{9,13},{10,14},{11,15},{20,16},{21,... | collective-permute-start | bytes 2396168 | tf_op jit(solution)/shard_map/ppermute | solution.py:566
  37.0 13.2 %collective-permute-done.7.refs_0_ = bf16[3120,128]{1,0:T(8,128)(2,1)} collective-permute-done((bf16[3120,128]{1,0:T(8,128)(2,1)}, bf16[3120,128]{1,0:T(8,128)(2,1)}, u32[]{:S(2)}, u32[]{:S(2)}) %collective-permute-start.7) | collective-permute-done | bytes 798752 | tf_op jit(solution)/shard_map/ppermute | solution.py:566
  50.2 4.2 %visit.5 = (f32[48,2,128,128]{3,2,1,0:T(8,128)S(1)}, bf16[12,128,128]{2,1,0:T(8,128)(2,1)S(1)}, bf16[12,128,128]{2,1,0:T(8,128)(2,1)S(1)}) custom-call(s32[2]{0:T(128)S(1)} %pad_add_fusion.me_ref, s32[576]{0:T(1024)S(1)} %reshape.12.layout, bf16[3120,128]{1,0:T(8,128)(2,1)} %collective-permute-done.refs_0_, ...), custom_call_target="tpu_custom_call", output_to_operand_aliasing={{0}: (6, {})} | custom-call | tf_op jit(solution)/shard_map/visit/pallas_call | solution.py:529
  54.4 4.2 %visit.6 = (f32[48,2,128,128]{3,2,1,0:T(8,128)S(1)}, bf16[12,128,128]{2,1,0:T(8,128)(2,1)S(1)}, bf16[12,128,128]{2,1,0:T(8,128)(2,1)S(1)}) custom-call(s32[2]{0:T(128)S(1)} %pad_add_fusion.me_ref, s32[576]{0:T(1024)S(1)} %reshape.12.layout, bf16[3120,128]{1,0:T(8,128)(2,1)} %collective-permute-done.7.refs_0_, ...), custom_call_target="tpu_custom_call", output_to_operand_aliasing={{0}: (6, {})} | custom-call | tf_op jit(solution)/shard_map/visit/pallas_call | solution.py:529
  58.7 1.6 %collective-permute-start.8 = (bf16[12,128,128]{2,1,0:T(8,128)(2,1)S(1)}, bf16[12,128,128]{2,1,0:T(8,128)(2,1)S(1)}, u32[]{:S(2)}, u32[]{:S(2)}) collective-permute-start(bf16[12,128,128]{2,1,0:T(8,128)(2,1)S(1)} %get-tuple-element.53), channel_id=1, source_target_pairs={{0,4},{1,5},{2,6},{3,7},{12,8},{13,9},{14,10},{15,11},{16,20},{17,... | collective-permute-start | bytes 1179656 | tf_op jit(solution)/shard_map/ppermute | solution.py:566
  60.3 0.7 collective-permute-start.9
  61.0 5.1 %collective-permute-done.5.refs_0_ = bf16[3120,128]{1,0:T(8,128)(2,1)S(1)} collective-permute-done((bf16[3120,128]{1,0:T(8,128)(2,1)}, bf16[3120,128]{1,0:T(8,128)(2,1)S(1)}, u32[]{:S(2)}, u32[]{:S(2)}) %collective-permute-start.5) | collective-permute-done | bytes 798752 | tf_op jit(solution)/shard_map/ppermute | solution.py:566
  66.1 3.4 %visit.7 = (f32[48,2,128,128]{3,2,1,0:T(8,128)S(1)}, bf16[12,128,128]{2,1,0:T(8,128)(2,1)S(1)}) custom-call(s32[2]{0:T(128)S(1)} %pad_add_fusion.me_ref, s32[576]{0:T(1024)S(1)} %reshape.12.layout, bf16[3120,128]{1,0:T(8,128)(2,1)S(1)} %collective-permute-done.5.refs_0_, ...), custom_call_target="tpu_custom_call", output_to_operand_aliasing={{0}: (5, {})} | custom-call | flops 5033164800 | tf_op jit(solution)/shard_map/visit/pallas_call | solution.py:529
  69.5 0.0 collective-permute-done.8
  69.5 0.0 collective-permute-done.9
  69.5 0.2 add_convert_fusion
  69.7 0.2 share.2
  69.9 0.1 collective-permute-start.10
  70.0 0.4 collective-permute-start.12
  70.5 0.7 collective-permute-start.13
  71.1 2.3 %collective-permute-done.10.refs_0_ = bf16[2,2,12,128,128]{4,3,2,1,0:T(8,128)(2,1)S(1)} collective-permute-done((bf16[2,2,12,128,128]{4,3,2,1,0:T(8,128)(2,1)S(1)}, bf16[2,2,12,128,128]{4,3,2,1,0:T(8,128)(2,1)S(1)}, u32[]{:S(2)}, u32[]{:S(2)}) %collective-permute-start.10) | collective-permute-done | bytes 1572896 | tf_op jit(solution)/shard_map/ppermute | solution.py:566
  73.4 0.3 share.3
  73.7 1.0 %collective-permute-start.11 = (bf16[2,1,12,128,128]{4,3,2,1,0:T(8,128)(2,1)S(1)}, bf16[2,1,12,128,128]{4,3,2,1,0:T(8,128)(2,1)S(1)}, u32[]{:S(2)}, u32[]{:S(2)}) collective-permute-start(bf16[2,1,12,128,128]{4,3,2,1,0:T(8,128)(2,1)S(1)} %share.3), channel_id=1, source_target_pairs={{0,2},{1,3},{2,0},{3,1},{4,6},{5,7},{6,4},{7,5},{8,10},{9,11},{10,... | collective-permute-start | bytes 2359304 | tf_op jit(solution)/shard_map/ppermute | solution.py:566
  74.7 3.5 %collective-permute-start.14 = (bf16[12,128,128]{2,1,0:T(8,128)(2,1)S(1)}, bf16[12,128,128]{2,1,0:T(8,128)(2,1)S(1)}, u32[]{:S(2)}, u32[]{:S(2)}) collective-permute-start(bf16[12,128,128]{2,1,0:T(8,128)(2,1)S(1)} %get-tuple-element.63), channel_id=1, source_target_pairs={{12,0},{13,1},{14,2},{15,3},{0,12},{1,13},{2,14},{3,15},{28,16},{2... | collective-permute-start | bytes 1179656 | tf_op jit(solution)/shard_map/ppermute | solution.py:566
  78.2 11.8 %collective-permute-done.12.refs_0_ = bf16[12,128,128]{2,1,0:T(8,128)(2,1)S(1)} collective-permute-done((bf16[12,128,128]{2,1,0:T(8,128)(2,1)S(1)}, bf16[12,128,128]{2,1,0:T(8,128)(2,1)S(1)}, u32[]{:S(2)}, u32[]{:S(2)}) %collective-permute-start.12) | collective-permute-done | bytes 393248 | tf_op jit(solution)/shard_map/ppermute | solution.py:566
  90.0 0.0 collective-permute-done.13.refs_1_
  90.0 0.1 add.30.base
  90.1 0.0 collective-permute-done.14.refs_0_
  90.2 0.9 add.31
  91.0 2.3 %collective-permute-done.11.refs_1_ = bf16[2,1,12,128,128]{4,3,2,1,0:T(8,128)(2,1)S(1)} collective-permute-done((bf16[2,1,12,128,128]{4,3,2,1,0:T(8,128)(2,1)S(1)}, bf16[2,1,12,128,128]{4,3,2,1,0:T(8,128)(2,1)S(1)}, u32[]{:S(2)}, u32[]{:S(2)}) %collective-permute-start.11) | collective-permute-done | bytes 786464 | tf_op jit(solution)/shard_map/ppermute | solution.py:566
  93.3 1.1 %finish.1 = (bf16[1536,128]{1,0:T(8,128)(2,1)}, bf16[1536,128]{1,0:T(8,128)(2,1)}) custom-call(f32[48,2,128,128]{3,2,1,0:T(8,128)S(1)} %get-tuple-element.59.acc, bf16[2,2,12,128,128]{4,3,2,1,0:T(8,128)(2,1)S(1)} %collective-permute-done.10.refs_0_, bf16[2,1,12,128,128]{4,3,2,1,0:T(8,128)(2,1)S(1)} %collective-permute-done.11.refs_1_), custom_call_target="tpu_custom_call" | custom-call | tf_op jit(solution)/shard_map/finish/pallas_call | solution.py:462
  (4 shorter events, 0.0 us)
Async XLA Ops:
  0.6 25.0 %copy-start.2 = (s32[192,3]{0,1:T(4,128)S(1)}, s32[192,3]{0,1:T(4,128)}, u32[]{:S(2)}) copy-start(s32[192,3]{0,1:T(4,128)} %param.13) | copy-start | bytes 6916
  2.6 21.0 %collective-permute-start = (bf16[3120,128]{1,0:T(8,128)(2,1)S(1)}, bf16[3120,128]{1,0:T(8,128)(2,1)}, u32[]{:S(2)}, u32[]{:S(2)}) collective-permute-start(bf16[3120,128]{1,0:T(8,128)(2,1)S(1)} %get-tuple-element.36.unit.refs_0_), channel_id=1, source_target_pairs={{0,4},{1,5},{2,6},{3,7},{4,0},{5,1},{6,2},{7,3},{8,12},{9,13},{10,... | collective-permute-start | bytes 2396168 | tf_op jit(solution)/shard_map/ppermute | solution.py:566
  5.7 19.5 %collective-permute-start.3 = (bf16[3072,128]{1,0:T(8,128)(2,1)S(1)}, bf16[3072,128]{1,0:T(8,128)(2,1)}, u32[]{:S(2)}, u32[]{:S(2)}) collective-permute-start(bf16[3072,128]{1,0:T(8,128)(2,1)S(1)} %get-tuple-element.37.keyval.refs_1_), channel_id=1, source_target_pairs={{0,2},{1,3},{2,0},{3,1},{4,6},{5,7},{6,4},{7,5},{8,10},{9,11},{10,... | collective-permute-start | bytes 2359304 | tf_op jit(solution)/shard_map/ppermute | solution.py:566
  7.2 18.5 %collective-permute-start.6 = (bf16[3120,128]{1,0:T(8,128)(2,1)S(1)}, bf16[3120,128]{1,0:T(8,128)(2,1)}, u32[]{:S(2)}, u32[]{:S(2)}) collective-permute-start(bf16[3120,128]{1,0:T(8,128)(2,1)S(1)} %get-tuple-element.36.unit.refs_0_), channel_id=1, source_target_pairs={{4,8},{5,9},{6,10},{7,11},{8,4},{9,5},{10,6},{11,7},{20,24},{21,25... | collective-permute-start | bytes 2396168 | tf_op jit(solution)/shard_map/ppermute | solution.py:566
  12.4 0.9 copy-start
  23.6 12.1 %collective-permute-start.1 = (bf16[3120,128]{1,0:T(8,128)(2,1)}, bf16[3120,128]{1,0:T(8,128)(2,1)}, u32[]{:S(2)}, u32[]{:S(2)}) collective-permute-start(bf16[3120,128]{1,0:T(8,128)(2,1)} %collective-permute-done.refs_0_), channel_id=1, source_target_pairs={{4,8},{5,9},{6,10},{7,11},{8,4},{9,5},{10,6},{11,7},{20,24},{21,25... | collective-permute-start | bytes 2396168 | tf_op jit(solution)/shard_map/ppermute | solution.py:566
  25.1 3.5 %collective-permute-start.2 = (bf16[3072,128]{1,0:T(8,128)(2,1)S(1)}, bf16[3072,128]{1,0:T(8,128)(2,1)}, u32[]{:S(2)}, u32[]{:S(2)}) collective-permute-start(bf16[3072,128]{1,0:T(8,128)(2,1)S(1)} %get-tuple-element.37.keyval.refs_1_), channel_id=1, source_target_pairs={{0,1},{1,0},{2,3},{3,2},{4,5},{5,4},{6,7},{7,6},{8,9},{9,8},{10,11... | collective-permute-start | bytes 2359304 | tf_op jit(solution)/shard_map/ppermute | solution.py:566
  25.1 3.7 %collective-permute-start.4 = (bf16[3072,128]{1,0:T(8,128)(2,1)}, bf16[3072,128]{1,0:T(8,128)(2,1)}, u32[]{:S(2)}, u32[]{:S(2)}) collective-permute-start(bf16[3072,128]{1,0:T(8,128)(2,1)} %collective-permute-done.3.refs_3_), channel_id=1, source_target_pairs={{0,1},{1,0},{2,3},{3,2},{4,5},{5,4},{6,7},{7,6},{8,9},{9,8},{10,11... | collective-permute-start | bytes 2359304 | tf_op jit(solution)/shard_map/ppermute | solution.py:566
  25.7 24.5 %collective-permute-start.7 = (bf16[3120,128]{1,0:T(8,128)(2,1)}, bf16[3120,128]{1,0:T(8,128)(2,1)}, u32[]{:S(2)}, u32[]{:S(2)}) collective-permute-start(bf16[3120,128]{1,0:T(8,128)(2,1)} %collective-permute-done.6.refs_1_), channel_id=1, source_target_pairs={{4,0},{5,1},{6,2},{7,3},{8,12},{9,13},{10,14},{11,15},{20,16},{21,... | collective-permute-start | bytes 2396168 | tf_op jit(solution)/shard_map/ppermute | solution.py:566
  28.9 1.1 %copy-start.1 = (f32[12,128,128]{2,1,0:T(8,128)S(1)}, f32[12,128,128]{2,1,0:T(8,128)}, u32[]{:S(2)}) copy-start(f32[12,128,128]{2,1,0:T(8,128)} %copy-done) | copy-start | bytes 2359300
  35.7 30.4 %collective-permute-start.5 = (bf16[3120,128]{1,0:T(8,128)(2,1)}, bf16[3120,128]{1,0:T(8,128)(2,1)S(1)}, u32[]{:S(2)}, u32[]{:S(2)}) collective-permute-start(bf16[3120,128]{1,0:T(8,128)(2,1)} %collective-permute-done.1.refs_1_), channel_id=1, source_target_pairs={{4,0},{5,1},{6,2},{7,3},{8,12},{9,13},{10,14},{11,15},{20,16},{21,... | collective-permute-start | bytes 2396168 | tf_op jit(solution)/shard_map/ppermute | solution.py:566
  58.7 10.8 %collective-permute-start.8 = (bf16[12,128,128]{2,1,0:T(8,128)(2,1)S(1)}, bf16[12,128,128]{2,1,0:T(8,128)(2,1)S(1)}, u32[]{:S(2)}, u32[]{:S(2)}) collective-permute-start(bf16[12,128,128]{2,1,0:T(8,128)(2,1)S(1)} %get-tuple-element.53), channel_id=1, source_target_pairs={{0,4},{1,5},{2,6},{3,7},{12,8},{13,9},{14,10},{15,11},{16,20},{17,... | collective-permute-start | bytes 1179656 | tf_op jit(solution)/shard_map/ppermute | solution.py:566
  60.3 9.2 %collective-permute-start.9 = (bf16[12,128,128]{2,1,0:T(8,128)(2,1)S(1)}, bf16[12,128,128]{2,1,0:T(8,128)(2,1)S(1)}, u32[]{:S(2)}, u32[]{:S(2)}) collective-permute-start(bf16[12,128,128]{2,1,0:T(8,128)(2,1)S(1)} %get-tuple-element.54), channel_id=1, source_target_pairs={{8,4},{9,5},{10,6},{11,7},{4,8},{5,9},{6,10},{7,11},{24,20},{25,21... | collective-permute-start | bytes 1179656 | tf_op jit(solution)/shard_map/ppermute | solution.py:566
  69.9 3.5 %collective-permute-start.10 = (bf16[2,2,12,128,128]{4,3,2,1,0:T(8,128)(2,1)S(1)}, bf16[2,2,12,128,128]{4,3,2,1,0:T(8,128)(2,1)S(1)}, u32[]{:S(2)}, u32[]{:S(2)}) collective-permute-start(bf16[2,2,12,128,128]{4,3,2,1,0:T(8,128)(2,1)S(1)} %share.2), channel_id=1, source_target_pairs={{0,1},{1,0},{2,3},{3,2},{4,5},{5,4},{6,7},{7,6},{8,9},{9,8},{10,11... | collective-permute-start | bytes 4718600 | tf_op jit(solution)/shard_map/ppermute | solution.py:566
  70.0 20.0 %collective-permute-start.12 = (bf16[12,128,128]{2,1,0:T(8,128)(2,1)S(1)}, bf16[12,128,128]{2,1,0:T(8,128)(2,1)S(1)}, u32[]{:S(2)}, u32[]{:S(2)}) collective-permute-start(bf16[12,128,128]{2,1,0:T(8,128)(2,1)S(1)} %get-tuple-element.61), channel_id=1, source_target_pairs={{4,0},{5,1},{6,2},{7,3},{0,4},{1,5},{2,6},{3,7},{12,8},{13,9},{14,... | collective-permute-start | bytes 1179656 | tf_op jit(solution)/shard_map/ppermute | solution.py:566
  70.5 19.5 %collective-permute-start.13 = (bf16[12,128,128]{2,1,0:T(8,128)(2,1)S(1)}, bf16[12,128,128]{2,1,0:T(8,128)(2,1)S(1)}, u32[]{:S(2)}, u32[]{:S(2)}) collective-permute-start(bf16[12,128,128]{2,1,0:T(8,128)(2,1)S(1)} %get-tuple-element.62), channel_id=1, source_target_pairs={{8,4},{9,5},{10,6},{11,7},{4,8},{5,9},{6,10},{7,11},{24,20},{25,21... | collective-permute-start | bytes 1179656 | tf_op jit(solution)/shard_map/ppermute | solution.py:566
  73.7 19.6 %collective-permute-start.11 = (bf16[2,1,12,128,128]{4,3,2,1,0:T(8,128)(2,1)S(1)}, bf16[2,1,12,128,128]{4,3,2,1,0:T(8,128)(2,1)S(1)}, u32[]{:S(2)}, u32[]{:S(2)}) collective-permute-start(bf16[2,1,12,128,128]{4,3,2,1,0:T(8,128)(2,1)S(1)} %share.3), channel_id=1, source_target_pairs={{0,2},{1,3},{2,0},{3,1},{4,6},{5,7},{6,4},{7,5},{8,10},{9,11},{10,... | collective-permute-start | bytes 2359304 | tf_op jit(solution)/shard_map/ppermute | solution.py:566
  74.7 15.5 %collective-permute-start.14 = (bf16[12,128,128]{2,1,0:T(8,128)(2,1)S(1)}, bf16[12,128,128]{2,1,0:T(8,128)(2,1)S(1)}, u32[]{:S(2)}, u32[]{:S(2)}) collective-permute-start(bf16[12,128,128]{2,1,0:T(8,128)(2,1)S(1)} %get-tuple-element.63), channel_id=1, source_target_pairs={{12,0},{13,1},{14,2},{15,3},{0,12},{1,13},{2,14},{3,15},{28,16},{2... | collective-permute-start | bytes 1179656 | tf_op jit(solution)/shard_map/ppermute | solution.py:566

commit v9 on v8

--- a/solution.py
+++ b/solution.py
@@ -11,7 +11,7 @@
 GLOB = 2
 TILE = 16
 CODE = 256
-PAIRS = 5
+PAIRS = 10
 TURNS = 6
 FAR = 1e30
 COST = 20

time: 95.1 us -> 94.8 us (level)
  no operation moved by 1% of the time
where the time goes in v9:
time: 94.8 us; the launch traced here: 94.4 us
  waiting for transfers between devices  46.6 us (49%)
  Pallas kernels  25.4 us (27%)
  starting transfers between devices  18.7 us (20%)
  local copies, waits for them, and re-layouts  2.34 us (2%)
  between operations  1 us (1%)
    ppermute x15, waiting for transfers between devices, send(): return lax.ppermute(array, 'qb', pairs)  46.6 us
    ppermute x15, starting transfers between devices, send(): return lax.ppermute(array, 'qb', pairs)  18.7 us
    pallas_call x4, Pallas kernels, visit(): pl.pallas_call(functools.partial(visit_kernel, plan), out_shape=outs, in_...  17.2 us
    pallas_call x1, Pallas kernels, own_visit(): pl.pallas_call(own_kernel, out_shape=(jax.ShapeDtypeStruct((count, 2, BLK...  3.67 us
    unnamed x6, local copies, waits for them, and re-layouts  2.03 us
    pallas_call x1, Pallas kernels, pack(): pl.pallas_call(pack_kernel, out_shape=(jax.ShapeDtypeStruct((2 * count *...  1.92 us
  transfers between devices with their start and end apart: 15, of which 8 were waited for; matrix products, arithmetic and copies ran while one was open for 0% of the time, Pallas kernels for 24%

profile of v9, /device:TPU:0, one launch (start us, length us, event | category | flops | bytes accessed | tf_op | source)
XLA Modules:
  0.0 94.4 jit_solution(8082688250352254332)
XLA Ops:
  0.6 0.0 copy-start.2
  0.6 1.9 %pack.1 = (bf16[3120,128]{1,0:T(8,128)(2,1)S(1)}, bf16[3072,128]{1,0:T(8,128)(2,1)S(1)}) custom-call(bf16[1536,128]{1,0:T(8,128)(2,1)} %query.1, bf16[1536,128]{1,0:T(8,128)(2,1)} %grad.1, bf16[1536,128]{1,0:T(8,128)(2,1)} %output.1, f32[12,128]{1,0:T(8,128)} %bitcast.2, bf16[1536,128]{1,0:T(8,128)(2,1)} %key.1, bf16[1536,128]{1,0:T(8,128)(2,1)} %value.1), custom_call_target="tpu_custom_call" | custom-call | tf_op jit(solution)/shard_map/pack/pallas_call | solution.py:101
  2.6 3.1 %collective-permute-start = (bf16[3120,128]{1,0:T(8,128)(2,1)S(1)}, bf16[3120,128]{1,0:T(8,128)(2,1)}, u32[]{:S(2)}, u32[]{:S(2)}) collective-permute-start(bf16[3120,128]{1,0:T(8,128)(2,1)S(1)} %get-tuple-element.36.unit.refs_0_), channel_id=1, source_target_pairs={{0,4},{1,5},{2,6},{3,7},{4,0},{5,1},{6,2},{7,3},{8,12},{9,13},{10,... | collective-permute-start | bytes 2396168 | tf_op jit(solution)/shard_map/ppermute | solution.py:566
  5.7 1.5 %collective-permute-start.3 = (bf16[3072,128]{1,0:T(8,128)(2,1)S(1)}, bf16[3072,128]{1,0:T(8,128)(2,1)}, u32[]{:S(2)}, u32[]{:S(2)}) collective-permute-start(bf16[3072,128]{1,0:T(8,128)(2,1)S(1)} %get-tuple-element.37.keyval.refs_1_), channel_id=1, source_target_pairs={{0,2},{1,3},{2,0},{3,1},{4,6},{5,7},{6,4},{7,5},{8,10},{9,11},{10,... | collective-permute-start | bytes 2359304 | tf_op jit(solution)/shard_map/ppermute | solution.py:566
  7.2 1.6 %collective-permute-start.6 = (bf16[3120,128]{1,0:T(8,128)(2,1)S(1)}, bf16[3120,128]{1,0:T(8,128)(2,1)}, u32[]{:S(2)}, u32[]{:S(2)}) collective-permute-start(bf16[3120,128]{1,0:T(8,128)(2,1)S(1)} %get-tuple-element.36.unit.refs_0_), channel_id=1, source_target_pairs={{4,8},{5,9},{6,10},{7,11},{8,4},{9,5},{10,6},{11,7},{20,24},{21,25... | collective-permute-start | bytes 2396168 | tf_op jit(solution)/shard_map/ppermute | solution.py:566
  8.8 3.7 %own.1 = (f32[12,2,128,128]{3,2,1,0:T(8,128)S(1)}, f32[12,128,128]{2,1,0:T(8,128)S(1)}) custom-call(bf16[3120,128]{1,0:T(8,128)(2,1)S(1)} %get-tuple-element.36.unit.refs_0_, bf16[3072,128]{1,0:T(8,128)(2,1)S(1)} %get-tuple-element.37.keyval.refs_1_), custom_call_target="tpu_custom_call" | custom-call | tf_op jit(solution)/shard_map/own/pallas_call | solution.py:433
  12.4 0.9 copy-done
  13.3 10.2 %collective-permute-done.refs_0_ = bf16[3120,128]{1,0:T(8,128)(2,1)} collective-permute-done((bf16[3120,128]{1,0:T(8,128)(2,1)S(1)}, bf16[3120,128]{1,0:T(8,128)(2,1)}, u32[]{:S(2)}, u32[]{:S(2)}) %collective-permute-start) | collective-permute-done | bytes 798752 | tf_op jit(solution)/shard_map/ppermute | solution.py:566
  23.6 1.6 %collective-permute-start.1 = (bf16[3120,128]{1,0:T(8,128)(2,1)}, bf16[3120,128]{1,0:T(8,128)(2,1)}, u32[]{:S(2)}, u32[]{:S(2)}) collective-permute-start(bf16[3120,128]{1,0:T(8,128)(2,1)} %collective-permute-done.refs_0_), channel_id=1, source_target_pairs={{4,8},{5,9},{6,10},{7,11},{8,4},{9,5},{10,6},{11,7},{20,24},{21,25... | collective-permute-start | bytes 2396168 | tf_op jit(solution)/shard_map/ppermute | solution.py:566
  25.1 0.0 collective-permute-start.2
  25.1 0.0 collective-permute-done.3.refs_3_
  25.1 0.5 collective-permute-start.4
  25.7 0.0 collective-permute-done.6.refs_1_
  25.7 1.3 %collective-permute-start.7 = (bf16[3120,128]{1,0:T(8,128)(2,1)}, bf16[3120,128]{1,0:T(8,128)(2,1)}, u32[]{:S(2)}, u32[]{:S(2)}) collective-permute-start(bf16[3120,128]{1,0:T(8,128)(2,1)} %collective-permute-done.6.refs_1_), channel_id=1, source_target_pairs={{4,0},{5,1},{6,2},{7,3},{8,12},{9,13},{10,14},{11,15},{20,16},{21,... | collective-permute-start | bytes 2396168 | tf_op jit(solution)/shard_map/ppermute | solution.py:566
  27.0 0.1 pad_add_fusion.me_ref
  27.0 0.1 copy.13
  27.2 0.2 reshape.12.layout
  27.4 1.2 %collective-permute-done.2.refs_2_ = bf16[3072,128]{1,0:T(8,128)(2,1)} collective-permute-done((bf16[3072,128]{1,0:T(8,128)(2,1)S(1)}, bf16[3072,128]{1,0:T(8,128)(2,1)}, u32[]{:S(2)}, u32[]{:S(2)}) %collective-permute-start.2) | collective-permute-done | bytes 786464 | tf_op jit(solution)/shard_map/ppermute | solution.py:566
  28.6 0.3 collective-permute-done.4.refs_4_
  28.9 1.1 %copy-done.1 = f32[12,128,128]{2,1,0:T(8,128)S(1)} copy-done((f32[12,128,128]{2,1,0:T(8,128)S(1)}, f32[12,128,128]{2,1,0:T(8,128)}, u32[]{:S(2)}) %copy-start.1) | copy-done | bytes 786456
  30.0 4.9 %visit.4 = (bf16[6144,128]{1,0:T(8,128)(2,1)S(1)}, bf16[6144,128]{1,0:T(8,128)(2,1)S(1)}, f32[48,2,128,128]{3,2,1,0:T(8,128)S(1)}, f32[12,128,128]{2,1,0:T(8,128)S(1)}) custom-call(s32[2]{0:T(128)S(1)} %pad_add_fusion.me_ref, s32[576]{0:T(1024)S(1)} %reshape.12.layout, bf16[3120,128]{1,0:T(8,128)(2,1)S(1)} %get-tuple-element.36.unit.refs_0_, ...), custom_call_target="tpu_custom_call" | custom-call | tf_op jit(solution)/shard_map/visit/pallas_call | solution.py:529
  34.9 0.0 collective-permute-done.1.refs_1_
  34.9 1.3 %collective-permute-start.5 = (bf16[3120,128]{1,0:T(8,128)(2,1)}, bf16[3120,128]{1,0:T(8,128)(2,1)S(1)}, u32[]{:S(2)}, u32[]{:S(2)}) collective-permute-start(bf16[3120,128]{1,0:T(8,128)(2,1)} %collective-permute-done.1.refs_1_), channel_id=1, source_target_pairs={{4,0},{5,1},{6,2},{7,3},{8,12},{9,13},{10,14},{11,15},{20,16},{21,... | collective-permute-start | bytes 2396168 | tf_op jit(solution)/shard_map/ppermute | solution.py:566
  36.2 14.0 %collective-permute-done.7.refs_0_ = bf16[3120,128]{1,0:T(8,128)(2,1)} collective-permute-done((bf16[3120,128]{1,0:T(8,128)(2,1)}, bf16[3120,128]{1,0:T(8,128)(2,1)}, u32[]{:S(2)}, u32[]{:S(2)}) %collective-permute-start.7) | collective-permute-done | bytes 798752 | tf_op jit(solution)/shard_map/ppermute | solution.py:566
  50.2 4.0 %visit.5 = (f32[48,2,128,128]{3,2,1,0:T(8,128)S(1)}, bf16[12,128,128]{2,1,0:T(8,128)(2,1)S(1)}, bf16[12,128,128]{2,1,0:T(8,128)(2,1)S(1)}) custom-call(s32[2]{0:T(128)S(1)} %pad_add_fusion.me_ref, s32[576]{0:T(1024)S(1)} %reshape.12.layout, bf16[3120,128]{1,0:T(8,128)(2,1)} %collective-permute-done.refs_0_, ...), custom_call_target="tpu_custom_call", output_to_operand_aliasing={{0}: (6, {})} | custom-call | tf_op jit(solution)/shard_map/visit/pallas_call | solution.py:529
  54.2 5.1 %visit.6 = (f32[48,2,128,128]{3,2,1,0:T(8,128)S(1)}, bf16[12,128,128]{2,1,0:T(8,128)(2,1)S(1)}, bf16[12,128,128]{2,1,0:T(8,128)(2,1)S(1)}) custom-call(s32[2]{0:T(128)S(1)} %pad_add_fusion.me_ref, s32[576]{0:T(1024)S(1)} %reshape.12.layout, bf16[3120,128]{1,0:T(8,128)(2,1)} %collective-permute-done.7.refs_0_, ...), custom_call_target="tpu_custom_call", output_to_operand_aliasing={{0}: (6, {})} | custom-call | tf_op jit(solution)/shard_map/visit/pallas_call | solution.py:529
  59.4 1.3 %collective-permute-start.8 = (bf16[12,128,128]{2,1,0:T(8,128)(2,1)S(1)}, bf16[12,128,128]{2,1,0:T(8,128)(2,1)S(1)}, u32[]{:S(2)}, u32[]{:S(2)}) collective-permute-start(bf16[12,128,128]{2,1,0:T(8,128)(2,1)S(1)} %get-tuple-element.53), channel_id=1, source_target_pairs={{0,4},{1,5},{2,6},{3,7},{12,8},{13,9},{14,10},{15,11},{16,20},{17,... | collective-permute-start | bytes 1179656 | tf_op jit(solution)/shard_map/ppermute | solution.py:566
  60.7 0.7 collective-permute-start.9
  61.4 4.6 %collective-permute-done.5.refs_0_ = bf16[3120,128]{1,0:T(8,128)(2,1)S(1)} collective-permute-done((bf16[3120,128]{1,0:T(8,128)(2,1)}, bf16[3120,128]{1,0:T(8,128)(2,1)S(1)}, u32[]{:S(2)}, u32[]{:S(2)}) %collective-permute-start.5) | collective-permute-done | bytes 798752 | tf_op jit(solution)/shard_map/ppermute | solution.py:566
  66.1 3.2 %visit.7 = (f32[48,2,128,128]{3,2,1,0:T(8,128)S(1)}, bf16[12,128,128]{2,1,0:T(8,128)(2,1)S(1)}) custom-call(s32[2]{0:T(128)S(1)} %pad_add_fusion.me_ref, s32[576]{0:T(1024)S(1)} %reshape.12.layout, bf16[3120,128]{1,0:T(8,128)(2,1)S(1)} %collective-permute-done.5.refs_0_, ...), custom_call_target="tpu_custom_call", output_to_operand_aliasing={{0}: (5, {})} | custom-call | flops 5033164800 | tf_op jit(solution)/shard_map/visit/pallas_call | solution.py:529
  69.2 0.0 collective-permute-done.8
  69.3 0.0 collective-permute-done.9
  69.3 0.2 add_convert_fusion
  69.5 0.2 share.2
  69.7 0.1 collective-permute-start.10
  69.8 0.6 collective-permute-start.12
  70.4 0.7 collective-permute-start.13
  71.1 2.1 %collective-permute-done.10.refs_0_ = bf16[2,2,12,128,128]{4,3,2,1,0:T(8,128)(2,1)S(1)} collective-permute-done((bf16[2,2,12,128,128]{4,3,2,1,0:T(8,128)(2,1)S(1)}, bf16[2,2,12,128,128]{4,3,2,1,0:T(8,128)(2,1)S(1)}, u32[]{:S(2)}, u32[]{:S(2)}) %collective-permute-start.10) | collective-permute-done | bytes 1572896 | tf_op jit(solution)/shard_map/ppermute | solution.py:566
  73.2 0.3 share.3
  73.5 1.6 %collective-permute-start.11 = (bf16[2,1,12,128,128]{4,3,2,1,0:T(8,128)(2,1)S(1)}, bf16[2,1,12,128,128]{4,3,2,1,0:T(8,128)(2,1)S(1)}, u32[]{:S(2)}, u32[]{:S(2)}) collective-permute-start(bf16[2,1,12,128,128]{4,3,2,1,0:T(8,128)(2,1)S(1)} %share.3), channel_id=1, source_target_pairs={{0,2},{1,3},{2,0},{3,1},{4,6},{5,7},{6,4},{7,5},{8,10},{9,11},{10,... | collective-permute-start | bytes 2359304 | tf_op jit(solution)/shard_map/ppermute | solution.py:566
  75.0 3.0 %collective-permute-start.14 = (bf16[12,128,128]{2,1,0:T(8,128)(2,1)S(1)}, bf16[12,128,128]{2,1,0:T(8,128)(2,1)S(1)}, u32[]{:S(2)}, u32[]{:S(2)}) collective-permute-start(bf16[12,128,128]{2,1,0:T(8,128)(2,1)S(1)} %get-tuple-element.63), channel_id=1, source_target_pairs={{12,0},{13,1},{14,2},{15,3},{0,12},{1,13},{2,14},{3,15},{28,16},{2... | collective-permute-start | bytes 1179656 | tf_op jit(solution)/shard_map/ppermute | solution.py:566
  78.0 11.8 %collective-permute-done.12.refs_0_ = bf16[12,128,128]{2,1,0:T(8,128)(2,1)S(1)} collective-permute-done((bf16[12,128,128]{2,1,0:T(8,128)(2,1)S(1)}, bf16[12,128,128]{2,1,0:T(8,128)(2,1)S(1)}, u32[]{:S(2)}, u32[]{:S(2)}) %collective-permute-start.12) | collective-permute-done | bytes 393248 | tf_op jit(solution)/shard_map/ppermute | solution.py:566
  89.8 0.0 collective-permute-done.13.refs_1_
  89.8 0.1 add.30.base
  89.9 0.0 collective-permute-done.14.refs_0_
  89.9 0.9 add.31
  90.8 2.3 %collective-permute-done.11.refs_1_ = bf16[2,1,12,128,128]{4,3,2,1,0:T(8,128)(2,1)S(1)} collective-permute-done((bf16[2,1,12,128,128]{4,3,2,1,0:T(8,128)(2,1)S(1)}, bf16[2,1,12,128,128]{4,3,2,1,0:T(8,128)(2,1)S(1)}, u32[]{:S(2)}, u32[]{:S(2)}) %collective-permute-start.11) | collective-permute-done | bytes 786464 | tf_op jit(solution)/shard_map/ppermute | solution.py:566
  93.1 1.1 %finish.1 = (bf16[1536,128]{1,0:T(8,128)(2,1)}, bf16[1536,128]{1,0:T(8,128)(2,1)}) custom-call(f32[48,2,128,128]{3,2,1,0:T(8,128)S(1)} %get-tuple-element.59.acc, bf16[2,2,12,128,128]{4,3,2,1,0:T(8,128)(2,1)S(1)} %collective-permute-done.10.refs_0_, bf16[2,1,12,128,128]{4,3,2,1,0:T(8,128)(2,1)S(1)} %collective-permute-done.11.refs_1_), custom_call_target="tpu_custom_call" | custom-call | tf_op jit(solution)/shard_map/finish/pallas_call | solution.py:462
  (4 shorter events, 0.0 us)
Async XLA Ops:
  0.6 25.0 %copy-start.2 = (s32[192,3]{0,1:T(4,128)S(1)}, s32[192,3]{0,1:T(4,128)}, u32[]{:S(2)}) copy-start(s32[192,3]{0,1:T(4,128)} %param.13) | copy-start | bytes 6916
  2.6 21.0 %collective-permute-start = (bf16[3120,128]{1,0:T(8,128)(2,1)S(1)}, bf16[3120,128]{1,0:T(8,128)(2,1)}, u32[]{:S(2)}, u32[]{:S(2)}) collective-permute-start(bf16[3120,128]{1,0:T(8,128)(2,1)S(1)} %get-tuple-element.36.unit.refs_0_), channel_id=1, source_target_pairs={{0,4},{1,5},{2,6},{3,7},{4,0},{5,1},{6,2},{7,3},{8,12},{9,13},{10,... | collective-permute-start | bytes 2396168 | tf_op jit(solution)/shard_map/ppermute | solution.py:566
  5.7 19.5 %collective-permute-start.3 = (bf16[3072,128]{1,0:T(8,128)(2,1)S(1)}, bf16[3072,128]{1,0:T(8,128)(2,1)}, u32[]{:S(2)}, u32[]{:S(2)}) collective-permute-start(bf16[3072,128]{1,0:T(8,128)(2,1)S(1)} %get-tuple-element.37.keyval.refs_1_), channel_id=1, source_target_pairs={{0,2},{1,3},{2,0},{3,1},{4,6},{5,7},{6,4},{7,5},{8,10},{9,11},{10,... | collective-permute-start | bytes 2359304 | tf_op jit(solution)/shard_map/ppermute | solution.py:566
  7.2 18.5 %collective-permute-start.6 = (bf16[3120,128]{1,0:T(8,128)(2,1)S(1)}, bf16[3120,128]{1,0:T(8,128)(2,1)}, u32[]{:S(2)}, u32[]{:S(2)}) collective-permute-start(bf16[3120,128]{1,0:T(8,128)(2,1)S(1)} %get-tuple-element.36.unit.refs_0_), channel_id=1, source_target_pairs={{4,8},{5,9},{6,10},{7,11},{8,4},{9,5},{10,6},{11,7},{20,24},{21,25... | collective-permute-start | bytes 2396168 | tf_op jit(solution)/shard_map/ppermute | solution.py:566
  12.4 0.9 copy-start
  23.6 11.3 %collective-permute-start.1 = (bf16[3120,128]{1,0:T(8,128)(2,1)}, bf16[3120,128]{1,0:T(8,128)(2,1)}, u32[]{:S(2)}, u32[]{:S(2)}) collective-permute-start(bf16[3120,128]{1,0:T(8,128)(2,1)} %collective-permute-done.refs_0_), channel_id=1, source_target_pairs={{4,8},{5,9},{6,10},{7,11},{8,4},{9,5},{10,6},{11,7},{20,24},{21,25... | collective-permute-start | bytes 2396168 | tf_op jit(solution)/shard_map/ppermute | solution.py:566
  25.1 3.5 %collective-permute-start.2 = (bf16[3072,128]{1,0:T(8,128)(2,1)S(1)}, bf16[3072,128]{1,0:T(8,128)(2,1)}, u32[]{:S(2)}, u32[]{:S(2)}) collective-permute-start(bf16[3072,128]{1,0:T(8,128)(2,1)S(1)} %get-tuple-element.37.keyval.refs_1_), channel_id=1, source_target_pairs={{0,1},{1,0},{2,3},{3,2},{4,5},{5,4},{6,7},{7,6},{8,9},{9,8},{10,11... | collective-permute-start | bytes 2359304 | tf_op jit(solution)/shard_map/ppermute | solution.py:566
  25.1 3.7 %collective-permute-start.4 = (bf16[3072,128]{1,0:T(8,128)(2,1)}, bf16[3072,128]{1,0:T(8,128)(2,1)}, u32[]{:S(2)}, u32[]{:S(2)}) collective-permute-start(bf16[3072,128]{1,0:T(8,128)(2,1)} %collective-permute-done.3.refs_3_), channel_id=1, source_target_pairs={{0,1},{1,0},{2,3},{3,2},{4,5},{5,4},{6,7},{7,6},{8,9},{9,8},{10,11... | collective-permute-start | bytes 2359304 | tf_op jit(solution)/shard_map/ppermute | solution.py:566
  25.7 24.5 %collective-permute-start.7 = (bf16[3120,128]{1,0:T(8,128)(2,1)}, bf16[3120,128]{1,0:T(8,128)(2,1)}, u32[]{:S(2)}, u32[]{:S(2)}) collective-permute-start(bf16[3120,128]{1,0:T(8,128)(2,1)} %collective-permute-done.6.refs_1_), channel_id=1, source_target_pairs={{4,0},{5,1},{6,2},{7,3},{8,12},{9,13},{10,14},{11,15},{20,16},{21,... | collective-permute-start | bytes 2396168 | tf_op jit(solution)/shard_map/ppermute | solution.py:566
  28.9 1.1 %copy-start.1 = (f32[12,128,128]{2,1,0:T(8,128)S(1)}, f32[12,128,128]{2,1,0:T(8,128)}, u32[]{:S(2)}) copy-start(f32[12,128,128]{2,1,0:T(8,128)} %copy-done) | copy-start | bytes 2359300
  34.9 31.2 %collective-permute-start.5 = (bf16[3120,128]{1,0:T(8,128)(2,1)}, bf16[3120,128]{1,0:T(8,128)(2,1)S(1)}, u32[]{:S(2)}, u32[]{:S(2)}) collective-permute-start(bf16[3120,128]{1,0:T(8,128)(2,1)} %collective-permute-done.1.refs_1_), channel_id=1, source_target_pairs={{4,0},{5,1},{6,2},{7,3},{8,12},{9,13},{10,14},{11,15},{20,16},{21,... | collective-permute-start | bytes 2396168 | tf_op jit(solution)/shard_map/ppermute | solution.py:566
  59.4 9.8 %collective-permute-start.8 = (bf16[12,128,128]{2,1,0:T(8,128)(2,1)S(1)}, bf16[12,128,128]{2,1,0:T(8,128)(2,1)S(1)}, u32[]{:S(2)}, u32[]{:S(2)}) collective-permute-start(bf16[12,128,128]{2,1,0:T(8,128)(2,1)S(1)} %get-tuple-element.53), channel_id=1, source_target_pairs={{0,4},{1,5},{2,6},{3,7},{12,8},{13,9},{14,10},{15,11},{16,20},{17,... | collective-permute-start | bytes 1179656 | tf_op jit(solution)/shard_map/ppermute | solution.py:566
  60.7 8.5 %collective-permute-start.9 = (bf16[12,128,128]{2,1,0:T(8,128)(2,1)S(1)}, bf16[12,128,128]{2,1,0:T(8,128)(2,1)S(1)}, u32[]{:S(2)}, u32[]{:S(2)}) collective-permute-start(bf16[12,128,128]{2,1,0:T(8,128)(2,1)S(1)} %get-tuple-element.54), channel_id=1, source_target_pairs={{8,4},{9,5},{10,6},{11,7},{4,8},{5,9},{6,10},{7,11},{24,20},{25,21... | collective-permute-start | bytes 1179656 | tf_op jit(solution)/shard_map/ppermute | solution.py:566
  69.7 3.5 %collective-permute-start.10 = (bf16[2,2,12,128,128]{4,3,2,1,0:T(8,128)(2,1)S(1)}, bf16[2,2,12,128,128]{4,3,2,1,0:T(8,128)(2,1)S(1)}, u32[]{:S(2)}, u32[]{:S(2)}) collective-permute-start(bf16[2,2,12,128,128]{4,3,2,1,0:T(8,128)(2,1)S(1)} %share.2), channel_id=1, source_target_pairs={{0,1},{1,0},{2,3},{3,2},{4,5},{5,4},{6,7},{7,6},{8,9},{9,8},{10,11... | collective-permute-start | bytes 4718600 | tf_op jit(solution)/shard_map/ppermute | solution.py:566
  69.8 20.0 %collective-permute-start.12 = (bf16[12,128,128]{2,1,0:T(8,128)(2,1)S(1)}, bf16[12,128,128]{2,1,0:T(8,128)(2,1)S(1)}, u32[]{:S(2)}, u32[]{:S(2)}) collective-permute-start(bf16[12,128,128]{2,1,0:T(8,128)(2,1)S(1)} %get-tuple-element.61), channel_id=1, source_target_pairs={{4,0},{5,1},{6,2},{7,3},{0,4},{1,5},{2,6},{3,7},{12,8},{13,9},{14,... | collective-permute-start | bytes 1179656 | tf_op jit(solution)/shard_map/ppermute | solution.py:566
  70.4 19.4 %collective-permute-start.13 = (bf16[12,128,128]{2,1,0:T(8,128)(2,1)S(1)}, bf16[12,128,128]{2,1,0:T(8,128)(2,1)S(1)}, u32[]{:S(2)}, u32[]{:S(2)}) collective-permute-start(bf16[12,128,128]{2,1,0:T(8,128)(2,1)S(1)} %get-tuple-element.62), channel_id=1, source_target_pairs={{8,4},{9,5},{10,6},{11,7},{4,8},{5,9},{6,10},{7,11},{24,20},{25,21... | collective-permute-start | bytes 1179656 | tf_op jit(solution)/shard_map/ppermute | solution.py:566
  73.5 19.6 %collective-permute-start.11 = (bf16[2,1,12,128,128]{4,3,2,1,0:T(8,128)(2,1)S(1)}, bf16[2,1,12,128,128]{4,3,2,1,0:T(8,128)(2,1)S(1)}, u32[]{:S(2)}, u32[]{:S(2)}) collective-permute-start(bf16[2,1,12,128,128]{4,3,2,1,0:T(8,128)(2,1)S(1)} %share.3), channel_id=1, source_target_pairs={{0,2},{1,3},{2,0},{3,1},{4,6},{5,7},{6,4},{7,5},{8,10},{9,11},{10,... | collective-permute-start | bytes 2359304 | tf_op jit(solution)/shard_map/ppermute | solution.py:566
  75.0 14.9 %collective-permute-start.14 = (bf16[12,128,128]{2,1,0:T(8,128)(2,1)S(1)}, bf16[12,128,128]{2,1,0:T(8,128)(2,1)S(1)}, u32[]{:S(2)}, u32[]{:S(2)}) collective-permute-start(bf16[12,128,128]{2,1,0:T(8,128)(2,1)S(1)} %get-tuple-element.63), channel_id=1, source_target_pairs={{12,0},{13,1},{14,2},{15,3},{0,12},{1,13},{2,14},{3,15},{28,16},{2... | collective-permute-start | bytes 1179656 | tf_op jit(solution)/shard_map/ppermute | solution.py:566
